TPU v7x, 32 devices: a whole 2x2x4 slice. The times are simulated.
32 devices in a mesh: wide: 16 (over z, x, core), narrow: 2 (over y).
Axes of the slice: x: 2, y: 2, z: 4, core: 2. Of those that a mesh axis runs over, the one named last changes fastest.
Arguments:
- tokens: bfloat16 [32, 532, 1024], P('wide'), may hold values from -6 to 6
- cotangent: bfloat16 [32, 532, 1024], P('wide'), may hold values from -6 to 6
- doc_ids: int32 [32, 512], P('wide'), may hold values from 0 to 7, never falling along the last dimension, each value on 1 to 128 neighbouring positions
- reset_flags: int32 [32, 8], P('wide'), may hold values 0 or 1
- mem_live: int32 [32], P('wide'), may hold values from 1 to 10
- qkv_weight: float32 [3, 1024, 1024], P(None, 'wide', 'narrow'), may hold values from -0.1875 to 0.1875
- qkv_moment: float32 [3, 1024, 1024], P(None, 'wide', 'narrow'), may hold values from -0.66 to 0.66
- qkv_square: float32 [3, 1024, 1024], P(None, 'wide', 'narrow'), may hold values from 0.0102 to 0.163
- qkv_average: float32 [3, 1024, 1024], P(None, 'wide', 'narrow'), may hold values from -0.1875 to 0.1875
- out_weight: float32 [1024, 1024], P('narrow', 'wide'), may hold values from -1.5 to 1.5
- out_moment: float32 [1024, 1024], P('narrow', 'wide'), may hold values from -0.66 to 0.66
- out_square: float32 [1024, 1024], P('narrow', 'wide'), may hold values from 0.002 to 0.008
- out_average: float32 [1024, 1024], P('narrow', 'wide'), may hold values from -1.5 to 1.5
- up_weight: float32 [1024, 4096], P('wide', 'narrow'), may hold values from -0.1875 to 0.1875
- up_moment: float32 [1024, 4096], P('wide', 'narrow'), may hold values from -0.66 to 0.66
- up_square: float32 [1024, 4096], P('wide', 'narrow'), may hold values from 0.0102 to 0.163
- up_average: float32 [1024, 4096], P('wide', 'narrow'), may hold values from -0.1875 to 0.1875
- down_weight: float32 [4096, 1024], P('narrow', 'wide'), may hold values from -0.09375 to 0.09375
- down_moment: float32 [4096, 1024], P('narrow', 'wide'), may hold values from -0.66 to 0.66
- down_square: float32 [4096, 1024], P('narrow', 'wide'), may hold values from 0.0102 to 0.163
- down_average: float32 [4096, 1024], P('narrow', 'wide'), may hold values from -0.09375 to 0.09375
- norm_params: float32 [4, 1024], P(None, 'wide'), may hold values from -1.2 to 1.5
- norm_moment: float32 [4, 1024], P(None, 'wide'), may hold values from -2.64 to 2.64
- norm_square: float32 [4, 1024], P(None, 'wide'), may hold values from 0.16 to 2.6
- norm_average: float32 [4, 1024], P(None, 'wide'), may hold values from -1.2 to 1.5
Outputs:
- output: bfloat16 [32, 532, 1024], P('wide')
- input_grad: float32 [32, 532, 1024], P('wide')
- grad_norm: float32 [], replicated
- new_qkv: float32 [3, 1024, 1024], P(None, 'wide', 'narrow')
- new_qkv_moment: float32 [3, 1024, 1024], P(None, 'wide', 'narrow')
- new_qkv_square: float32 [3, 1024, 1024], P(None, 'wide', 'narrow')
- new_qkv_average: float32 [3, 1024, 1024], P(None, 'wide', 'narrow')
- new_out: float32 [1024, 1024], P('narrow', 'wide')
- new_out_moment: float32 [1024, 1024], P('narrow', 'wide')
- new_out_square: float32 [1024, 1024], P('narrow', 'wide')
- new_out_average: float32 [1024, 1024], P('narrow', 'wide')
- new_up: float32 [1024, 4096], P('wide', 'narrow')
- new_up_moment: float32 [1024, 4096], P('wide', 'narrow')
- new_up_square: float32 [1024, 4096], P('wide', 'narrow')
- new_up_average: float32 [1024, 4096], P('wide', 'narrow')
- new_down: float32 [4096, 1024], P('narrow', 'wide')
- new_down_moment: float32 [4096, 1024], P('narrow', 'wide')
- new_down_square: float32 [4096, 1024], P('narrow', 'wide')
- new_down_average: float32 [4096, 1024], P('narrow', 'wide')
- new_norms: float32 [4, 1024], P(None, 'wide')
- new_norm_moment: float32 [4, 1024], P(None, 'wide')
- new_norm_square: float32 [4, 1024], P(None, 'wide')
- new_norm_average: float32 [4, 1024], P(None, 'wide')
Inputs may be any that keep to these rules, and one draw needn't show every extreme that they name: `doc_ids`: document numbers never fall along a segment; every document 0 to 7 has 1 to 128 tokens.
All inputs are finite; a program needn't handle non-finite values. No bound on the sum of `reset_flags` on one device may be relied on, other than what follows from the above.
Results may differ from a plain program's by a relative error of at most 0.01.
The roundings to bfloat16 on the way count: a program that leaves them out, or rounds other values in their place, can miss the bound.
Values may be sent and summed in bfloat16 or wider, within the bound.
No kernel may reach another device: no remote copies, remote signals or barrier semaphores. Data moves between devices by JAX's collectives and lax.ppermute only.
A program may use at most 192 MiB of HBM per device.

v0:
```python
import functools
import math

import jax
import jax.numpy as jnp
from jax import lax
from jax.experimental import pallas as pl
from jax.experimental.pallas import tpu as pltpu
from jax.sharding import PartitionSpec as P

D = 1024
HEAD = 64
FF = 4096
MEM = 10
STEP = 10


NORM_EPS = 1e-12
BETA_ONE = 0.9
BETA_TWO = 0.98
ADAM_EPS = 1e-06
AVERAGE_KEEP = 0.75
MASKED = -1e30


def allowed_mask(doc_row, reset_row, live_count):
    rows_all = doc_row.shape[0] + 2 * MEM
    kinds = jnp.concatenate(
        [jnp.full((MEM,), -1, jnp.int32), doc_row, jnp.full((MEM,), -2, jnp.int32)]
    )
    place = jnp.arange(rows_all, dtype=jnp.int32)
    read_key = place < MEM
    live_key = place < live_count
    choose = kinds[:, None] == jnp.arange(reset_row.shape[0], dtype=jnp.int32)[None, :]
    reset_query = jnp.sum(jnp.where(choose, reset_row[None, :], 0), axis=1)
    memory_query = kinds < 0
    same_doc = kinds[:, None] == kinds[None, :]
    token_sees = same_doc | (read_key & live_key)[None, :] & (reset_query == 0)[:, None]
    memory_sees = jnp.broadcast_to((~read_key | live_key)[None, :], (rows_all, rows_all))
    return jnp.where(memory_query[:, None], memory_sees, token_sees)


def norm_forward(rows_in, gain, shift):
    center = rows_in - jnp.mean(rows_in, axis=-1, keepdims=True)
    inverse = lax.rsqrt(jnp.mean(center * center, axis=-1, keepdims=True) + NORM_EPS)
    normed = center * inverse
    return (normed * gain + shift, normed, inverse)


def norm_backward(grad, normed, inverse, gain):
    scaled = grad * gain
    back = inverse * (
        scaled
        - jnp.mean(scaled, axis=-1, keepdims=True)
        - normed * jnp.mean(scaled * normed, axis=-1, keepdims=True)
    )
    return (back, jnp.stack([jnp.sum(grad * normed, axis=0), jnp.sum(grad, axis=0)]))


def masked_scores(query, keys, allowed):
    scores = jnp.einsum("qhd,khd->hqk", query, keys, preferred_element_type=jnp.float32) * (
        1.0 / math.sqrt(HEAD)
    )
    return jnp.where(allowed[None], scores, MASKED)


def attend(inputs):
    query, keys, values, allowed = inputs
    scores = masked_scores(query, keys, allowed)
    row_top = jnp.max(scores, axis=-1, keepdims=True)
    expo = jnp.exp(scores - row_top)
    row_total = jnp.sum(expo, axis=-1, keepdims=True)
    probs = (expo / row_total).astype(jnp.bfloat16)
    context = jnp.einsum("hqk,khd->qhd", probs, values, preferred_element_type=jnp.float32)
    return (context.astype(jnp.bfloat16), row_top + jnp.log(row_total))


def attend_back(inputs):
    query, keys, values, allowed, log_total, context_grad = inputs
    probs = jnp.exp(masked_scores(query, keys, allowed) - log_total)
    value_grad = jnp.einsum(
        "hqk,qhd->khd", probs.astype(jnp.bfloat16), context_grad, preferred_element_type=jnp.float32
    )
    prob_grad = jnp.einsum("qhd,khd->hqk", context_grad, values, preferred_element_type=jnp.float32)
    score_grad = probs * (prob_grad - jnp.sum(probs * prob_grad, axis=-1, keepdims=True))
    score_grad = score_grad.astype(jnp.bfloat16)
    scale_now = 1.0 / math.sqrt(HEAD)
    query_grad = (
        jnp.einsum("hqk,khd->qhd", score_grad, keys, preferred_element_type=jnp.float32) * scale_now
    )
    key_grad = (
        jnp.einsum("hqk,qhd->khd", score_grad, query, preferred_element_type=jnp.float32)
        * scale_now
    )
    return (
        query_grad.astype(jnp.bfloat16),
        key_grad.astype(jnp.bfloat16),
        value_grad.astype(jnp.bfloat16),
    )


def adam_step(weight, moment, square, average, grad, rate, decay):
    moment = BETA_ONE * moment + (1.0 - BETA_ONE) * grad
    square = BETA_TWO * square + (1.0 - BETA_TWO) * grad * grad
    first_hat = moment / (1.0 - BETA_ONE**STEP)
    second_hat = square / (1.0 - BETA_TWO**STEP)
    weight = weight - rate * (first_hat / (jnp.sqrt(second_hat) + ADAM_EPS) + decay * weight)
    average = AVERAGE_KEEP * average + (1.0 - AVERAGE_KEEP) * weight
    return (weight, moment, square, average)


def row_scatter(terms):
    return lax.psum_scatter(terms, "narrow", scatter_dimension=0, tiled=True)


def row_gather(piece):
    return lax.all_gather(piece, "narrow", axis=0, tiled=True)


def narrow_norm(grads):
    return lax.psum(grads, "narrow")


def shared_rows(
    tokens,
    cotangent,
    doc_ids,
    reset_flags,
    mem_live,
    qkv_weight,
    qkv_moment,
    qkv_square,
    qkv_average,
    out_weight,
    out_moment,
    out_square,
    out_average,
    up_weight,
    up_moment,
    up_square,
    up_average,
    down_weight,
    down_moment,
    down_square,
    down_average,
    norm_params,
    norm_moment,
    norm_square,
    norm_average,
):
    narrow_count = lax.axis_size("narrow")
    seg_count, rows_all, width = tokens.shape
    w_qkv, w_out, w_up, w_down, norms_low = (
        lax.all_gather(qkv_weight.astype(jnp.bfloat16), "wide", axis=1, tiled=True),
        lax.all_gather(out_weight.astype(jnp.bfloat16), "wide", axis=1, tiled=True),
        lax.all_gather(up_weight.astype(jnp.bfloat16), "wide", axis=0, tiled=True),
        lax.all_gather(down_weight.astype(jnp.bfloat16), "wide", axis=1, tiled=True),
        lax.all_gather(norm_params.astype(jnp.bfloat16), "wide", axis=1, tiled=True),
    )
    norms = norms_low.astype(jnp.float32)
    local_cols = w_qkv.shape[2]
    local_heads = local_cols // HEAD
    total_rows = seg_count * rows_all
    flat_in = tokens.reshape(total_rows, width)
    flat_cot = cotangent.reshape(total_rows, width)
    allowed = jax.vmap(allowed_mask)(doc_ids, reset_flags, mem_live)
    projected = jnp.einsum(
        "md,kdc->kmc", flat_in, w_qkv, preferred_element_type=jnp.float32
    ).astype(jnp.bfloat16)
    split_heads = projected.reshape(3, seg_count, rows_all, local_heads, HEAD)
    query, keys, values = (split_heads[0], split_heads[1], split_heads[2])
    context, log_total = lax.map(attend, (query, keys, values, allowed))
    context_flat = context.reshape(total_rows, local_cols)
    attention_terms = jnp.dot(context_flat, w_out, preferred_element_type=jnp.float32)
    share = total_rows // narrow_count
    row_start = lax.axis_index("narrow") * share
    own_in = lax.dynamic_slice_in_dim(flat_in, row_start, share, 0)
    own_cot = lax.dynamic_slice_in_dim(flat_cot, row_start, share, 0)
    first_sum = own_in.astype(jnp.float32) + row_scatter(attention_terms)
    hidden, normed_one, inverse_one = norm_forward(first_sum, norms[0], norms[1])
    hidden_low = row_gather(hidden.astype(jnp.bfloat16))
    inner = jnp.dot(hidden_low, w_up, preferred_element_type=jnp.float32)
    active, gelu_pull = jax.vjp(lambda value_in: jax.nn.gelu(value_in, approximate=False), inner)
    active_low = active.astype(jnp.bfloat16)
    feed_terms = jnp.dot(active_low, w_down, preferred_element_type=jnp.float32)
    feed = row_scatter(feed_terms)
    second_sum = hidden + feed
    result, normed_two, inverse_two = norm_forward(second_sum, norms[2], norms[3])
    result_low = result.astype(jnp.bfloat16)
    second_grad, norm_two_grads = norm_backward(
        own_cot.astype(jnp.float32), normed_two, inverse_two, norms[2]
    )
    norm_two_grads = narrow_norm(norm_two_grads)
    output = row_gather(result_low)
    feed_grad = row_gather(second_grad.astype(jnp.bfloat16))
    output = output.reshape(seg_count, rows_all, width)
    down_grad = jnp.einsum("mf,md->fd", active_low, feed_grad, preferred_element_type=jnp.float32)
    active_grad = jnp.einsum("md,fd->mf", feed_grad, w_down, preferred_element_type=jnp.float32)
    inner_grad = gelu_pull(active_grad)[0].astype(jnp.bfloat16)
    up_grad = jnp.einsum("md,mf->df", hidden_low, inner_grad, preferred_element_type=jnp.float32)
    hidden_terms = jnp.einsum("mf,df->md", inner_grad, w_up, preferred_element_type=jnp.float32)
    hidden_grad = second_grad + row_scatter(hidden_terms)
    first_grad, norm_one_grads = norm_backward(hidden_grad, normed_one, inverse_one, norms[0])
    norm_one_grads = narrow_norm(norm_one_grads)
    branch_grad = row_gather(first_grad.astype(jnp.bfloat16))
    out_grad_weight = jnp.einsum(
        "mc,md->cd", context_flat, branch_grad, preferred_element_type=jnp.float32
    )
    context_grad = jnp.einsum(
        "md,cd->mc", branch_grad, w_out, preferred_element_type=jnp.float32
    ).astype(jnp.bfloat16)
    context_grad = context_grad.reshape(seg_count, rows_all, local_heads, HEAD)
    query_grad, key_grad, value_grad = lax.map(
        attend_back, (query, keys, values, allowed, log_total, context_grad)
    )
    stacked_grad = jnp.stack([query_grad, key_grad, value_grad]).reshape(3, total_rows, local_cols)
    qkv_grad = jnp.einsum("md,kmc->kdc", flat_in, stacked_grad, preferred_element_type=jnp.float32)
    input_terms = jnp.einsum("kmc,kdc->md", stacked_grad, w_qkv, preferred_element_type=jnp.float32)
    input_grad = lax.all_gather(first_grad + row_scatter(input_terms), "narrow", axis=0, tiled=True)
    input_grad = input_grad.reshape(seg_count, rows_all, width)
    norm_grads = jnp.concatenate([norm_one_grads, norm_two_grads], axis=0)
    qkv_sum, out_sum, up_sum, down_sum, norm_sum = (
        lax.psum_scatter(qkv_grad, "wide", scatter_dimension=1, tiled=True),
        lax.psum_scatter(out_grad_weight, "wide", scatter_dimension=1, tiled=True),
        lax.psum_scatter(up_grad, "wide", scatter_dimension=0, tiled=True),
        lax.psum_scatter(down_grad, "wide", scatter_dimension=1, tiled=True),
        lax.psum_scatter(norm_grads, "wide", scatter_dimension=1, tiled=True),
    )
    local_squares = (
        jnp.sum(qkv_sum * qkv_sum)
        + jnp.sum(out_sum * out_sum)
        + jnp.sum(up_sum * up_sum)
        + jnp.sum(down_sum * down_sum)
        + jnp.sum(norm_sum * norm_sum) / narrow_count
    )
    grad_norm = jnp.sqrt(lax.psum(local_squares, ("wide", "narrow")))
    threshold = math.sqrt(4 * D * D + 2 * D * FF + 4 * D)
    factor = jnp.minimum(1.0, threshold / (grad_norm + 1e-06))
    new_qkv = adam_step(
        qkv_weight, qkv_moment, qkv_square, qkv_average, qkv_sum * factor, 0.02, 0.01
    )
    new_out = adam_step(
        out_weight, out_moment, out_square, out_average, out_sum * factor, 0.06, 0.01
    )
    new_up = adam_step(up_weight, up_moment, up_square, up_average, up_sum * factor, 0.02, 0.01)
    new_down = adam_step(
        down_weight, down_moment, down_square, down_average, down_sum * factor, 0.02, 0.01
    )
    new_norm = adam_step(
        norm_params, norm_moment, norm_square, norm_average, norm_sum * factor, 0.4, 0.0
    )
    return (
        output,
        input_grad,
        grad_norm,
        new_qkv[0],
        new_qkv[1],
        new_qkv[2],
        new_qkv[3],
        new_out[0],
        new_out[1],
        new_out[2],
        new_out[3],
        new_up[0],
        new_up[1],
        new_up[2],
        new_up[3],
        new_down[0],
        new_down[1],
        new_down[2],
        new_down[3],
        new_norm[0],
        new_norm[1],
        new_norm[2],
        new_norm[3],
    )


SWAP = ((0, 1), (1, 0))
RING = ((0, 1), (1, 3), (3, 2), (2, 0))
RING_BACK = tuple((b, a) for a, b in RING)


def send(block, axes, pairs):
    return lax.ppermute(block, axes, list(pairs))


def ring_place():
    x, y = lax.axis_index("x"), lax.axis_index("y")
    return jnp.where(x == 0, y, 3 - y)


def place_xy(place):
    place = lax.rem(place + 4, 4)
    x = place // 2
    return x, jnp.where(x == 0, place, 3 - place)


def ring_gather(block):
    left = send(block, ("x", "y"), RING)
    right = send(block, ("x", "y"), RING_BACK)
    half = block.shape[0] // 2
    far_one = send(left[:half], ("x", "y"), RING)
    far_two = send(right[half:], ("x", "y"), RING_BACK)
    return block, left, right, far_one, far_two


def ring_scatter(take, half_of):
    place = ring_place()
    far = half_of(take(*place_xy(place + 2)))
    from_left = send(far[0].astype(jnp.bfloat16), ("x", "y"), RING)
    from_right = send(far[1].astype(jnp.bfloat16), ("x", "y"), RING_BACK)
    right = half_of(take(*place_xy(place + 1)))
    left = half_of(take(*place_xy(place - 1)))
    to_right = jnp.concatenate([right[0] + from_left.astype(jnp.float32), right[1]]).astype(jnp.bfloat16)
    to_left = jnp.concatenate([left[0], left[1] + from_right.astype(jnp.float32)]).astype(jnp.bfloat16)
    from_left = send(to_right, ("x", "y"), RING)
    from_right = send(to_left, ("x", "y"), RING_BACK)
    return take(*place_xy(place)) + from_left.astype(jnp.float32) + from_right.astype(jnp.float32)


def line_scatter(take):
    count, z = lax.axis_size("z"), lax.axis_index("z")
    up = down = None
    for step in range(1, count):
        pairs = [(i, i + 1) for i in range(step)]
        above = take(jnp.minimum(z + count - step, count - 1))
        below = take(jnp.maximum(z - count + step, 0))
        if up is not None:
            above, below = above + up.astype(jnp.float32), below + down.astype(jnp.float32)
        up = send(above.astype(jnp.bfloat16), "z", pairs)
        down = send(below.astype(jnp.bfloat16), "z", [(count - 1 - a, count - 1 - b) for a, b in pairs])
    return take(z) + up.astype(jnp.float32) + down.astype(jnp.float32)


STEP_WIDTH = 512
RING_SHIFTS = (0, -1, 1, 2, 2)
NT = (((1,), (1,)), ((), ()))
TN = (((0,), (0,)), ((), ()))
NN = (((1,), (0,)), ((), ()))
F32, LOW = jnp.float32, jnp.bfloat16
ANYWHERE = pl.BlockSpec(memory_space=pl.ANY)


def params(mib):
    return pltpu.CompilerParams(vmem_limit_bytes=mib << 20)


def shaped(shape, dtype):
    return jax.ShapeDtypeStruct(shape, dtype)


def full(shape):
    return pl.BlockSpec(shape, lambda *_: (0,) * len(shape))


def mm(a, b, dims=NN):
    return lax.dot_general(a, b, dims, preferred_element_type=F32)


def join_column_kernel(count, *refs):
    own, ups, downs = refs[0], refs[1:count], refs[count : 2 * count - 1]
    out, sem = refs[-2:]
    z = lax.axis_index("z")
    moves = [(None, own, z)]
    for k in range(1, count):
        moves += [(z >= k, ups[k - 1], z - k), (z + k < count, downs[k - 1], z + k)]
    for end in (False, True):
        for i, (here, ref, at) in enumerate(moves):
            copy = pltpu.make_async_copy(ref, out.at[at], sem.at[i])
            act = copy.wait if end else copy.start
            act() if here is None else pl.when(here)(act)


def line_pieces(block):
    count = lax.axis_size("z")
    ups, downs = [block], [block]
    for step in range(1, count):
        pairs = [(i, i + 1) for i in range(step - 1, count - 1)]
        ups.append(send(ups[-1], "z", pairs))
        downs.append(send(downs[-1], "z", [(count - 1 - a, count - 1 - b) for a, b in pairs]))
    return [block] + ups[1:] + downs[1:]


def join_column(pieces):
    count = (len(pieces) + 1) // 2
    shape = (count,) + pieces[0].shape
    return pl.pallas_call(
        functools.partial(join_column_kernel, count),
        in_specs=[ANYWHERE] * len(pieces),
        out_specs=pl.BlockSpec(memory_space=pltpu.VMEM),
        out_shape=shaped(shape, pieces[0].dtype),
        scratch_shapes=[pltpu.SemaphoreType.DMA((len(pieces),))],
        name="join_column",
    )(*pieces)


def join_square_kernel(own, left, right, far_one, far_two, out, sem):
    place = ring_place()
    half = far_one.shape[0]
    copies = []
    for i, (ref, shift) in enumerate(zip((own, left, right, far_one, far_two), RING_SHIFTS)):
        x, y = place_xy(place + shift)
        to = out.at[x, y] if i < 3 else out.at[x, y, pl.ds(half * (i - 3), half)]
        copies.append(pltpu.make_async_copy(ref, to, sem.at[i]))
    for copy in copies:
        copy.start()
    for copy in copies:
        copy.wait()


def join_square(pieces):
    return pl.pallas_call(
        join_square_kernel,
        in_specs=[ANYWHERE] * 5,
        out_specs=pl.BlockSpec(memory_space=pltpu.VMEM),
        out_shape=shaped((2, 2) + pieces[0].shape, pieces[0].dtype),
        scratch_shapes=[pltpu.SemaphoreType.DMA((5,))],
        name="join_square",
    )(*pieces)


def both_cores(pieces):
    return list(pieces) + [send(p, "c", SWAP) for p in pieces]


def weights_square_last(block):
    return both_cores(ring_gather(join_column(line_pieces(block))))


def weights_line_last(block):
    return both_cores(line_pieces(join_square(ring_gather(block))))


def load_square_last(pieces, w, sem, column, width, per_side):
    place, core = ring_place(), lax.axis_index("c")
    rows = w.shape[4]
    for k in range(per_side):
        for group, core_at in ((pieces[:5], core), (pieces[5:], 1 - core)):
            for i, (ref, shift) in enumerate(zip(group, RING_SHIFTS)):
                x, y = place_xy(place + shift)
                chunk = y * per_side + k
                first = ref.shape[0] if i == 4 else 0
                pltpu.make_async_copy(
                    ref.at[:, pl.ds(0, rows), pl.ds(column + k * width, width)],
                    w.at[chunk, pl.ds(first, ref.shape[0]), x, core_at],
                    sem.at[chunk],
                ).start()


def load_line_last(pieces, w, sem, width, per_side):
    z, core = lax.axis_index("z"), lax.axis_index("c")
    group_size = len(pieces) // 2
    count = (group_size + 1) // 2
    for k in range(per_side):
        for group, core_at in ((pieces[:group_size], core), (pieces[group_size:], 1 - core)):
            places = [(None, z)] + [(z >= s, z - s) for s in range(1, count)]
            places += [(z + s < count, z + s) for s in range(1, count)]
            for ref, (here, at) in zip(group, places):

                def begin(ref=ref, at=at, core_at=core_at):
                    for y in range(2):
                        chunk = y * per_side + k
                        pltpu.make_async_copy(
                            ref.at[:, y, :, pl.ds(k * width, width)], w.at[chunk, at, :, core_at], sem.at[chunk]
                        ).start()

                begin() if here is None else pl.when(here)(begin)


def ready(w, sem, chunk):
    pltpu.make_async_copy(w.at[chunk], w.at[chunk], sem.at[chunk]).wait()


def matrix(w, chunk):
    block = w[chunk]
    return block.reshape(-1, block.shape[-1])


def chunk_buffer(shapes, chunks, width):
    z, rows = shapes
    return [pltpu.VMEM((chunks, z, 2, 2, rows, width), LOW), pltpu.SemaphoreType.DMA((chunks,))]


def alternate(per_side):
    return lambda j: (j % 2) * per_side + j // 2


def project_kernel(per_side, x_ref, *refs):
    pieces, (o_ref, w, sem) = refs[:10], refs[10:]
    j = pl.program_id(0)

    @pl.when(j == 0)
    def _():
        load_square_last(pieces, w, sem, 0, o_ref.shape[2], per_side)

    chunk = alternate(per_side)(j)
    ready(w, sem, chunk)
    o_ref[0] = mm(x_ref[...], matrix(w, chunk)).astype(LOW)


def project(x, pieces, rows):
    count, width = pieces[0].shape[0], STEP_WIDTH
    per_side = pieces[0].shape[2] // width
    at = alternate(per_side)
    return pl.pallas_call(
        functools.partial(project_kernel, per_side),
        grid=(2 * per_side,),
        in_specs=[full(x.shape)] + [ANYWHERE] * 10,
        out_specs=pl.BlockSpec((1, x.shape[0], width), lambda j: (at(j), 0, 0)),
        out_shape=shaped((2 * per_side, x.shape[0], width), LOW),
        scratch_shapes=chunk_buffer((count, rows), 2 * per_side, width),
        compiler_params=params(32),
        name="project",
    )(x, *pieces)


def head_parts(a, lane, scale=None):
    a = a if scale is None else a * jnp.asarray(scale, a.dtype)
    none = jnp.zeros_like(a)
    return jnp.where(lane < HEAD, a, none), jnp.where(lane < HEAD, none, a)


def attend_kernel(q_ref, k_ref, v_ref, bias_ref, o_ref, l_ref):
    k, v = k_ref[0], v_ref[0]
    lane = lax.broadcasted_iota(jnp.int32, k.shape, 1)
    outs, logs = [], []
    for q in head_parts(q_ref[0], lane, HEAD**-0.5):
        scores = mm(q, k, NT) + bias_ref[...].astype(F32)
        top = jnp.max(scores, axis=-1, keepdims=True)
        expo = jnp.exp(scores - top)
        total = jnp.sum(expo, axis=-1, keepdims=True)
        outs.append(mm((expo * (1.0 / total)).astype(LOW), v))
        logs.append(top + jnp.log(total))
    o_ref[...] = jnp.where(lane < HEAD, outs[0], outs[1]).astype(LOW)
    l_ref[...] = jnp.where(lane < HEAD, logs[0], logs[1])


def pair_specs(total, per_side):
    def spec(k):
        return pl.BlockSpec((1, total, 128), lambda g: ((g // per_side) * 3 + k, 0, g % per_side))

    return [spec(k) for k in range(3)]


def attention(qkv, bias):
    total, width = qkv.shape[1], qkv.shape[2] * 2
    pairs = width // 128
    return pl.pallas_call(
        attend_kernel,
        grid=(pairs,),
        in_specs=pair_specs(total, pairs // 2) + [full(bias.shape)],
        out_specs=[pl.BlockSpec((total, 128), lambda g: (0, g))] * 2,
        out_shape=[shaped((total, width), LOW), shaped((total, width), F32)],
        compiler_params=params(48),
        name="attention",
    )(qkv, qkv, qkv, bias)


ROWS_AT_ONCE = 32


def by_rows(total, body, carry=0):
    def step(i, held):
        return body(pl.ds(pl.multiple_of(i * ROWS_AT_ONCE, ROWS_AT_ONCE), ROWS_AT_ONCE), held)

    return lax.fori_loop(0, total // ROWS_AT_ONCE, step, carry)


def normalize(v):
    center = v - jnp.mean(v, axis=-1, keepdims=True)
    inverse = lax.rsqrt(jnp.mean(center * center, axis=-1, keepdims=True) + NORM_EPS)
    return center * inverse, inverse


def unnormalize(scaled, normed, inverse):
    return inverse * (
        scaled
        - jnp.mean(scaled, axis=-1, keepdims=True)
        - normed * jnp.mean(scaled * normed, axis=-1, keepdims=True)
    )


def fold(a):
    return jnp.sum(a.reshape(-1, 8, a.shape[-1]), axis=0)


def gelu_parts(u):
    expo = jnp.exp(-0.5 * (u * u))
    t = 1.0 / (1.0 + 0.3275911 * 0.7071067811865476 * jnp.abs(u))
    poly = ((((1.061405429 * t - 1.453152027) * t + 1.421413741) * t - 0.284496736) * t + 0.254829592) * t
    tail = 0.5 * poly * expo
    phi = jnp.where(u < 0, tail, 1.0 - tail)
    return u * phi, phi + u * expo * 0.3989422804014327


def up_kernel(per_side, x_ref, ctx_ref, *refs):
    pieces = refs[:10]
    h_ref, n_ref, i_ref, norms_ref, g_ref, d_ref, wu, us, wo, os, nw, ns, acc = refs[10:]
    j = pl.program_id(0)
    width = g_ref.shape[2]

    @pl.when(j == 0)
    def _():
        first = 2 * per_side // 2 * width
        load_square_last(pieces, nw, ns, first + width, 128, 1)
        load_square_last(pieces, wo, os, first, width, 1)
        load_square_last(pieces, wu, us, 0, width, per_side)
        ready(nw, ns, 0)
        ready(nw, ns, 1)
        cells = nw[0].reshape(-1, nw.shape[4], 128).astype(F32)
        side = x_ref.shape[1] // cells.shape[0]
        norms_ref[...] = jnp.concatenate([cells[i, :8, :side] for i in range(cells.shape[0])], axis=1)
        ready(wo, os, 0)
        acc[...] = mm(ctx_ref[:, :width], matrix(wo, 0), NT)
        ready(wo, os, 1)
        acc[...] += mm(ctx_ref[:, width:], matrix(wo, 1), NT)
        gain, shift = norms_ref[0:1], norms_ref[1:2]

        def rows(r, held):
            normed, inverse = normalize(x_ref[r].astype(F32) + acc[r])
            n_ref[r] = normed
            i_ref[r] = jnp.broadcast_to(inverse, (ROWS_AT_ONCE, 128))
            h_ref[r] = (normed * gain + shift).astype(LOW)
            return held

        by_rows(x_ref.shape[0], rows)

    chunk = alternate(per_side)(j)
    ready(wu, us, chunk)
    active, slope = gelu_parts(mm(h_ref[...], matrix(wu, chunk)))
    g_ref[0] = active.astype(LOW)
    d_ref[0] = slope.astype(LOW)


def up(x, context, pieces, rows, inner_part):
    count, width = pieces[0].shape[0], STEP_WIDTH
    per_side = inner_part // width
    at = alternate(per_side)
    total, model = x.shape
    chunks = pl.BlockSpec((1, total, width), lambda j: (at(j), 0, 0))
    return pl.pallas_call(
        functools.partial(up_kernel, per_side),
        grid=(2 * per_side,),
        in_specs=[full(x.shape)] * 2 + [ANYWHERE] * 10,
        out_specs=[full(x.shape), full(x.shape), full((total, 128)), full((8, model)), chunks, chunks],
        out_shape=[
            shaped(x.shape, LOW),
            shaped(x.shape, F32),
            shaped((total, 128), F32),
            shaped((8, model), F32),
            shaped((2 * per_side, total, width), LOW),
            shaped((2 * per_side, total, width), LOW),
        ],
        scratch_shapes=chunk_buffer((count, rows), 2 * per_side, width)
        + chunk_buffer((count, rows), 2, width)
        + chunk_buffer((count, 16), 2, 128)
        + [pltpu.VMEM(x.shape, F32)],
        compiler_params=params(56),
        name="up",
    )(x, context, *pieces)


def down_kernel(per_side, pieces_count, g_ref, n_ref, norms_ref, cot_ref, *refs):
    pieces = refs[:pieces_count]
    o_ref, d_ref, f_ref, ng_ref, w, sem, acc = refs[pieces_count:]
    j = pl.program_id(0)

    @pl.when(j == 0)
    def _():
        load_line_last(pieces, w, sem, g_ref.shape[2], per_side)
        acc[...] = jnp.zeros_like(acc)

    chunk = alternate(per_side)(j)
    ready(w, sem, chunk)
    acc[...] += mm(g_ref[0], matrix(w, chunk), NT)

    @pl.when(j == 2 * per_side - 1)
    def _():
        gain_one, shift_one, gain, shift = (norms_ref[i : i + 1] for i in range(4))

        def rows(r, held):
            normed, inverse = normalize(n_ref[r] * gain_one + shift_one + acc[r])
            o_ref[r] = (normed * gain + shift).astype(LOW)
            dy = cot_ref[r].astype(F32)
            back = unnormalize(dy * gain, normed, inverse)
            d_ref[r] = back
            f_ref[r] = back.astype(LOW)
            return held[0] + fold(dy * normed), held[1] + fold(dy)

        none = jnp.zeros((8, acc.shape[1]), F32)
        gains, shifts = by_rows(acc.shape[0], rows, (none, none))
        ng_ref[...] = jnp.concatenate(
            [jnp.sum(gains, axis=0, keepdims=True), jnp.sum(shifts, axis=0, keepdims=True), none[:6]], axis=0
        )


def down(active, normed, norms, cot, pieces, rows):
    width = STEP_WIDTH
    chunks, total = active.shape[0], active.shape[1]
    at = alternate(chunks // 2)
    shape = normed.shape
    count = (len(pieces) // 2 + 1) // 2
    return pl.pallas_call(
        functools.partial(down_kernel, chunks // 2, len(pieces)),
        grid=(chunks,),
        in_specs=[pl.BlockSpec((1, total, width), lambda j: (at(j), 0, 0)), full(shape), full(norms.shape), full(shape)]
        + [ANYWHERE] * len(pieces),
        out_specs=[full(shape), full(shape), full(shape), full(norms.shape)],
        out_shape=[shaped(shape, LOW), shaped(shape, F32), shaped(shape, LOW), shaped(norms.shape, F32)],
        scratch_shapes=chunk_buffer((count, rows), chunks, width) + [pltpu.VMEM(shape, F32)],
        compiler_params=params(56),
        name="down",
    )(active, normed, norms, cot, *pieces)


def share_out(value, own_ref, other_ref):
    core = lax.axis_index("c")
    z, x, _, rows, width = own_ref.shape
    value = value.reshape(z, x, 2, rows, width)
    for parity in range(2):
        part = value[:, :, parity]

        @pl.when(core == parity)
        def _(part=part):
            own_ref[:, :, 0] = part

        @pl.when(core != parity)
        def _(part=part):
            other_ref[:, :, 0] = part


def share_specs(count, rows, per_side, columns):
    spec = pl.BlockSpec((count, 2, 1, rows, STEP_WIDTH), lambda j: (0, 0, j // per_side, 0, j % per_side))
    return [spec] * 2, [shaped((count, 2, 2, rows, columns), LOW)] * 2


def weight_grad_kernel(a_ref, b_ref, own_ref, other_ref):
    share_out(mm(a_ref[...], b_ref[0], TN).astype(LOW), own_ref, other_ref)


def weight_grad(a, b, spec, chunks, count, rows, name):
    out_specs, out_shape = share_specs(count, rows, chunks // 2, chunks // 2 * STEP_WIDTH)
    return pl.pallas_call(
        weight_grad_kernel,
        grid=(chunks,),
        in_specs=[full(a.shape), spec],
        out_specs=out_specs,
        out_shape=out_shape,
        compiler_params=params(32),
        name=name,
    )(a, b)


def inner_kernel(per_side, down_count, f_ref, d_ref, h_ref, r_ref, n_ref, i_ref, norms_ref, *refs):
    downs, ups = refs[:down_count], refs[down_count : down_count + 10]
    own_ref, other_ref, g_ref, a_ref, ng_ref, wd, ds, wu, us, acc = refs[down_count + 10 :]
    j = pl.program_id(0)
    width = d_ref.shape[2]

    @pl.when(j == 0)
    def _():
        load_line_last(downs, wd, ds, width, per_side)
        load_square_last(ups, wu, us, 0, width, per_side)
        acc[...] = r_ref[...]

    ready(wd, ds, j)
    grad = (mm(f_ref[...], matrix(wd, j)) * d_ref[0].astype(F32)).astype(LOW)
    share_out(mm(h_ref[...], grad, TN).astype(LOW), own_ref, other_ref)
    ready(wu, us, j)
    acc[...] += mm(grad, matrix(wu, j), NT)

    @pl.when(j == 2 * per_side - 1)
    def _():
        gain = norms_ref[0:1]

        def rows(r, held):
            dy, normed = acc[r], n_ref[r]
            back = unnormalize(dy * gain, normed, i_ref[r][:, :1])
            g_ref[r] = back
            a_ref[r] = back.astype(LOW)
            return held[0] + fold(dy * normed), held[1] + fold(dy)

        none = jnp.zeros((8, acc.shape[1]), F32)
        gains, shifts = by_rows(acc.shape[0], rows, (none, none))
        ng_ref[...] = jnp.concatenate(
            [jnp.sum(gains, axis=0, keepdims=True), jnp.sum(shifts, axis=0, keepdims=True), none[:6]], axis=0
        )


def inner_back(feed_grad, slope, hidden, second_grad, normed, inverse, norms, downs, ups, rows, columns):
    chunks, total, width = slope.shape
    shape = normed.shape
    count = ups[0].shape[0]
    out_specs, out_shape = share_specs(count, rows, chunks // 2, columns)
    once = pl.Buffered(1)

    def held(a):
        return pl.BlockSpec(a.shape, lambda j: (0,) * a.ndim, pipeline_mode=once)

    return pl.pallas_call(
        functools.partial(inner_kernel, chunks // 2, len(downs)),
        grid=(chunks,),
        in_specs=[held(feed_grad), pl.BlockSpec((1, total, width), lambda j: (j, 0, 0))]
        + [held(a) for a in (hidden, second_grad, normed, inverse, norms)]
        + [ANYWHERE] * (len(downs) + 10),
        out_specs=out_specs + [full(shape), full(shape), full(norms.shape)],
        out_shape=out_shape + [shaped(shape, F32), shaped(shape, LOW), shaped(norms.shape, F32)],
        scratch_shapes=chunk_buffer((count, rows), chunks, width) * 2 + [pltpu.VMEM(shape, F32)],
        compiler_params=params(58),
        name="inner_back",
    )(feed_grad, slope, hidden, second_grad, normed, inverse, norms, *downs, *ups)


def out_kernel(column, a_ref, ctx_ref, one_ref, two_ref, own_in, other_in, *refs):
    pieces = refs[:10]
    own_ref, other_ref, o_ref, w, sem, tiles, out_sem = refs[10:]
    _, _, z, x, rows, _ = tiles.shape
    width = w.shape[5]
    core = lax.axis_index("c")
    load_square_last(pieces, w, sem, column, width, 1)
    norm_grads = jnp.concatenate([one_ref[0:2], two_ref[0:2], one_ref[2:6]], axis=0)
    for y in range(2):
        grad = mm(a_ref[...], ctx_ref[:, y * width : (y + 1) * width], TN).astype(LOW).reshape(z, x, 2, rows, width)
        for parity in range(2):
            slot = (parity + core) % 2
            tiles[slot, y, :, :, :, :width] = grad[:, :, parity]
            for at in range(z * x):
                cell = norm_grads[:, (at * 2 + parity) * rows : (at * 2 + parity + 1) * rows]
                cell = jnp.concatenate([cell, jnp.zeros((8, 128 - rows), F32)], axis=1)
                cell = jnp.concatenate([cell, jnp.zeros((rows - 8, 128), F32)], axis=0)
                tiles[slot, y, at // x, at % x, :, width:] = cell.astype(LOW)
    copies = []
    for slot, ref in enumerate((own_ref, other_ref)):
        for y in range(2):
            copies.append(
                pltpu.make_async_copy(
                    tiles.at[slot, y], ref.at[:, :, y, :, pl.ds(column, width + 128)], out_sem.at[slot, y]
                )
            )
    for copy in copies:
        copy.start()
    for y in range(2):
        ready(w, sem, y)
        o_ref[:, y * width : (y + 1) * width] = mm(a_ref[...], matrix(w, y)).astype(LOW)
    for copy in copies:
        copy.wait()


def out_back(branch_grad, context, one, two, own, other, pieces, rows, column):
    count, width = pieces[0].shape[0], STEP_WIDTH
    inside = pl.BlockSpec(memory_space=pltpu.VMEM)
    return pl.pallas_call(
        functools.partial(out_kernel, column),
        in_specs=[inside] * 4 + [ANYWHERE] * 12,
        out_specs=[ANYWHERE, ANYWHERE, inside],
        out_shape=[shaped(own.shape, LOW), shaped(other.shape, LOW), shaped(context.shape, LOW)],
        scratch_shapes=chunk_buffer((count, rows), 2, width)
        + [pltpu.VMEM((2, 2, count, 2, rows, width + 128), LOW), pltpu.SemaphoreType.DMA((2, 2))],
        input_output_aliases={4: 0, 5: 1},
        compiler_params=params(40),
        name="out_back",
    )(branch_grad, context, one, two, own, other, *pieces)


def attend_back_kernel(q_ref, k_ref, v_ref, bias_ref, l_ref, g_ref, o_ref):
    k, v, grad = k_ref[0], v_ref[0], g_ref[...]
    lane = lax.broadcasted_iota(jnp.int32, k.shape, 1)
    scale = HEAD**-0.5
    queries = q_ref[0]
    outs = []
    for h, (q, own_grad) in enumerate(zip(head_parts(queries, lane, scale), head_parts(grad, lane))):
        log_total = l_ref[:, h * HEAD : h * HEAD + 1]
        probs = jnp.exp(mm(q, k, NT) + bias_ref[...].astype(F32) - log_total)
        prob_grad = mm(own_grad, v, NT)
        score_grad = probs * (prob_grad - jnp.sum(probs * prob_grad, axis=-1, keepdims=True))
        score_grad = score_grad.astype(LOW)
        outs.append(
            (mm(score_grad, k) * scale, mm(score_grad, queries, TN) * scale, mm(probs.astype(LOW), grad, TN))
        )
    for i in range(3):
        o_ref[i] = jnp.where(lane < HEAD, outs[0][i], outs[1][i]).astype(LOW)


def attention_back(qkv, bias, logs, grad):
    total, width = grad.shape
    pairs = width // 128
    column = pl.BlockSpec((total, 128), lambda g: (0, g))
    return pl.pallas_call(
        attend_back_kernel,
        grid=(pairs,),
        in_specs=pair_specs(total, pairs // 2) + [full(bias.shape), column, column],
        out_specs=pl.BlockSpec((3, total, 128), lambda g: (0, 0, g)),
        out_shape=shaped((3, total, width), LOW),
        compiler_params=params(48),
        name="attention_back",
    )(qkv, qkv, qkv, bias, logs, grad)


def input_kernel(per_side, g_ref, r_ref, *refs):
    pieces, (o_ref, w, sem, acc) = refs[:10], refs[10:]
    j = pl.program_id(0)

    @pl.when(j == 0)
    def _():
        load_square_last(pieces, w, sem, 0, g_ref.shape[2], per_side)
        acc[...] = r_ref[...]

    chunk = alternate(per_side)(j)
    ready(w, sem, chunk)
    acc[...] += mm(g_ref[0], matrix(w, chunk), NT)

    @pl.when(j == 2 * per_side - 1)
    def _():
        o_ref[...] = acc[...].astype(LOW)


def input_back(grads, first_grad, pieces, rows):
    count, width = pieces[0].shape[0], STEP_WIDTH
    per_side = grads.shape[0]
    shape = first_grad.shape
    return pl.pallas_call(
        functools.partial(input_kernel, per_side),
        grid=(2 * per_side,),
        in_specs=[pl.BlockSpec((1, shape[0], width), lambda j: (j // 2, 0, j % 2)), full(shape)] + [ANYWHERE] * 10,
        out_specs=full(shape),
        out_shape=shaped(shape, LOW),
        scratch_shapes=chunk_buffer((count, rows), 2 * per_side, width) + [pltpu.VMEM(shape, F32)],
        compiler_params=params(40),
        name="input_back",
    )(grads, first_grad, *pieces)


def at(a, index, axis):
    return lax.dynamic_index_in_dim(a, index, axis, keepdims=False)


def sum_square_first(own, other):
    def take(x, y):
        return at(at(own, x, 1), y, 1).astype(F32) + at(at(other, x, 1), y, 1).astype(F32)

    half = own.shape[0] // 2
    column = ring_scatter(take, lambda a: (a[:half], a[half:]))
    return line_scatter(lambda z: at(column, z, 0))


def sum_line_first(own, other):
    square = line_scatter(lambda z: at(own, z, 0).astype(F32) + at(other, z, 0).astype(F32))
    half = own.shape[3] // 2
    return ring_scatter(lambda x, y: at(at(square, x, 0), y, 0), lambda a: (a[:half], a[half:]))


def sum_over_all(value):
    value = value + send(value, "c", SWAP)
    square = [send(value, ("x", "y"), tuple((i, i ^ k) for i in range(4))) for k in (1, 2, 3)]
    value = (value + square[0]) + (square[1] + square[2])
    count, k = lax.axis_size("z"), 1
    while k < count:
        value = value + send(value, "z", tuple((i, i ^ k) for i in range(count)))
        k *= 2
    return value


def pad_rows(a, total):
    return jnp.pad(a, ((0, total - a.shape[0]), (0, 0)))


def mask_bias(doc_row, reset_row, live, total):
    kinds = jnp.concatenate([jnp.full((MEM,), -1, jnp.int32), doc_row, jnp.full((MEM,), -2, jnp.int32)])
    real = kinds.shape[0]
    kinds = jnp.pad(kinds, (0, total - real), constant_values=-3)
    place = jnp.arange(total, dtype=jnp.int32)
    choose = kinds[:, None] == jnp.arange(reset_row.shape[0], dtype=jnp.int32)[None, :]
    reset_query = jnp.sum(jnp.where(choose, reset_row[None, :], 0), axis=1)
    same = kinds[:, None] == kinds[None, :]
    live_key = place < jnp.minimum(live, MEM)
    token_sees = same | (live_key[None, :] & (reset_query == 0)[:, None])
    memory_sees = ((place >= MEM) | live_key)[None, :]
    sees = jnp.where((kinds < 0)[:, None], memory_sees, token_sees) & (place < real)[None, :]
    return jnp.where(sees, 0.0, MASKED).astype(LOW)


def whole_segment(
    tokens,
    cotangent,
    doc_ids,
    reset_flags,
    mem_live,
    qkv_weight,
    qkv_moment,
    qkv_square,
    qkv_average,
    out_weight,
    out_moment,
    out_square,
    out_average,
    up_weight,
    up_moment,
    up_square,
    up_average,
    down_weight,
    down_moment,
    down_square,
    down_average,
    norm_params,
    norm_moment,
    norm_square,
    norm_average,
):
    y = lax.axis_index("y")
    rows, inner_part = up_weight.shape
    count = lax.axis_size("z")
    width = tokens.shape[2]
    part = qkv_weight.shape[2]
    real = tokens.shape[1]
    total = -(-real // ROWS_AT_ONCE) * ROWS_AT_ONCE

    def mine(a):
        return lax.dynamic_index_in_dim(a, y, 0, keepdims=False)

    qkv_block = jnp.concatenate([qkv_weight[k] for k in range(3)], axis=1).astype(LOW)
    norm_block = jnp.pad(norm_params.astype(LOW), ((0, rows - 4), (0, 128 - rows)))
    second_block = jnp.concatenate([up_weight.astype(LOW), out_weight.T.astype(LOW), norm_block], axis=1)
    down_block = down_weight.T.astype(LOW)

    x = pad_rows(mine(tokens), total)
    cot = pad_rows(mine(cotangent), total)
    bias = mask_bias(mine(doc_ids), mine(reset_flags), mine(mem_live), total)

    w_qkv = weights_square_last(qkv_block)
    w_second = weights_square_last(second_block)
    w_down = weights_line_last(down_block)

    qkv = project(x, w_qkv, rows)
    context, logs = attention(qkv, bias)
    hidden, normed, inverse, norms, active, slope = up(x, context, w_second, rows, inner_part)
    result, second_grad, feed_grad, norm_two = down(active, normed, norms, cot, w_down, rows)

    chunks = active.shape[0]
    own, other = weight_grad(
        feed_grad,
        active,
        pl.BlockSpec((1, total, STEP_WIDTH), lambda j: (j, 0, 0)),
        chunks,
        count,
        rows,
        "down_grad",
    )
    down_sum = sum_line_first(own, send(other, "c", SWAP))
    columns = inner_part + part + 128
    own, other, first_grad, branch_grad, norm_one = inner_back(
        feed_grad, slope, hidden, second_grad, normed, inverse, norms, w_down, w_second, rows, columns
    )
    own, other, context_grad = out_back(
        branch_grad, context, norm_one, norm_two, own, other, w_second, rows, inner_part
    )
    second_sum = sum_square_first(own, send(other, "c", SWAP))
    grads = attention_back(qkv, bias, logs, context_grad)
    own, other = weight_grad(
        x,
        grads,
        pl.BlockSpec((1, total, STEP_WIDTH), lambda j: (j % 3, 0, j // 3)),
        6,
        count,
        rows,
        "qkv_grad",
    )
    qkv_sum = sum_square_first(own, send(other, "c", SWAP))
    own_grad = input_back(grads, first_grad, w_qkv, rows)

    def both(own):
        own = own[:real]
        other = send(own, "y", SWAP)
        return jnp.where(y == 0, jnp.stack([own, other]), jnp.stack([other, own]))

    output = both(result)
    input_grad = both(own_grad).astype(F32)

    qkv_sum = qkv_sum.reshape(rows, 3, part).transpose(1, 0, 2)
    up_sum = second_sum[:, :inner_part]
    out_sum = second_sum[:, inner_part : inner_part + part].T
    norm_sum = second_sum[:4, inner_part + part : inner_part + part + rows]
    down_sum = down_sum.T
    local_squares = (
        jnp.sum(qkv_sum * qkv_sum)
        + jnp.sum(out_sum * out_sum)
        + jnp.sum(up_sum * up_sum)
        + jnp.sum(down_sum * down_sum)
        + jnp.sum(norm_sum * norm_sum) / lax.axis_size("y")
    )
    grad_norm = jnp.sqrt(sum_over_all(jnp.full((8, 128), local_squares))[0, 0])
    threshold = math.sqrt(4 * D * D + 2 * D * FF + 4 * D)
    factor = jnp.minimum(1.0, threshold / (grad_norm + 1e-06))
    new_qkv = adam_step(qkv_weight, qkv_moment, qkv_square, qkv_average, qkv_sum * factor, 0.02, 0.01)
    new_out = adam_step(out_weight, out_moment, out_square, out_average, out_sum * factor, 0.06, 0.01)
    new_up = adam_step(up_weight, up_moment, up_square, up_average, up_sum * factor, 0.02, 0.01)
    new_down = adam_step(down_weight, down_moment, down_square, down_average, down_sum * factor, 0.02, 0.01)
    new_norm = adam_step(norm_params, norm_moment, norm_square, norm_average, norm_sum * factor, 0.4, 0.0)
    return (output, input_grad, grad_norm) + new_qkv + new_out + new_up + new_down + new_norm


def solution(mesh):
    wide, narrow = mesh.shape["wide"], mesh.shape["narrow"]

    def placed(w, n):
        state = [P(None, w, n)] * 4 + [P(n, w)] * 4 + [P(w, n)] * 4 + [P(n, w)] * 4 + [P(None, w)] * 4
        return (
            tuple([P(w, None, None)] * 2 + [P(w, None)] * 2 + [P(w)] + state),
            tuple([P(w, None, None)] * 2 + [P()] + state),
        )

    def run(*args):
        if narrow == 2 and wide % 8 == 0 and args[0].shape[0] == wide * narrow:
            body = whole_segment
            grid = jax.sharding.Mesh(mesh.devices.reshape(wide // 4, 2, 2, 2), ("z", "x", "c", "y"))
            ins, outs = placed(("z", "x", "c"), "y")
        else:
            body, grid = shared_rows, mesh
            ins, outs = placed("wide", "narrow")
        return jax.shard_map(body, mesh=grid, in_specs=ins, out_specs=outs, check_vma=False)(*args)

    return run
```

profile of v0, /device:TPU:0, one launch (start us, length us, event | category | flops | bytes accessed | tf_op | source)
XLA Modules:
  0.0 584.6 jit_solution(4259768492820160256)
XLA Ops:
  1.9 4.9 collective-permute-start
  9.3 4.6 collective-permute-start.15
  17.2 3.4 collective-permute-done.15.refs_1_
  21.3 5.5 collective-permute-done.18.refs_4_
  32.8 7.7 %collective-permute-done.5.refs_6_ = bf16[64,1536]{1,0:T(8,128)(2,1)S(1)} collective-permute-done((bf16[64,1536]{1,0:T(8,128)(2,1)S(1)}, bf16[64,1536]{1,0:T(8,128)(2,1)S(1)}, u32[]{:S(2)}, u32[]{:S(2)}) %collective-permute-start.5) | collective-permute-done | bytes 196640 | tf_op jit(solution)/shard_map/ppermute | solution.py:285
  41.2 2.2 join_column.2.refs_0_
  49.8 3.0 collective-permute-done.31.right
  53.3 9.5 %collective-permute-done.32.far_one = bf16[32,2048]{1,0:T(8,128)(2,1)S(1)} collective-permute-done((bf16[32,2048]{1,0:T(8,128)(2,1)S(1)}, bf16[32,2048]{1,0:T(8,128)(2,1)S(1)}, u32[]{:S(2)}, u32[]{:S(2)}) %collective-permute-start.32) | collective-permute-done | bytes 131104 | tf_op jit(solution)/shard_map/ppermute | solution.py:285
  65.0 2.2 join_square.1.refs_0_
  67.3 2.3 collective-permute-start.34
  72.5 6.1 %collective-permute-done.7.refs_2_ = bf16[4,64,1536]{2,1,0:T(8,128)(2,1)} collective-permute-done((bf16[4,64,1536]{2,1,0:T(8,128)(2,1)}, bf16[4,64,1536]{2,1,0:T(8,128)(2,1)}, u32[]{:S(2)}, u32[]{:S(2)}) %collective-permute-start.7) | collective-permute-done | bytes 786464 | tf_op jit(solution)/shard_map/ppermute | solution.py:285
  80.2 2.4 join_column.3.refs_0_.refs_14_
  89.0 3.6 collective-permute-done.37.refs_4_
  103.1 11.8 %collective-permute-done.21.refs_1_.refs_15_ = bf16[4,64,2688]{2,1,0:T(8,128)(2,1)S(1)} collective-permute-done((bf16[4,64,2688]{2,1,0:T(8,128)(2,1)}, bf16[4,64,2688]{2,1,0:T(8,128)(2,1)S(1)}, u32[]{:S(2)}, u32[]{:S(2)}) %collective-permute-start.21) | collective-permute-done | bytes 1376288 | tf_op jit(solution)/shard_map/ppermute | solution.py:285
  114.9 14.7 %collective-permute-done.22.refs_2_.refs_16_ = bf16[4,64,2688]{2,1,0:T(8,128)(2,1)S(1)} collective-permute-done((bf16[4,64,2688]{2,1,0:T(8,128)(2,1)}, bf16[4,64,2688]{2,1,0:T(8,128)(2,1)S(1)}, u32[]{:S(2)}, u32[]{:S(2)}) %collective-permute-start.22) | collective-permute-done | bytes 1376288 | tf_op jit(solution)/shard_map/ppermute | solution.py:285
  133.1 13.8 %collective-permute-done.23.refs_3_.refs_17_ = bf16[2,64,2688]{2,1,0:T(8,128)(2,1)} collective-permute-done((bf16[2,64,2688]{2,1,0:T(8,128)(2,1)S(1)}, bf16[2,64,2688]{2,1,0:T(8,128)(2,1)}, u32[]{:S(2)}, u32[]{:S(2)}) %collective-permute-start.23) | collective-permute-done | bytes 688160 | tf_op jit(solution)/shard_map/ppermute | solution.py:285
  149.4 6.9 %constant_dynamic-slice_fusion = (bf16[1,532,1024]{2,0,1:T(2,128)(2,1)S(1)}, bf16[1,532,1024]{2,0,1:T(2,128)(2,1)S(1)}) fusion(bf16[2,532,1024]{2,0,1:T(2,128)(2,1)} %param.26, s32[]{:T(128)S(6)} %select_n.200, bf16[2,532,1024]{2,0,1:T(2,128)(2,1)} %param.25), kind=kLoop, calls=%fused_computation.145 | loop fusion | bytes 4358148 | tf_op jit(solution)/shard_map/jit(dynamic_index_in_dim)/dynamic_slice | solution.py:1019
  156.3 16.9 %collective-permute-done.39.refs_6_ = bf16[2,2,64,2048]{3,2,1,0:T(8,128)(2,1)} collective-permute-done((bf16[2,2,64,2048]{3,2,1,0:T(8,128)(2,1)}, bf16[2,2,64,2048]{3,2,1,0:T(8,128)(2,1)}, u32[]{:S(2)}, u32[]{:S(2)}) %collective-permute-start.39) | collective-permute-done | bytes 1048608 | tf_op jit(solution)/shard_map/ppermute | solution.py:285
  179.1 6.1 %project.1.q_ref.k_ref.v_ref = bf16[6,544,512]{2,1,0:T(8,128)(2,1)S(1)} custom-call(bf16[544,1024]{1,0:T(8,128)(2,1)S(1)} %pad.15.x_ref.a_ref, bf16[4,64,1536]{2,1,0:T(8,128)(2,1)S(1)} %copy-done.16, bf16[4,64,1536]{2,1,0:T(8,128)(2,1)} %collective-permute-done.6.refs_1_, bf16[4,64,1536]{2,1,0:T(8,128)(2,1)} %collective-permute-done.7.refs_2_, ...), custom_call_target="tpu_custom_call" | custom-call | tf_op jit(solution)/shard_map/project/pallas_call | solution.py:506
  187.0 17.4 %attention.1 = (bf16[544,1024]{1,0:T(8,128)(2,1)S(1)}, f32[544,1024]{1,0:T(8,128)S(1)}) custom-call(bf16[6,544,512]{2,1,0:T(8,128)(2,1)} %copy-done.2, bf16[6,544,512]{2,1,0:T(8,128)(2,1)} %copy-done.2, bf16[6,544,512]{2,1,0:T(8,128)(2,1)} %copy-done.2, bf16[544,544]{1,0:T(8,128)(2,1)S(1)} %select_convert_fusion.bias_ref), custom_call_target="tpu_custom_call" | custom-call | tf_op jit(solution)/shard_map/attention/pallas_call | solution.py:549
  206.8 22.2 %up.1 = (bf16[544,1024]{1,0:T(8,128)(2,1)}, f32[544,1024]{1,0:T(8,128)}, f32[544,128]{1,0:T(8,128)}, f32[8,1024]{1,0:T(8,128)}, bf16[8,544,512]{2,1,0:T(8,128)(2,1)}, /*index=5*/bf16[8,544,512]{2,1,0:T(8,128)(2,1)}) custom-call(bf16[544,1024]{1,0:T(8,128)(2,1)} %copy-done.6, bf16[544,1024]{1,0:T(8,128)(2,1)} %copy-done.20, ...), custom_call_target="tpu_custom_call" | custom-call | tf_op jit(solution)/shard_map/up/pallas_call | solution.py:642
  230.4 18.8 %down.1 = (bf16[544,1024]{1,0:T(8,128)(2,1)}, f32[544,1024]{1,0:T(8,128)}, bf16[544,1024]{1,0:T(8,128)(2,1)}, f32[8,1024]{1,0:T(8,128)}) custom-call(bf16[8,544,512]{2,1,0:T(8,128)(2,1)} %get-tuple-element.48.g_ref.b_ref, f32[544,1024]{1,0:T(8,128)} %get-tuple-element.49.n_ref, f32[8,1024]{1,0:T(8,128)} %get-tuple-element.50.norms_ref, ...), custom_call_target="tpu_custom_call" | custom-call | tf_op jit(solution)/shard_map/down/pallas_call | solution.py:704
  249.2 32.0 %inner_back.1 = (bf16[4,2,2,64,2688]{4,3,2,1,0:T(8,128)(2,1)}, bf16[4,2,2,64,2688]{4,3,2,1,0:T(8,128)(2,1)}, f32[544,1024]{1,0:T(8,128)}, bf16[544,1024]{1,0:T(8,128)(2,1)}, f32[8,1024]{1,0:T(8,128)}) custom-call(bf16[544,1024]{1,0:T(8,128)(2,1)} %get-tuple-element.53.f_ref.a_ref, bf16[8,544,512]{2,1,0:T(8,128)(2,1)} %get-tuple-element.54.d_ref, ...), custom_call_target="tpu_custom_call" | custom-call | tf_op jit(solution)/shard_map/inner_back/pallas_call | solution.py:801
  284.6 3.8 out_back.1
  288.4 25.4 %attention_back.1.g_ref.b_ref = bf16[3,544,1024]{2,1,0:T(8,128)(2,1)} custom-call(bf16[6,544,512]{2,1,0:T(8,128)(2,1)} %copy-done.2, bf16[6,544,512]{2,1,0:T(8,128)(2,1)} %copy-done.2, bf16[6,544,512]{2,1,0:T(8,128)(2,1)} %copy-done.2, bf16[544,544]{1,0:T(8,128)(2,1)S(1)} %copy-done.19, f32[544,1024]{1,0:T(8,128)S(1)} %copy-done.35, ...), custom_call_target="tpu_custom_call" | custom-call | tf_op jit(solution)/shard_map/attention_back/pallas_call | solution.py:889
  313.8 1.9 copy-done.3
  315.8 8.4 %qkv_grad.1 = (bf16[4,2,2,64,1536]{4,3,2,1,0:T(8,128)(2,1)S(1)}, bf16[4,2,2,64,1536]{4,3,2,1,0:T(8,128)(2,1)}) custom-call(bf16[544,1024]{1,0:T(8,128)(2,1)S(1)} %copy-done.7, bf16[3,544,1024]{2,1,0:T(8,128)(2,1)S(1)} %copy-done.3), custom_call_target="tpu_custom_call" | custom-call | tf_op jit(solution)/shard_map/qkv_grad/pallas_call | solution.py:744
  324.6 10.4 %down_grad.1 = (bf16[4,2,2,64,2048]{4,3,2,1,0:T(8,128)(2,1)S(1)}, bf16[4,2,2,64,2048]{4,3,2,1,0:T(8,128)(2,1)}) custom-call(bf16[544,1024]{1,0:T(8,128)(2,1)S(1)} %copy-done.22, bf16[8,544,512]{2,1,0:T(8,128)(2,1)S(1)} %bitcast.219), custom_call_target="tpu_custom_call" | custom-call | tf_op jit(solution)/shard_map/down_grad/pallas_call | solution.py:744
  334.9 2.0 copy-done.12
  337.1 5.4 copy.125
  342.9 1.9 convert_add_fusion.3
  348.3 7.7 %collective-permute-done.50 = bf16[2,64,1536]{2,1,0:T(8,128)(2,1)S(1)} collective-permute-done((bf16[2,64,1536]{2,1,0:T(8,128)(2,1)S(1)}, bf16[2,64,1536]{2,1,0:T(8,128)(2,1)S(1)}, u32[]{:S(2)}, u32[]{:S(2)}) %collective-permute-start.50) | collective-permute-done | bytes 393248 | tf_op jit(solution)/shard_map/ppermute | solution.py:285
  370.3 6.6 %input_back.1 = bf16[544,1024]{1,0:T(8,128)(2,1)S(1)} custom-call(bf16[3,544,1024]{2,1,0:T(8,128)(2,1)S(1)} %copy-done.4, f32[544,1024]{1,0:T(8,128)S(1)} %copy-done.33, bf16[4,64,1536]{2,1,0:T(8,128)(2,1)S(1)} %copy-done.17, bf16[4,64,1536]{2,1,0:T(8,128)(2,1)} %collective-permute-done.6.refs_1_, bf16[4,64,1536]{2,1,0:T(8,128)(2,1)} %collective-permute-done.7.refs_2_, ...), custom_call_target="tpu_custom_call" | custom-call | tf_op jit(solution)/shard_map/input_back/pallas_call | solution.py:922
  377.0 2.5 fusion.12
  383.4 2.4 fusion.7
  387.8 16.7 %collective-permute-done.72 = bf16[2,2,64,2048]{3,2,1,0:T(8,128)(2,1)S(1)} collective-permute-done((bf16[2,2,64,2048]{3,2,1,0:T(8,128)(2,1)S(1)}, bf16[2,2,64,2048]{3,2,1,0:T(8,128)(2,1)S(1)}, u32[]{:S(2)}, u32[]{:S(2)}) %collective-permute-start.72) | collective-permute-done | bytes 1048608 | tf_op jit(solution)/shard_map/ppermute | solution.py:285
  404.5 1.8 fusion.4
  406.3 4.4 collective-permute-start.73
  410.7 3.4 convert_add_fusion.1
  415.6 11.6 %collective-permute-done.61 = bf16[2,64,2688]{2,1,0:T(8,128)(2,1)S(1)} collective-permute-done((bf16[2,64,2688]{2,1,0:T(8,128)(2,1)S(1)}, bf16[2,64,2688]{2,1,0:T(8,128)(2,1)S(1)}, u32[]{:S(2)}, u32[]{:S(2)}) %collective-permute-start.61) | collective-permute-done | bytes 688160 | tf_op jit(solution)/shard_map/ppermute | solution.py:285
  427.3 1.7 collective-permute-start.63
  429.3 12.5 %collective-permute-done.63 = bf16[2,64,2688]{2,1,0:T(8,128)(2,1)S(1)} collective-permute-done((bf16[2,64,2688]{2,1,0:T(8,128)(2,1)S(1)}, bf16[2,64,2688]{2,1,0:T(8,128)(2,1)S(1)}, u32[]{:S(2)}, u32[]{:S(2)}) %collective-permute-start.63) | collective-permute-done | bytes 688160 | tf_op jit(solution)/shard_map/ppermute | solution.py:285
  442.6 1.9 collective-permute-start.64
  444.6 2.2 collective-permute-start.55
  451.2 3.0 fusion.5
  454.9 17.9 %collective-permute-done.62 = bf16[4,64,2688]{2,1,0:T(8,128)(2,1)S(1)} collective-permute-done((bf16[4,64,2688]{2,1,0:T(8,128)(2,1)S(1)}, bf16[4,64,2688]{2,1,0:T(8,128)(2,1)S(1)}, u32[]{:S(2)}, u32[]{:S(2)}) %collective-permute-start.62) | collective-permute-done | bytes 1376288 | tf_op jit(solution)/shard_map/ppermute | solution.py:285
  472.9 2.2 collective-permute-start.74
  476.0 2.1 fusion
  478.2 2.2 collective-permute-start.65
  480.4 1.8 fusion.3
  483.4 13.3 %collective-permute-done.65 = bf16[64,2688]{1,0:T(8,128)(2,1)S(1)} collective-permute-done((bf16[64,2688]{1,0:T(8,128)(2,1)S(1)}, bf16[64,2688]{1,0:T(8,128)(2,1)S(1)}, u32[]{:S(2)}, u32[]{:S(2)}) %collective-permute-start.65) | collective-permute-done | bytes 344096 | tf_op jit(solution)/shard_map/ppermute | solution.py:285
  497.5 4.4 collective-permute-start.66
  502.0 1.9 collective-permute-start.56
  503.9 2.7 collective-permute-done.66
  508.1 1.8 fusion.6
  510.0 2.5 collective-permute-start.78
  514.2 2.9 collective-permute-done.78
  520.1 16.1 %collective-permute-start.67 = (bf16[64,2688]{1,0:T(8,128)(2,1)S(1)}, bf16[64,2688]{1,0:T(8,128)(2,1)S(1)}, u32[]{:S(2)}, u32[]{:S(2)}) collective-permute-start(bf16[64,2688]{1,0:T(8,128)(2,1)S(1)} %get-tuple-element.194), channel_id=1, source_target_pairs={{0,8},{8,16},{16,24},{1,9},{9,17},{17,25},{2,10},{10,18},{18,26},{... | collective-permute-start | bytes 1032200 | tf_op jit(solution)/shard_map/ppermute | solution.py:285
  541.2 4.2 collective-permute-done.70
  558.7 2.6 maximum_select_fusion
  562.1 2.1 fusion.1
  564.2 5.4 copy.131
  569.7 3.6 copy.130
  575.2 3.2 multiply_add_fusion.1
  (431 shorter events, 126.6 us)
Async XLA Ops:
  1.9 13.3 %collective-permute-start = (bf16[64,1536]{1,0:T(8,128)(2,1)S(1)}, bf16[64,1536]{1,0:T(8,128)(2,1)S(1)}, u32[]{:S(2)}, u32[]{:S(2)}) collective-permute-start(bf16[64,1536]{1,0:T(8,128)(2,1)S(1)} %pad_maximum_fusion.6.refs_0_), channel_id=1, source_target_pairs={{0,8},{8,16},{16,24},{1,9},{9,17},{17,25},{2,10},{10,18},{18,26},{... | collective-permute-start | bytes 589832 | tf_op jit(solution)/shard_map/ppermute | solution.py:285
  13.8 12.9 %collective-permute-start.18 = (bf16[64,2688]{1,0:T(8,128)(2,1)S(1)}, bf16[64,2688]{1,0:T(8,128)(2,1)S(1)}, u32[]{:S(2)}, u32[]{:S(2)}) collective-permute-start(bf16[64,2688]{1,0:T(8,128)(2,1)S(1)} %fusion.40.refs_0_), channel_id=1, source_target_pairs={{24,16},{16,8},{8,0},{25,17},{17,9},{9,1},{26,18},{18,10},{10,2},{... | collective-permute-start | bytes 1032200 | tf_op jit(solution)/shard_map/ppermute | solution.py:285
  15.2 12.9 %collective-permute-start.1 = (bf16[64,1536]{1,0:T(8,128)(2,1)S(1)}, bf16[64,1536]{1,0:T(8,128)(2,1)S(1)}, u32[]{:S(2)}, u32[]{:S(2)}) collective-permute-start(bf16[64,1536]{1,0:T(8,128)(2,1)S(1)} %collective-permute-done.refs_1_), channel_id=1, source_target_pairs={{8,16},{16,24},{9,17},{17,25},{10,18},{18,26},{11,19},{19,27},{12,... | collective-permute-start | bytes 589832 | tf_op jit(solution)/shard_map/ppermute | solution.py:285
  15.9 14.0 %collective-permute-start.4 = (bf16[64,1536]{1,0:T(8,128)(2,1)S(1)}, bf16[64,1536]{1,0:T(8,128)(2,1)S(1)}, u32[]{:S(2)}, u32[]{:S(2)}) collective-permute-start(bf16[64,1536]{1,0:T(8,128)(2,1)S(1)} %collective-permute-done.3.refs_4_), channel_id=1, source_target_pairs={{16,8},{8,0},{17,9},{9,1},{18,10},{10,2},{19,11},{11,3},{20,12},{1... | collective-permute-start | bytes 589832 | tf_op jit(solution)/shard_map/ppermute | solution.py:285
  20.6 24.9 %collective-permute-start.16 = (bf16[64,2688]{1,0:T(8,128)(2,1)S(1)}, bf16[64,2688]{1,0:T(8,128)(2,1)S(1)}, u32[]{:S(2)}, u32[]{:S(2)}) collective-permute-start(bf16[64,2688]{1,0:T(8,128)(2,1)S(1)} %collective-permute-done.15.refs_1_), channel_id=1, source_target_pairs={{8,16},{16,24},{9,17},{17,25},{10,18},{18,26},{11,19},{19,27},{12,... | collective-permute-start | bytes 1032200 | tf_op jit(solution)/shard_map/ppermute | solution.py:285
  26.7 20.1 %collective-permute-start.19 = (bf16[64,2688]{1,0:T(8,128)(2,1)S(1)}, bf16[64,2688]{1,0:T(8,128)(2,1)}, u32[]{:S(2)}, u32[]{:S(2)}) collective-permute-start(bf16[64,2688]{1,0:T(8,128)(2,1)S(1)} %collective-permute-done.18.refs_4_), channel_id=1, source_target_pairs={{16,8},{8,0},{17,9},{9,1},{18,10},{10,2},{19,11},{11,3},{20,12},{1... | collective-permute-start | bytes 1032200 | tf_op jit(solution)/shard_map/ppermute | solution.py:285
  31.3 16.9 %collective-permute-start.30 = (bf16[64,2048]{1,0:T(8,128)(2,1)S(1)}, bf16[64,2048]{1,0:T(8,128)(2,1)S(1)}, u32[]{:S(2)}, u32[]{:S(2)}) collective-permute-start(bf16[64,2048]{1,0:T(8,128)(2,1)S(1)} %convert_bitcast_fusion.own), channel_id=1, source_target_pairs={{0,1},{1,5},{5,4},{4,0},{2,3},{3,7},{7,6},{6,2},{8,9},{9,13},{13,1... | collective-permute-start | bytes 786440 | tf_op jit(solution)/shard_map/ppermute | solution.py:285
  43.4 27.6 %collective-permute-start.6 = (bf16[4,64,1536]{2,1,0:T(8,128)(2,1)}, bf16[4,64,1536]{2,1,0:T(8,128)(2,1)}, u32[]{:S(2)}, u32[]{:S(2)}) collective-permute-start(bf16[4,64,1536]{2,1,0:T(8,128)(2,1)} %join_column.2.refs_0_), channel_id=1, source_target_pairs={{0,1},{1,5},{5,4},{4,0},{2,3},{3,7},{7,6},{6,2},{8,9},{9,13},{13,1... | collective-permute-start | bytes 2359304 | tf_op jit(solution)/shard_map/ppermute | solution.py:285
  45.5 24.1 %collective-permute-start.17 = (bf16[64,2688]{1,0:T(8,128)(2,1)S(1)}, bf16[64,2688]{1,0:T(8,128)(2,1)}, u32[]{:S(2)}, u32[]{:S(2)}) collective-permute-start(bf16[64,2688]{1,0:T(8,128)(2,1)S(1)} %collective-permute-done.16.refs_2_), channel_id=1, source_target_pairs={{16,24},{17,25},{18,26},{19,27},{20,28},{21,29},{22,30},{23,31}} | collective-permute-start | bytes 1032200 | tf_op jit(solution)/shard_map/ppermute | solution.py:285
  46.9 24.0 %collective-permute-start.20 = (bf16[64,2688]{1,0:T(8,128)(2,1)}, bf16[64,2688]{1,0:T(8,128)(2,1)}, u32[]{:S(2)}, u32[]{:S(2)}) collective-permute-start(bf16[64,2688]{1,0:T(8,128)(2,1)} %collective-permute-done.19.refs_5_), channel_id=1, source_target_pairs={{8,0},{9,1},{10,2},{11,3},{12,4},{13,5},{14,6},{15,7}} | collective-permute-start | bytes 1032200 | tf_op jit(solution)/shard_map/ppermute | solution.py:285
  48.2 14.6 %collective-permute-start.32 = (bf16[32,2048]{1,0:T(8,128)(2,1)S(1)}, bf16[32,2048]{1,0:T(8,128)(2,1)S(1)}, u32[]{:S(2)}, u32[]{:S(2)}) collective-permute-start(bf16[32,2048]{1,0:T(8,128)(2,1)S(1)} %slice.208), channel_id=1, source_target_pairs={{0,1},{1,5},{5,4},{4,0},{2,3},{3,7},{7,6},{6,2},{8,9},{9,13},{13,1... | collective-permute-start | bytes 393224 | tf_op jit(solution)/shard_map/ppermute | solution.py:285
  52.8 11.5 %collective-permute-start.33 = (bf16[32,2048]{1,0:T(8,128)(2,1)S(1)}, bf16[32,2048]{1,0:T(8,128)(2,1)S(1)}, u32[]{:S(2)}, u32[]{:S(2)}) collective-permute-start(bf16[32,2048]{1,0:T(8,128)(2,1)S(1)} %slice.209), channel_id=1, source_target_pairs={{1,0},{5,1},{4,5},{0,4},{3,2},{7,3},{6,7},{2,6},{9,8},{13,9},{12,1... | collective-permute-start | bytes 393224 | tf_op jit(solution)/shard_map/ppermute | solution.py:285
  62.8 15.8 %collective-permute-start.7 = (bf16[4,64,1536]{2,1,0:T(8,128)(2,1)}, bf16[4,64,1536]{2,1,0:T(8,128)(2,1)}, u32[]{:S(2)}, u32[]{:S(2)}) collective-permute-start(bf16[4,64,1536]{2,1,0:T(8,128)(2,1)} %join_column.2.refs_0_), channel_id=1, source_target_pairs={{1,0},{5,1},{4,5},{0,4},{3,2},{7,3},{6,7},{2,6},{9,8},{13,9},{12,1... | collective-permute-start | bytes 2359304 | tf_op jit(solution)/shard_map/ppermute | solution.py:285
  67.3 20.2 %collective-permute-start.34 = (bf16[2,2,64,2048]{3,2,1,0:T(8,128)(2,1)}, bf16[2,2,64,2048]{3,2,1,0:T(8,128)(2,1)}, u32[]{:S(2)}, u32[]{:S(2)}) collective-permute-start(bf16[2,2,64,2048]{3,2,1,0:T(8,128)(2,1)} %join_square.1.refs_0_), channel_id=1, source_target_pairs={{0,8},{8,16},{16,24},{1,9},{9,17},{17,25},{2,10},{10,18},{18,26},{... | collective-permute-start | bytes 3145736 | tf_op jit(solution)/shard_map/ppermute | solution.py:285
  69.6 23.0 %collective-permute-start.37 = (bf16[2,2,64,2048]{3,2,1,0:T(8,128)(2,1)}, bf16[2,2,64,2048]{3,2,1,0:T(8,128)(2,1)}, u32[]{:S(2)}, u32[]{:S(2)}) collective-permute-start(bf16[2,2,64,2048]{3,2,1,0:T(8,128)(2,1)} %join_square.1.refs_0_), channel_id=1, source_target_pairs={{24,16},{16,8},{8,0},{25,17},{17,9},{9,1},{26,18},{18,10},{10,2},{... | collective-permute-start | bytes 3145736 | tf_op jit(solution)/shard_map/ppermute | solution.py:285
  70.9 11.7 %collective-permute-start.10 = (bf16[4,64,1536]{2,1,0:T(8,128)(2,1)S(1)}, bf16[4,64,1536]{2,1,0:T(8,128)(2,1)S(1)}, u32[]{:S(2)}, u32[]{:S(2)}) collective-permute-start(bf16[4,64,1536]{2,1,0:T(8,128)(2,1)S(1)} %copy-done.16), channel_id=1, source_target_pairs={{0,2},{2,0},{1,3},{3,1},{4,6},{6,4},{5,7},{7,5},{8,10},{10,8},{9,1... | collective-permute-start | bytes 2359304 | tf_op jit(solution)/shard_map/ppermute | solution.py:285
  71.0 22.8 %collective-permute-start.40 = (bf16[2,2,64,2048]{3,2,1,0:T(8,128)(2,1)}, bf16[2,2,64,2048]{3,2,1,0:T(8,128)(2,1)}, u32[]{:S(2)}, u32[]{:S(2)}) collective-permute-start(bf16[2,2,64,2048]{3,2,1,0:T(8,128)(2,1)} %join_square.1.refs_0_), channel_id=1, source_target_pairs={{0,2},{2,0},{1,3},{3,1},{4,6},{6,4},{5,7},{7,5},{8,10},{10,8},{9,1... | collective-permute-start | bytes 3145736 | tf_op jit(solution)/shard_map/ppermute | solution.py:285
  78.6 14.0 %collective-permute-start.8 = (bf16[2,64,1536]{2,1,0:T(8,128)(2,1)S(1)}, bf16[2,64,1536]{2,1,0:T(8,128)(2,1)S(1)}, u32[]{:S(2)}, u32[]{:S(2)}) collective-permute-start(bf16[2,64,1536]{2,1,0:T(8,128)(2,1)S(1)} %slice.204), channel_id=1, source_target_pairs={{0,1},{1,5},{5,4},{4,0},{2,3},{3,7},{7,6},{6,2},{8,9},{9,13},{13,1... | collective-permute-start | bytes 1179656 | tf_op jit(solution)/shard_map/ppermute | solution.py:285
  83.5 31.4 %collective-permute-start.21 = (bf16[4,64,2688]{2,1,0:T(8,128)(2,1)}, bf16[4,64,2688]{2,1,0:T(8,128)(2,1)S(1)}, u32[]{:S(2)}, u32[]{:S(2)}) collective-permute-start(bf16[4,64,2688]{2,1,0:T(8,128)(2,1)} %join_column.3.refs_0_.refs_14_), channel_id=1, source_target_pairs={{0,1},{1,5},{5,4},{4,0},{2,3},{3,7},{7,6},{6,2},{8,9},{9,13},{13,1... | collective-permute-start | bytes 4128776 | tf_op jit(solution)/shard_map/ppermute | solution.py:285
  96.8 32.8 %collective-permute-start.22 = (bf16[4,64,2688]{2,1,0:T(8,128)(2,1)}, bf16[4,64,2688]{2,1,0:T(8,128)(2,1)S(1)}, u32[]{:S(2)}, u32[]{:S(2)}) collective-permute-start(bf16[4,64,2688]{2,1,0:T(8,128)(2,1)} %join_column.3.refs_0_.refs_14_), channel_id=1, source_target_pairs={{1,0},{5,1},{4,5},{0,4},{3,2},{7,3},{6,7},{2,6},{9,8},{13,9},{12,1... | collective-permute-start | bytes 4128776 | tf_op jit(solution)/shard_map/ppermute | solution.py:285
  99.1 31.5 %collective-permute-start.35 = (bf16[2,2,64,2048]{3,2,1,0:T(8,128)(2,1)}, bf16[2,2,64,2048]{3,2,1,0:T(8,128)(2,1)S(1)}, u32[]{:S(2)}, u32[]{:S(2)}) collective-permute-start(bf16[2,2,64,2048]{3,2,1,0:T(8,128)(2,1)} %collective-permute-done.34.refs_1_), channel_id=1, source_target_pairs={{8,16},{16,24},{9,17},{17,25},{10,18},{18,26},{11,19},{19,27},{12,... | collective-permute-start | bytes 3145736 | tf_op jit(solution)/shard_map/ppermute | solution.py:285
  100.7 30.6 %collective-permute-start.25 = (bf16[4,64,2688]{2,1,0:T(8,128)(2,1)}, bf16[4,64,2688]{2,1,0:T(8,128)(2,1)S(1)}, u32[]{:S(2)}, u32[]{:S(2)}) collective-permute-start(bf16[4,64,2688]{2,1,0:T(8,128)(2,1)} %join_column.3.refs_0_.refs_14_), channel_id=1, source_target_pairs={{0,2},{2,0},{1,3},{3,1},{4,6},{6,4},{5,7},{7,5},{8,10},{10,8},{9,1... | collective-permute-start | bytes 4128776 | tf_op jit(solution)/shard_map/ppermute | solution.py:285
  101.8 30.7 %collective-permute-start.38 = (bf16[2,2,64,2048]{3,2,1,0:T(8,128)(2,1)}, bf16[2,2,64,2048]{3,2,1,0:T(8,128)(2,1)}, u32[]{:S(2)}, u32[]{:S(2)}) collective-permute-start(bf16[2,2,64,2048]{3,2,1,0:T(8,128)(2,1)} %collective-permute-done.37.refs_4_), channel_id=1, source_target_pairs={{16,8},{8,0},{17,9},{9,1},{18,10},{10,2},{19,11},{11,3},{20,12},{1... | collective-permute-start | bytes 3145736 | tf_op jit(solution)/shard_map/ppermute | solution.py:285
  114.9 17.6 %collective-permute-start.41 = (bf16[2,2,64,2048]{3,2,1,0:T(8,128)(2,1)}, bf16[2,2,64,2048]{3,2,1,0:T(8,128)(2,1)S(1)}, u32[]{:S(2)}, u32[]{:S(2)}) collective-permute-start(bf16[2,2,64,2048]{3,2,1,0:T(8,128)(2,1)} %collective-permute-done.34.refs_1_), channel_id=1, source_target_pairs={{0,2},{2,0},{1,3},{3,1},{4,6},{6,4},{5,7},{7,5},{8,10},{10,8},{9,1... | collective-permute-start | bytes 3145736 | tf_op jit(solution)/shard_map/ppermute | solution.py:285
  129.6 17.3 %collective-permute-start.23 = (bf16[2,64,2688]{2,1,0:T(8,128)(2,1)S(1)}, bf16[2,64,2688]{2,1,0:T(8,128)(2,1)}, u32[]{:S(2)}, u32[]{:S(2)}) collective-permute-start(bf16[2,64,2688]{2,1,0:T(8,128)(2,1)S(1)} %slice.206), channel_id=1, source_target_pairs={{0,1},{1,5},{5,4},{4,0},{2,3},{3,7},{7,6},{6,2},{8,9},{9,13},{13,1... | collective-permute-start | bytes 2064392 | tf_op jit(solution)/shard_map/ppermute | solution.py:285
  130.5 17.9 %collective-permute-start.36 = (bf16[2,2,64,2048]{3,2,1,0:T(8,128)(2,1)S(1)}, bf16[2,2,64,2048]{3,2,1,0:T(8,128)(2,1)S(1)}, u32[]{:S(2)}, u32[]{:S(2)}) collective-permute-start(bf16[2,2,64,2048]{3,2,1,0:T(8,128)(2,1)S(1)} %collective-permute-done.35.refs_2_), channel_id=1, source_target_pairs={{16,24},{17,25},{18,26},{19,27},{20,28},{21,29},{22,30},{23,31}} | collective-permute-start | bytes 3145736 | tf_op jit(solution)/shard_map/ppermute | solution.py:285
  131.3 17.0 %collective-permute-start.24 = (bf16[2,64,2688]{2,1,0:T(8,128)(2,1)S(1)}, bf16[2,64,2688]{2,1,0:T(8,128)(2,1)}, u32[]{:S(2)}, u32[]{:S(2)}) collective-permute-start(bf16[2,64,2688]{2,1,0:T(8,128)(2,1)S(1)} %slice.207), channel_id=1, source_target_pairs={{1,0},{5,1},{4,5},{0,4},{3,2},{7,3},{6,7},{2,6},{9,8},{13,9},{12,1... | collective-permute-start | bytes 2064392 | tf_op jit(solution)/shard_map/ppermute | solution.py:285
  132.5 41.3 %collective-permute-start.26 = (bf16[4,64,2688]{2,1,0:T(8,128)(2,1)S(1)}, bf16[4,64,2688]{2,1,0:T(8,128)(2,1)}, u32[]{:S(2)}, u32[]{:S(2)}) collective-permute-start(bf16[4,64,2688]{2,1,0:T(8,128)(2,1)S(1)} %collective-permute-done.21.refs_1_.refs_15_), channel_id=1, source_target_pairs={{0,2},{2,0},{1,3},{3,1},{4,6},{6,4},{5,7},{7,5},{8,10},{10,8},{9,1... | collective-permute-start | bytes 4128776 | tf_op jit(solution)/shard_map/ppermute | solution.py:285
  132.5 41.7 %collective-permute-start.27 = (bf16[4,64,2688]{2,1,0:T(8,128)(2,1)S(1)}, bf16[4,64,2688]{2,1,0:T(8,128)(2,1)}, u32[]{:S(2)}, u32[]{:S(2)}) collective-permute-start(bf16[4,64,2688]{2,1,0:T(8,128)(2,1)S(1)} %collective-permute-done.22.refs_2_.refs_16_), channel_id=1, source_target_pairs={{0,2},{2,0},{1,3},{3,1},{4,6},{6,4},{5,7},{7,5},{8,10},{10,8},{9,1... | collective-permute-start | bytes 4128776 | tf_op jit(solution)/shard_map/ppermute | solution.py:285
  146.9 26.3 %collective-permute-start.39 = (bf16[2,2,64,2048]{3,2,1,0:T(8,128)(2,1)}, bf16[2,2,64,2048]{3,2,1,0:T(8,128)(2,1)}, u32[]{:S(2)}, u32[]{:S(2)}) collective-permute-start(bf16[2,2,64,2048]{3,2,1,0:T(8,128)(2,1)} %collective-permute-done.38.refs_5_), channel_id=1, source_target_pairs={{8,0},{9,1},{10,2},{11,3},{12,4},{13,5},{14,6},{15,7}} | collective-permute-start | bytes 3145736 | tf_op jit(solution)/shard_map/ppermute | solution.py:285
  148.4 24.8 %collective-permute-start.28 = (bf16[2,64,2688]{2,1,0:T(8,128)(2,1)}, bf16[2,64,2688]{2,1,0:T(8,128)(2,1)}, u32[]{:S(2)}, u32[]{:S(2)}) collective-permute-start(bf16[2,64,2688]{2,1,0:T(8,128)(2,1)} %collective-permute-done.23.refs_3_.refs_17_), channel_id=1, source_target_pairs={{0,2},{2,0},{1,3},{3,1},{4,6},{6,4},{5,7},{7,5},{8,10},{10,8},{9,1... | collective-permute-start | bytes 2064392 | tf_op jit(solution)/shard_map/ppermute | solution.py:285
  148.4 25.3 %collective-permute-start.29 = (bf16[2,64,2688]{2,1,0:T(8,128)(2,1)}, bf16[2,64,2688]{2,1,0:T(8,128)(2,1)}, u32[]{:S(2)}, u32[]{:S(2)}) collective-permute-start(bf16[2,64,2688]{2,1,0:T(8,128)(2,1)} %collective-permute-done.24.refs_4_.refs_18_), channel_id=1, source_target_pairs={{0,2},{2,0},{1,3},{3,1},{4,6},{6,4},{5,7},{7,5},{8,10},{10,8},{9,1... | collective-permute-start | bytes 2064392 | tf_op jit(solution)/shard_map/ppermute | solution.py:285
  173.2 55.8 %collective-permute-start.44 = (bf16[2,2,64,2048]{3,2,1,0:T(8,128)(2,1)}, bf16[2,2,64,2048]{3,2,1,0:T(8,128)(2,1)}, u32[]{:S(2)}, u32[]{:S(2)}) collective-permute-start(bf16[2,2,64,2048]{3,2,1,0:T(8,128)(2,1)} %collective-permute-done.37.refs_4_), channel_id=1, source_target_pairs={{0,2},{2,0},{1,3},{3,1},{4,6},{6,4},{5,7},{7,5},{8,10},{10,8},{9,1... | collective-permute-start | bytes 3145736 | tf_op jit(solution)/shard_map/ppermute | solution.py:285
  173.2 55.8 %collective-permute-start.42 = (bf16[2,2,64,2048]{3,2,1,0:T(8,128)(2,1)S(1)}, bf16[2,2,64,2048]{3,2,1,0:T(8,128)(2,1)}, u32[]{:S(2)}, u32[]{:S(2)}) collective-permute-start(bf16[2,2,64,2048]{3,2,1,0:T(8,128)(2,1)S(1)} %copy-done.52), channel_id=1, source_target_pairs={{0,2},{2,0},{1,3},{3,1},{4,6},{6,4},{5,7},{7,5},{8,10},{10,8},{9,1... | collective-permute-start | bytes 3145736 | tf_op jit(solution)/shard_map/ppermute | solution.py:285
  173.7 55.3 %collective-permute-start.45 = (bf16[2,2,64,2048]{3,2,1,0:T(8,128)(2,1)}, bf16[2,2,64,2048]{3,2,1,0:T(8,128)(2,1)}, u32[]{:S(2)}, u32[]{:S(2)}) collective-permute-start(bf16[2,2,64,2048]{3,2,1,0:T(8,128)(2,1)} %collective-permute-done.38.refs_5_), channel_id=1, source_target_pairs={{0,2},{2,0},{1,3},{3,1},{4,6},{6,4},{5,7},{7,5},{8,10},{10,8},{9,1... | collective-permute-start | bytes 3145736 | tf_op jit(solution)/shard_map/ppermute | solution.py:285
  173.8 55.2 %collective-permute-start.43 = (bf16[2,2,64,2048]{3,2,1,0:T(8,128)(2,1)S(1)}, bf16[2,2,64,2048]{3,2,1,0:T(8,128)(2,1)S(1)}, u32[]{:S(2)}, u32[]{:S(2)}) collective-permute-start(bf16[2,2,64,2048]{3,2,1,0:T(8,128)(2,1)S(1)} %copy-done.55), channel_id=1, source_target_pairs={{0,2},{2,0},{1,3},{3,1},{4,6},{6,4},{5,7},{7,5},{8,10},{10,8},{9,1... | collective-permute-start | bytes 3145736 | tf_op jit(solution)/shard_map/ppermute | solution.py:285
  174.2 54.8 %collective-permute-start.46 = (bf16[2,2,64,2048]{3,2,1,0:T(8,128)(2,1)}, bf16[2,2,64,2048]{3,2,1,0:T(8,128)(2,1)S(1)}, u32[]{:S(2)}, u32[]{:S(2)}) collective-permute-start(bf16[2,2,64,2048]{3,2,1,0:T(8,128)(2,1)} %collective-permute-done.39.refs_6_), channel_id=1, source_target_pairs={{0,2},{2,0},{1,3},{3,1},{4,6},{6,4},{5,7},{7,5},{8,10},{10,8},{9,1... | collective-permute-start | bytes 3145736 | tf_op jit(solution)/shard_map/ppermute | solution.py:285
  324.2 18.7 %collective-permute-start.49 = (bf16[4,2,2,64,1536]{4,3,2,1,0:T(8,128)(2,1)}, bf16[4,2,2,64,1536]{4,3,2,1,0:T(8,128)(2,1)}, u32[]{:S(2)}, u32[]{:S(2)}) collective-permute-start(bf16[4,2,2,64,1536]{4,3,2,1,0:T(8,128)(2,1)} %get-tuple-element.66), channel_id=1, source_target_pairs={{0,2},{2,0},{1,3},{3,1},{4,6},{6,4},{5,7},{7,5},{8,10},{10,8},{9,1... | collective-permute-start | bytes 9437192 | tf_op jit(solution)/shard_map/ppermute | solution.py:285
  337.0 40.0 %collective-permute-start.71 = (bf16[4,2,2,64,2048]{4,3,2,1,0:T(8,128)(2,1)}, bf16[4,2,2,64,2048]{4,3,2,1,0:T(8,128)(2,1)}, u32[]{:S(2)}, u32[]{:S(2)}) collective-permute-start(bf16[4,2,2,64,2048]{4,3,2,1,0:T(8,128)(2,1)} %get-tuple-element.70), channel_id=1, source_target_pairs={{0,2},{2,0},{1,3},{3,1},{4,6},{6,4},{5,7},{7,5},{8,10},{10,8},{9,1... | collective-permute-start | bytes 12582920 | tf_op jit(solution)/shard_map/ppermute | solution.py:285
  342.5 68.2 %collective-permute-start.60 = (bf16[4,2,2,64,2688]{4,3,0,2,1:T(8,128)(2,1)}, bf16[4,2,2,64,2688]{4,3,0,2,1:T(8,128)(2,1)}, u32[]{:S(2)}, u32[]{:S(2)}) collective-permute-start(bf16[4,2,2,64,2688]{4,3,0,2,1:T(8,128)(2,1)} %copy.125), channel_id=1, source_target_pairs={{0,2},{2,0},{1,3},{3,1},{4,6},{6,4},{5,7},{7,5},{8,10},{10,8},{9,1... | collective-permute-start | bytes 16515080 | tf_op jit(solution)/shard_map/ppermute | solution.py:285
  346.1 12.2 %collective-permute-start.52 = (bf16[2,64,1536]{2,1,0:T(8,128)(2,1)S(1)}, bf16[2,64,1536]{2,1,0:T(8,128)(2,1)S(1)}, u32[]{:S(2)}, u32[]{:S(2)}) collective-permute-start(bf16[2,64,1536]{2,1,0:T(8,128)(2,1)S(1)} %get-tuple-element.213), channel_id=1, source_target_pairs={{1,0},{5,1},{4,5},{0,4},{3,2},{7,3},{6,7},{2,6},{9,8},{13,9},{12,1... | collective-permute-start | bytes 1179656 | tf_op jit(solution)/shard_map/ppermute | solution.py:285
  357.1 26.2 %collective-permute-start.51 = (bf16[4,64,1536]{2,1,0:T(8,128)(2,1)}, bf16[4,64,1536]{2,1,0:T(8,128)(2,1)}, u32[]{:S(2)}, u32[]{:S(2)}) collective-permute-start(bf16[4,64,1536]{2,1,0:T(8,128)(2,1)} %pad_maximum_fusion.2), channel_id=1, source_target_pairs={{0,1},{1,5},{5,4},{4,0},{2,3},{3,7},{7,6},{6,2},{8,9},{9,13},{13,1... | collective-permute-start | bytes 2359304 | tf_op jit(solution)/shard_map/ppermute | solution.py:285
  359.3 24.0 %collective-permute-start.53 = (bf16[4,64,1536]{2,1,0:T(8,128)(2,1)}, bf16[4,64,1536]{2,1,0:T(8,128)(2,1)}, u32[]{:S(2)}, u32[]{:S(2)}) collective-permute-start(bf16[4,64,1536]{2,1,0:T(8,128)(2,1)} %pad_maximum_fusion.3), channel_id=1, source_target_pairs={{1,0},{5,1},{4,5},{0,4},{3,2},{7,3},{6,7},{2,6},{9,8},{13,9},{12,1... | collective-permute-start | bytes 2359304 | tf_op jit(solution)/shard_map/ppermute | solution.py:285
  379.4 25.0 %collective-permute-start.72 = (bf16[2,2,64,2048]{3,2,1,0:T(8,128)(2,1)S(1)}, bf16[2,2,64,2048]{3,2,1,0:T(8,128)(2,1)S(1)}, u32[]{:S(2)}, u32[]{:S(2)}) collective-permute-start(bf16[2,2,64,2048]{3,2,1,0:T(8,128)(2,1)S(1)} %get-tuple-element.190), channel_id=1, source_target_pairs={{0,8},{1,9},{2,10},{3,11},{4,12},{5,13},{6,14},{7,15}} | collective-permute-start | bytes 3145736 | tf_op jit(solution)/shard_map/ppermute | solution.py:285
  382.3 68.2 %collective-permute-start.75 = (bf16[2,2,64,2048]{3,2,1,0:T(8,128)(2,1)S(1)}, bf16[2,2,64,2048]{3,2,1,0:T(8,128)(2,1)S(1)}, u32[]{:S(2)}, u32[]{:S(2)}) collective-permute-start(bf16[2,2,64,2048]{3,2,1,0:T(8,128)(2,1)S(1)} %get-tuple-element.191), channel_id=1, source_target_pairs={{24,16},{25,17},{26,18},{27,19},{28,20},{29,21},{30,22},{31,23}} | collective-permute-start | bytes 3145736 | tf_op jit(solution)/shard_map/ppermute | solution.py:285
  385.8 56.8 %collective-permute-start.54 = (bf16[64,1536]{1,0:T(8,128)(2,1)S(1)}, bf16[64,1536]{1,0:T(8,128)(2,1)S(1)}, u32[]{:S(2)}, u32[]{:S(2)}) collective-permute-start(bf16[64,1536]{1,0:T(8,128)(2,1)S(1)} %get-tuple-element.204), channel_id=1, source_target_pairs={{0,8},{1,9},{2,10},{3,11},{4,12},{5,13},{6,14},{7,15}} | collective-permute-start | bytes 589832 | tf_op jit(solution)/shard_map/ppermute | solution.py:285
  387.1 57.4 %collective-permute-start.57 = (bf16[64,1536]{1,0:T(8,128)(2,1)S(1)}, bf16[64,1536]{1,0:T(8,128)(2,1)S(1)}, u32[]{:S(2)}, u32[]{:S(2)}) collective-permute-start(bf16[64,1536]{1,0:T(8,128)(2,1)S(1)} %get-tuple-element.205), channel_id=1, source_target_pairs={{24,16},{25,17},{26,18},{27,19},{28,20},{29,21},{30,22},{31,23}} | collective-permute-start | bytes 589832 | tf_op jit(solution)/shard_map/ppermute | solution.py:285
  406.3 44.9 %collective-permute-start.73 = (bf16[2,2,64,2048]{3,2,1,0:T(8,128)(2,1)S(1)}, bf16[2,2,64,2048]{3,2,1,0:T(8,128)(2,1)S(1)}, u32[]{:S(2)}, u32[]{:S(2)}) collective-permute-start(bf16[2,2,64,2048]{3,2,1,0:T(8,128)(2,1)S(1)} %fusion.4), channel_id=1, source_target_pairs={{0,8},{8,16},{1,9},{9,17},{2,10},{10,18},{3,11},{11,19},{4,12},{12... | collective-permute-start | bytes 3145736 | tf_op jit(solution)/shard_map/ppermute | solution.py:285
  414.3 13.0 %collective-permute-start.61 = (bf16[2,64,2688]{2,1,0:T(8,128)(2,1)S(1)}, bf16[2,64,2688]{2,1,0:T(8,128)(2,1)S(1)}, u32[]{:S(2)}, u32[]{:S(2)}) collective-permute-start(bf16[2,64,2688]{2,1,0:T(8,128)(2,1)S(1)} %get-tuple-element.206), channel_id=1, source_target_pairs={{0,1},{1,5},{5,4},{4,0},{2,3},{3,7},{7,6},{6,2},{8,9},{9,13},{13,1... | collective-permute-start | bytes 2064392 | tf_op jit(solution)/shard_map/ppermute | solution.py:285
  427.3 14.5 %collective-permute-start.63 = (bf16[2,64,2688]{2,1,0:T(8,128)(2,1)S(1)}, bf16[2,64,2688]{2,1,0:T(8,128)(2,1)S(1)}, u32[]{:S(2)}, u32[]{:S(2)}) collective-permute-start(bf16[2,64,2688]{2,1,0:T(8,128)(2,1)S(1)} %get-tuple-element.207), channel_id=1, source_target_pairs={{1,0},{5,1},{4,5},{0,4},{3,2},{7,3},{6,7},{2,6},{9,8},{13,9},{12,1... | collective-permute-start | bytes 2064392 | tf_op jit(solution)/shard_map/ppermute | solution.py:285
  441.8 31.1 %collective-permute-start.62 = (bf16[4,64,2688]{2,1,0:T(8,128)(2,1)S(1)}, bf16[4,64,2688]{2,1,0:T(8,128)(2,1)S(1)}, u32[]{:S(2)}, u32[]{:S(2)}) collective-permute-start(bf16[4,64,2688]{2,1,0:T(8,128)(2,1)S(1)} %pad_maximum_fusion), channel_id=1, source_target_pairs={{0,1},{1,5},{5,4},{4,0},{2,3},{3,7},{7,6},{6,2},{8,9},{9,13},{13,1... | collective-permute-start | bytes 4128776 | tf_op jit(solution)/shard_map/ppermute | solution.py:285
  442.6 33.4 %collective-permute-start.64 = (bf16[4,64,2688]{2,1,0:T(8,128)(2,1)S(1)}, bf16[4,64,2688]{2,1,0:T(8,128)(2,1)S(1)}, u32[]{:S(2)}, u32[]{:S(2)}) collective-permute-start(bf16[4,64,2688]{2,1,0:T(8,128)(2,1)S(1)} %pad_maximum_fusion.1), channel_id=1, source_target_pairs={{1,0},{5,1},{4,5},{0,4},{3,2},{7,3},{6,7},{2,6},{9,8},{13,9},{12,1... | collective-permute-start | bytes 4128776 | tf_op jit(solution)/shard_map/ppermute | solution.py:285
  449.9 112.2 %collective-permute-start.48 = (bf16[532,1024]{1,0:T(8,128)(2,1)}, bf16[532,1024]{1,0:T(8,128)(2,1)}, u32[]{:S(2)}, u32[]{:S(2)}) collective-permute-start(bf16[532,1024]{1,0:T(8,128)(2,1)} %get-tuple-element.209), channel_id=1, source_target_pairs={{0,1},{1,0},{2,3},{3,2},{4,5},{5,4},{6,7},{7,6},{8,9},{9,8},{10,11... | collective-permute-start | bytes 3268616 | tf_op jit(solution)/shard_map/ppermute | solution.py:285
  450.5 47.0 %collective-permute-start.58 = (bf16[64,1536]{1,0:T(8,128)(2,1)S(1)}, bf16[64,1536]{1,0:T(8,128)(2,1)S(1)}, u32[]{:S(2)}, u32[]{:S(2)}) collective-permute-start(bf16[64,1536]{1,0:T(8,128)(2,1)S(1)} %get-tuple-element.203), channel_id=1, source_target_pairs={{24,16},{16,8},{25,17},{17,9},{26,18},{18,10},{27,19},{19,11},{28,... | collective-permute-start | bytes 589832 | tf_op jit(solution)/shard_map/ppermute | solution.py:285
  454.2 26.2 %collective-permute-start.76 = (bf16[2,2,64,2048]{3,2,1,0:T(8,128)(2,1)S(1)}, bf16[2,2,64,2048]{3,2,1,0:T(8,128)(2,1)S(1)}, u32[]{:S(2)}, u32[]{:S(2)}) collective-permute-start(bf16[2,2,64,2048]{3,2,1,0:T(8,128)(2,1)S(1)} %get-tuple-element.189), channel_id=1, source_target_pairs={{24,16},{16,8},{25,17},{17,9},{26,18},{18,10},{27,19},{19,11},{28,... | collective-permute-start | bytes 3145736 | tf_op jit(solution)/shard_map/ppermute | solution.py:285
  472.9 35.2 %collective-permute-start.74 = (bf16[2,2,64,2048]{3,2,1,0:T(8,128)(2,1)S(1)}, bf16[2,2,64,2048]{3,2,1,0:T(8,128)(2,1)S(1)}, u32[]{:S(2)}, u32[]{:S(2)}) collective-permute-start(bf16[2,2,64,2048]{3,2,1,0:T(8,128)(2,1)S(1)} %get-tuple-element.188), channel_id=1, source_target_pairs={{0,8},{8,16},{16,24},{1,9},{9,17},{17,25},{2,10},{10,18},{18,26},{... | collective-permute-start | bytes 3145736 | tf_op jit(solution)/shard_map/ppermute | solution.py:285
  478.2 18.6 %collective-permute-start.65 = (bf16[64,2688]{1,0:T(8,128)(2,1)S(1)}, bf16[64,2688]{1,0:T(8,128)(2,1)S(1)}, u32[]{:S(2)}, u32[]{:S(2)}) collective-permute-start(bf16[64,2688]{1,0:T(8,128)(2,1)S(1)} %get-tuple-element.196), channel_id=1, source_target_pairs={{0,8},{1,9},{2,10},{3,11},{4,12},{5,13},{6,14},{7,15}} | collective-permute-start | bytes 1032200 | tf_op jit(solution)/shard_map/ppermute | solution.py:285
  482.1 26.0 %collective-permute-start.77 = (bf16[2,2,64,2048]{3,2,1,0:T(8,128)(2,1)S(1)}, bf16[2,2,64,2048]{3,2,1,0:T(8,128)(2,1)S(1)}, u32[]{:S(2)}, u32[]{:S(2)}) collective-permute-start(bf16[2,2,64,2048]{3,2,1,0:T(8,128)(2,1)S(1)} %fusion.3), channel_id=1, source_target_pairs={{24,16},{16,8},{8,0},{25,17},{17,9},{9,1},{26,18},{18,10},{10,2},{... | collective-permute-start | bytes 3145736 | tf_op jit(solution)/shard_map/ppermute | solution.py:285
  502.0 18.1 %collective-permute-start.56 = (bf16[64,1536]{1,0:T(8,128)(2,1)S(1)}, bf16[64,1536]{1,0:T(8,128)(2,1)S(1)}, u32[]{:S(2)}, u32[]{:S(2)}) collective-permute-start(bf16[64,1536]{1,0:T(8,128)(2,1)S(1)} %get-tuple-element.202), channel_id=1, source_target_pairs={{0,8},{8,16},{16,24},{1,9},{9,17},{17,25},{2,10},{10,18},{18,26},{... | collective-permute-start | bytes 589832 | tf_op jit(solution)/shard_map/ppermute | solution.py:285
  506.7 29.6 %collective-permute-start.59 = (bf16[64,1536]{1,0:T(8,128)(2,1)S(1)}, bf16[64,1536]{1,0:T(8,128)(2,1)S(1)}, u32[]{:S(2)}, u32[]{:S(2)}) collective-permute-start(bf16[64,1536]{1,0:T(8,128)(2,1)S(1)} %fusion.36), channel_id=1, source_target_pairs={{24,16},{16,8},{8,0},{25,17},{17,9},{9,1},{26,18},{18,10},{10,2},{... | collective-permute-start | bytes 589832 | tf_op jit(solution)/shard_map/ppermute | solution.py:285
  517.8 20.7 %collective-permute-start.79 = (bf16[64,2048]{1,0:T(8,128)(2,1)S(1)}, bf16[64,2048]{1,0:T(8,128)(2,1)S(1)}, u32[]{:S(2)}, u32[]{:S(2)}) collective-permute-start(bf16[64,2048]{1,0:T(8,128)(2,1)S(1)} %pad_maximum_fusion.4), channel_id=1, source_target_pairs={{0,1},{1,5},{5,4},{4,0},{2,3},{3,7},{7,6},{6,2},{8,9},{9,13},{13,1... | collective-permute-start | bytes 786440 | tf_op jit(solution)/shard_map/ppermute | solution.py:285
  519.2 20.5 %collective-permute-start.81 = (bf16[64,2048]{1,0:T(8,128)(2,1)S(1)}, bf16[64,2048]{1,0:T(8,128)(2,1)S(1)}, u32[]{:S(2)}, u32[]{:S(2)}) collective-permute-start(bf16[64,2048]{1,0:T(8,128)(2,1)S(1)} %pad_maximum_fusion.5), channel_id=1, source_target_pairs={{1,0},{5,1},{4,5},{0,4},{3,2},{7,3},{6,7},{2,6},{9,8},{13,9},{12,1... | collective-permute-start | bytes 786440 | tf_op jit(solution)/shard_map/ppermute | solution.py:285
  520.1 21.2 %collective-permute-start.67 = (bf16[64,2688]{1,0:T(8,128)(2,1)S(1)}, bf16[64,2688]{1,0:T(8,128)(2,1)S(1)}, u32[]{:S(2)}, u32[]{:S(2)}) collective-permute-start(bf16[64,2688]{1,0:T(8,128)(2,1)S(1)} %get-tuple-element.194), channel_id=1, source_target_pairs={{0,8},{8,16},{16,24},{1,9},{9,17},{17,25},{2,10},{10,18},{18,26},{... | collective-permute-start | bytes 1032200 | tf_op jit(solution)/shard_map/ppermute | solution.py:285
  538.5 20.2 %collective-permute-start.47 = (bf16[532,1024]{1,0:T(8,128)(2,1)}, bf16[532,1024]{1,0:T(8,128)(2,1)}, u32[]{:S(2)}, u32[]{:S(2)}) collective-permute-start(bf16[532,1024]{1,0:T(8,128)(2,1)} %get-tuple-element.211), channel_id=1, source_target_pairs={{0,1},{1,0},{2,3},{3,2},{4,5},{5,4},{6,7},{7,6},{8,9},{9,8},{10,11... | collective-permute-start | bytes 3268616 | tf_op jit(solution)/shard_map/ppermute | solution.py:285
  (129 other events, 1455.7 us)
where the time goes:
time: 595 us; the launch traced here: 585 us
  waiting for transfers between devices  197 us (33%)
  Pallas kernels  158 us (27%)
  starting transfers between devices  114 us (19%)
  local copies, waits for them, and re-layouts  61.2 us (10%)
  other arithmetic  44.8 us (8%)
  between operations  9.53 us (2%)
    ppermute x88, waiting for transfers between devices, send(): return lax.ppermute(block, axes, list(pairs))  197 us
    ppermute x88, starting transfers between devices, send(): return lax.ppermute(block, axes, list(pairs))  114 us
    unnamed x214, local copies, waits for them, and re-layouts  40.9 us
    pallas_call x1, Pallas kernels, inner_back(): pl.pallas_call(functools.partial(inner_kernel, chunks // 2, len(downs)),...  32 us
    pallas_call x1, Pallas kernels, attention_back(): pl.pallas_call(attend_back_kernel, grid=(pairs,), in_specs=pair_specs(tot...  25.4 us
    pallas_call x1, Pallas kernels, up(): pl.pallas_call(functools.partial(up_kernel, per_side), grid=(2 * per_side...  22.2 us
    pallas_call x1, Pallas kernels, down(): pl.pallas_call(functools.partial(down_kernel, chunks // 2, len(pieces)),...  18.8 us
    pallas_call x2, Pallas kernels, weight_grad(): pl.pallas_call(weight_grad_kernel, grid=(chunks,), in_specs=[full(a.shape...  18.8 us
  transfers between devices with their start and end apart: 88, of which 31 were waited for; matrix products, arithmetic and copies ran while one was open for 11% of the time, Pallas kernels for 12%

commit v1 on v0

--- a/solution.py
+++ b/solution.py
@@ -296,41 +296,17 @@
     return x, jnp.where(x == 0, place, 3 - place)
 
 
-def ring_gather(block):
-    left = send(block, ("x", "y"), RING)
-    right = send(block, ("x", "y"), RING_BACK)
-    half = block.shape[0] // 2
-    far_one = send(left[:half], ("x", "y"), RING)
-    far_two = send(right[half:], ("x", "y"), RING_BACK)
-    return block, left, right, far_one, far_two
-
-
-def ring_scatter(take, half_of):
-    place = ring_place()
-    far = half_of(take(*place_xy(place + 2)))
-    from_left = send(far[0].astype(jnp.bfloat16), ("x", "y"), RING)
-    from_right = send(far[1].astype(jnp.bfloat16), ("x", "y"), RING_BACK)
-    right = half_of(take(*place_xy(place + 1)))
-    left = half_of(take(*place_xy(place - 1)))
-    to_right = jnp.concatenate([right[0] + from_left.astype(jnp.float32), right[1]]).astype(jnp.bfloat16)
-    to_left = jnp.concatenate([left[0], left[1] + from_right.astype(jnp.float32)]).astype(jnp.bfloat16)
-    from_left = send(to_right, ("x", "y"), RING)
-    from_right = send(to_left, ("x", "y"), RING_BACK)
-    return take(*place_xy(place)) + from_left.astype(jnp.float32) + from_right.astype(jnp.float32)
-
-
-def line_scatter(take):
-    count, z = lax.axis_size("z"), lax.axis_index("z")
-    up = down = None
-    for step in range(1, count):
-        pairs = [(i, i + 1) for i in range(step)]
-        above = take(jnp.minimum(z + count - step, count - 1))
-        below = take(jnp.maximum(z - count + step, 0))
-        if up is not None:
-            above, below = above + up.astype(jnp.float32), below + down.astype(jnp.float32)
-        up = send(above.astype(jnp.bfloat16), "z", pairs)
-        down = send(below.astype(jnp.bfloat16), "z", [(count - 1 - a, count - 1 - b) for a, b in pairs])
-    return take(z) + up.astype(jnp.float32) + down.astype(jnp.float32)
+def ring_near(block):
+    return send(block, ("x", "y"), RING), send(block, ("x", "y"), RING_BACK)
+
+
+def ring_far(left, right):
+    half = left.shape[0] // 2
+    return send(left[:half], ("x", "y"), RING), send(right[half:], ("x", "y"), RING_BACK)
+
+
+def after(value, *others):
+    return lax.optimization_barrier((value,) + others)[0]
 
 
 STEP_WIDTH = 512
@@ -346,6 +322,10 @@
     return pltpu.CompilerParams(vmem_limit_bytes=mib << 20)
 
 
+def cost(flops, moved):
+    return pl.CostEstimate(flops=int(flops), bytes_accessed=int(moved), transcendentals=0)
+
+
 def shaped(shape, dtype):
     return jax.ShapeDtypeStruct(shape, dtype)
 
@@ -359,64 +339,33 @@
 
 
 def join_column_kernel(count, *refs):
-    own, ups, downs = refs[0], refs[1:count], refs[count : 2 * count - 1]
     out, sem = refs[-2:]
     z = lax.axis_index("z")
-    moves = [(None, own, z)]
-    for k in range(1, count):
-        moves += [(z >= k, ups[k - 1], z - k), (z + k < count, downs[k - 1], z + k)]
-    for end in (False, True):
-        for i, (here, ref, at) in enumerate(moves):
-            copy = pltpu.make_async_copy(ref, out.at[at], sem.at[i])
-            act = copy.wait if end else copy.start
-            act() if here is None else pl.when(here)(act)
-
-
-def line_pieces(block):
-    count = lax.axis_size("z")
-    ups, downs = [block], [block]
-    for step in range(1, count):
-        pairs = [(i, i + 1) for i in range(step - 1, count - 1)]
-        ups.append(send(ups[-1], "z", pairs))
-        downs.append(send(downs[-1], "z", [(count - 1 - a, count - 1 - b) for a, b in pairs]))
-    return [block] + ups[1:] + downs[1:]
-
-
-def join_column(pieces):
-    count = (len(pieces) + 1) // 2
-    shape = (count,) + pieces[0].shape
-    return pl.pallas_call(
-        functools.partial(join_column_kernel, count),
-        in_specs=[ANYWHERE] * len(pieces),
-        out_specs=pl.BlockSpec(memory_space=pltpu.VMEM),
-        out_shape=shaped(shape, pieces[0].dtype),
-        scratch_shapes=[pltpu.SemaphoreType.DMA((len(pieces),))],
-        name="join_column",
-    )(*pieces)
-
-
-def join_square_kernel(own, left, right, far_one, far_two, out, sem):
-    place = ring_place()
-    half = far_one.shape[0]
-    copies = []
-    for i, (ref, shift) in enumerate(zip((own, left, right, far_one, far_two), RING_SHIFTS)):
-        x, y = place_xy(place + shift)
-        to = out.at[x, y] if i < 3 else out.at[x, y, pl.ds(half * (i - 3), half)]
-        copies.append(pltpu.make_async_copy(ref, to, sem.at[i]))
+    copies = [pltpu.make_async_copy(ref, out.at[z ^ k], sem.at[k]) for k, ref in enumerate(refs[:count])]
     for copy in copies:
         copy.start()
     for copy in copies:
         copy.wait()
 
 
-def join_square(pieces):
+def partners(k):
+    return tuple((i, i ^ k) for i in range(lax.axis_size("z")))
+
+
+def line_pieces(block):
+    return [block] + [send(block, "z", partners(k)) for k in range(1, lax.axis_size("z"))]
+
+
+def join_column(pieces):
+    count = len(pieces)
+    shape = (count,) + pieces[0].shape
     return pl.pallas_call(
-        join_square_kernel,
-        in_specs=[ANYWHERE] * 5,
+        functools.partial(join_column_kernel, count),
+        in_specs=[ANYWHERE] * count,
         out_specs=pl.BlockSpec(memory_space=pltpu.VMEM),
-        out_shape=shaped((2, 2) + pieces[0].shape, pieces[0].dtype),
-        scratch_shapes=[pltpu.SemaphoreType.DMA((5,))],
-        name="join_square",
+        out_shape=shaped(shape, pieces[0].dtype),
+        scratch_shapes=[pltpu.SemaphoreType.DMA((count,))],
+        name="join_column",
     )(*pieces)
 
 
@@ -424,15 +373,7 @@
     return list(pieces) + [send(p, "c", SWAP) for p in pieces]
 
 
-def weights_square_last(block):
-    return both_cores(ring_gather(join_column(line_pieces(block))))
-
-
-def weights_line_last(block):
-    return both_cores(line_pieces(join_square(ring_gather(block))))
-
-
-def load_square_last(pieces, w, sem, column, width, per_side):
+def load_weights(pieces, w, sem, column, width, per_side):
     place, core = ring_place(), lax.axis_index("c")
     rows = w.shape[4]
     for k in range(per_side):
@@ -448,26 +389,6 @@
                 ).start()
 
 
-def load_line_last(pieces, w, sem, width, per_side):
-    z, core = lax.axis_index("z"), lax.axis_index("c")
-    group_size = len(pieces) // 2
-    count = (group_size + 1) // 2
-    for k in range(per_side):
-        for group, core_at in ((pieces[:group_size], core), (pieces[group_size:], 1 - core)):
-            places = [(None, z)] + [(z >= s, z - s) for s in range(1, count)]
-            places += [(z + s < count, z + s) for s in range(1, count)]
-            for ref, (here, at) in zip(group, places):
-
-                def begin(ref=ref, at=at, core_at=core_at):
-                    for y in range(2):
-                        chunk = y * per_side + k
-                        pltpu.make_async_copy(
-                            ref.at[:, y, :, pl.ds(k * width, width)], w.at[chunk, at, :, core_at], sem.at[chunk]
-                        ).start()
-
-                begin() if here is None else pl.when(here)(begin)
-
-
 def ready(w, sem, chunk):
     pltpu.make_async_copy(w.at[chunk], w.at[chunk], sem.at[chunk]).wait()
 
@@ -492,7 +413,7 @@
 
     @pl.when(j == 0)
     def _():
-        load_square_last(pieces, w, sem, 0, o_ref.shape[2], per_side)
+        load_weights(pieces, w, sem, 0, o_ref.shape[2], per_side)
 
     chunk = alternate(per_side)(j)
     ready(w, sem, chunk)
@@ -511,6 +432,7 @@
         out_shape=shaped((2 * per_side, x.shape[0], width), LOW),
         scratch_shapes=chunk_buffer((count, rows), 2 * per_side, width),
         compiler_params=params(32),
+        cost_estimate=cost(6 * 1.1e9, 6 * 2e6),
         name="project",
     )(x, *pieces)
 
@@ -553,6 +475,7 @@
         out_specs=[pl.BlockSpec((total, 128), lambda g: (0, g))] * 2,
         out_shape=[shaped((total, width), LOW), shaped((total, width), F32)],
         compiler_params=params(48),
+        cost_estimate=cost(17 * 1.1e9, 17 * 2e6),
         name="attention",
     )(qkv, qkv, qkv, bias)
 
@@ -603,9 +526,9 @@
     @pl.when(j == 0)
     def _():
         first = 2 * per_side // 2 * width
-        load_square_last(pieces, nw, ns, first + width, 128, 1)
-        load_square_last(pieces, wo, os, first, width, 1)
-        load_square_last(pieces, wu, us, 0, width, per_side)
+        load_weights(pieces, nw, ns, first + width, 128, 1)
+        load_weights(pieces, wo, os, first, width, 1)
+        load_weights(pieces, wu, us, 0, width, per_side)
         ready(nw, ns, 0)
         ready(nw, ns, 1)
         cells = nw[0].reshape(-1, nw.shape[4], 128).astype(F32)
@@ -657,6 +580,7 @@
         + chunk_buffer((count, 16), 2, 128)
         + [pltpu.VMEM(x.shape, F32)],
         compiler_params=params(56),
+        cost_estimate=cost(22 * 1.1e9, 22 * 2e6),
         name="up",
     )(x, context, *pieces)
 
@@ -668,7 +592,7 @@
 
     @pl.when(j == 0)
     def _():
-        load_line_last(pieces, w, sem, g_ref.shape[2], per_side)
+        load_weights(pieces, w, sem, 0, g_ref.shape[2], per_side)
         acc[...] = jnp.zeros_like(acc)
 
     chunk = alternate(per_side)(j)
@@ -700,7 +624,7 @@
     chunks, total = active.shape[0], active.shape[1]
     at = alternate(chunks // 2)
     shape = normed.shape
-    count = (len(pieces) // 2 + 1) // 2
+    count = pieces[0].shape[0]
     return pl.pallas_call(
         functools.partial(down_kernel, chunks // 2, len(pieces)),
         grid=(chunks,),
@@ -710,6 +634,7 @@
         out_shape=[shaped(shape, LOW), shaped(shape, F32), shaped(shape, LOW), shaped(norms.shape, F32)],
         scratch_shapes=chunk_buffer((count, rows), chunks, width) + [pltpu.VMEM(shape, F32)],
         compiler_params=params(56),
+        cost_estimate=cost(17 * 1.1e9, 17 * 2e6),
         name="down",
     )(active, normed, norms, cot, *pieces)
 
@@ -748,6 +673,7 @@
         out_specs=out_specs,
         out_shape=out_shape,
         compiler_params=params(32),
+        cost_estimate=cost(9 * 1.1e9, 9 * 2e6),
         name=name,
     )(a, b)
 
@@ -760,8 +686,8 @@
 
     @pl.when(j == 0)
     def _():
-        load_line_last(downs, wd, ds, width, per_side)
-        load_square_last(ups, wu, us, 0, width, per_side)
+        load_weights(downs, wd, ds, 0, width, per_side)
+        load_weights(ups, wu, us, 0, width, per_side)
         acc[...] = r_ref[...]
 
     ready(wd, ds, j)
@@ -808,6 +734,7 @@
         out_shape=out_shape + [shaped(shape, F32), shaped(shape, LOW), shaped(norms.shape, F32)],
         scratch_shapes=chunk_buffer((count, rows), chunks, width) * 2 + [pltpu.VMEM(shape, F32)],
         compiler_params=params(58),
+        cost_estimate=cost(32 * 1.1e9, 32 * 2e6),
         name="inner_back",
     )(feed_grad, slope, hidden, second_grad, normed, inverse, norms, *downs, *ups)
 
@@ -818,7 +745,7 @@
     _, _, z, x, rows, _ = tiles.shape
     width = w.shape[5]
     core = lax.axis_index("c")
-    load_square_last(pieces, w, sem, column, width, 1)
+    load_weights(pieces, w, sem, column, width, 1)
     norm_grads = jnp.concatenate([one_ref[0:2], two_ref[0:2], one_ref[2:6]], axis=0)
     for y in range(2):
         grad = mm(a_ref[...], ctx_ref[:, y * width : (y + 1) * width], TN).astype(LOW).reshape(z, x, 2, rows, width)
@@ -859,6 +786,7 @@
         + [pltpu.VMEM((2, 2, count, 2, rows, width + 128), LOW), pltpu.SemaphoreType.DMA((2, 2))],
         input_output_aliases={4: 0, 5: 1},
         compiler_params=params(40),
+        cost_estimate=cost(4 * 1.1e9, 4 * 2e6),
         name="out_back",
     )(branch_grad, context, one, two, own, other, *pieces)
 
@@ -893,6 +821,7 @@
         out_specs=pl.BlockSpec((3, total, 128), lambda g: (0, 0, g)),
         out_shape=shaped((3, total, width), LOW),
         compiler_params=params(48),
+        cost_estimate=cost(25 * 1.1e9, 25 * 2e6),
         name="attention_back",
     )(qkv, qkv, qkv, bias, logs, grad)
 
@@ -903,7 +832,7 @@
 
     @pl.when(j == 0)
     def _():
-        load_square_last(pieces, w, sem, 0, g_ref.shape[2], per_side)
+        load_weights(pieces, w, sem, 0, g_ref.shape[2], per_side)
         acc[...] = r_ref[...]
 
     chunk = alternate(per_side)(j)
@@ -927,6 +856,7 @@
         out_shape=shaped(shape, LOW),
         scratch_shapes=chunk_buffer((count, rows), 2 * per_side, width) + [pltpu.VMEM(shape, F32)],
         compiler_params=params(40),
+        cost_estimate=cost(7 * 1.1e9, 7 * 2e6),
         name="input_back",
     )(grads, first_grad, *pieces)
 
@@ -935,19 +865,43 @@
     return lax.dynamic_index_in_dim(a, index, axis, keepdims=False)
 
 
-def sum_square_first(own, other):
-    def take(x, y):
-        return at(at(own, x, 1), y, 1).astype(F32) + at(at(other, x, 1), y, 1).astype(F32)
-
-    half = own.shape[0] // 2
-    column = ring_scatter(take, lambda a: (a[:half], a[half:]))
-    return line_scatter(lambda z: at(column, z, 0))
-
-
-def sum_line_first(own, other):
-    square = line_scatter(lambda z: at(own, z, 0).astype(F32) + at(other, z, 0).astype(F32))
-    half = own.shape[3] // 2
-    return ring_scatter(lambda x, y: at(at(square, x, 0), y, 0), lambda a: (a[:half], a[half:]))
+def chip_term(own, other, shift):
+    x, y = place_xy(ring_place() + shift)
+    return at(at(own, x, 1), y, 1).astype(F32) + at(at(other, x, 1), y, 1).astype(F32)
+
+
+def ring_pair(to_right, to_left):
+    return send(to_right, ("x", "y"), RING), send(to_left, ("x", "y"), RING_BACK)
+
+
+def far_terms(own, other):
+    far = chip_term(own, other, 2).astype(LOW)
+    half = far.shape[0] // 2
+    return far[:half], far[half:]
+
+
+def near_terms(own, other, from_left, from_right):
+    half = from_left.shape[0]
+    right, left = chip_term(own, other, 1), chip_term(own, other, -1)
+    to_right = jnp.concatenate([right[:half] + from_left.astype(F32), right[half:]]).astype(LOW)
+    to_left = jnp.concatenate([left[:half], left[half:] + from_right.astype(F32)]).astype(LOW)
+    return to_right, to_left
+
+
+def line_terms(own, other, from_left, from_right):
+    column = chip_term(own, other, 0) + from_left.astype(F32) + from_right.astype(F32)
+    z = lax.axis_index("z")
+    return [at(column, z, 0)] + [at(column, z ^ k, 0).astype(LOW) for k in range(1, column.shape[0])]
+
+
+def line_send(terms):
+    return [send(term, "z", partners(k + 1)) for k, term in enumerate(terms[1:])]
+
+
+def total_of(own, others):
+    for other in others:
+        own = own + other.astype(F32)
+    return own
 
 
 def sum_over_all(value):
@@ -1027,17 +981,34 @@
     cot = pad_rows(mine(cotangent), total)
     bias = mask_bias(mine(doc_ids), mine(reset_flags), mine(mem_live), total)
 
-    w_qkv = weights_square_last(qkv_block)
-    w_second = weights_square_last(second_block)
-    w_down = weights_line_last(down_block)
-
-    qkv = project(x, w_qkv, rows)
+    z_qkv = line_pieces(qkv_block)
+    z_second = line_pieces(after(second_block, *z_qkv))
+    column_qkv = join_column(z_qkv)
+    near_qkv = ring_near(column_qkv)
+    far_qkv = ring_far(*near_qkv)
+    w_qkv = both_cores((column_qkv,) + near_qkv + far_qkv)
+    z_down = line_pieces(after(down_block, *z_second))
+    column_second = after(join_column(z_second), *far_qkv)
+    near_second = ring_near(column_second)
+
+    qkv = project(after(x, column_second), w_qkv, rows)
     context, logs = attention(qkv, bias)
-    hidden, normed, inverse, norms, active, slope = up(x, context, w_second, rows, inner_part)
+
+    near_second = after(near_second, context)
+    far_second = ring_far(*near_second)
+    w_second = both_cores((column_second,) + near_second + far_second)
+    column_down = after(join_column([after(z_down[0], context)] + z_down[1:]), *far_second)
+    near_down = ring_near(column_down)
+
+    hidden, normed, inverse, norms, active, slope = up(x, after(context, column_down), w_second, rows, inner_part)
+
+    near_down = after(near_down, active)
+    far_down = ring_far(*near_down)
+    w_down = both_cores((column_down,) + near_down + far_down)
     result, second_grad, feed_grad, norm_two = down(active, normed, norms, cot, w_down, rows)
 
     chunks = active.shape[0]
-    own, other = weight_grad(
+    own_down, other = weight_grad(
         feed_grad,
         active,
         pl.BlockSpec((1, total, STEP_WIDTH), lambda j: (j, 0, 0)),
@@ -1046,18 +1017,43 @@
         rows,
         "down_grad",
     )
-    down_sum = sum_line_first(own, send(other, "c", SWAP))
+    other_down = send(other, "c", SWAP)
+    far = far_terms(own_down, other_down)
+    far_down = ring_pair(*far)
     columns = inner_part + part + 128
     own, other, first_grad, branch_grad, norm_one = inner_back(
-        feed_grad, slope, hidden, second_grad, normed, inverse, norms, w_down, w_second, rows, columns
-    )
-    own, other, context_grad = out_back(
-        branch_grad, context, norm_one, norm_two, own, other, w_second, rows, inner_part
-    )
-    second_sum = sum_square_first(own, send(other, "c", SWAP))
-    grads = attention_back(qkv, bias, logs, context_grad)
-    own, other = weight_grad(
-        x,
+        after(feed_grad, *far),
+        slope,
+        hidden,
+        second_grad,
+        normed,
+        inverse,
+        norms,
+        w_down,
+        w_second,
+        rows,
+        columns,
+    )
+    far_down = after(far_down, branch_grad)
+    near = near_terms(own_down, other_down, *far_down)
+    near_down = ring_pair(*near)
+    own_second, other, context_grad = out_back(
+        after(branch_grad, *near), context, norm_one, norm_two, own, other, w_second, rows, inner_part
+    )
+    other_second = send(other, "c", SWAP)
+    near_down = after(near_down, context_grad, other_second)
+    line_down = line_terms(own_down, other_down, *near_down)
+    others_down = line_send(line_down)
+    far = far_terms(own_second, after(other_second, *near_down))
+    far_second = ring_pair(*far)
+
+    grads = attention_back(qkv, bias, logs, after(context_grad, *far, *line_down))
+
+    far_second = after(far_second, grads)
+    near = near_terms(own_second, other_second, *far_second)
+    near_second = ring_pair(*near)
+    own_qkv, other = weight_grad(
+        after(x, *near),
         grads,
         pl.BlockSpec((1, total, STEP_WIDTH), lambda j: (j % 3, 0, j // 3)),
         6,
@@ -1065,8 +1061,20 @@
         rows,
         "qkv_grad",
     )
-    qkv_sum = sum_square_first(own, send(other, "c", SWAP))
-    own_grad = input_back(grads, first_grad, w_qkv, rows)
+    other_qkv = send(other, "c", SWAP)
+    own_grad = input_back(after(grads, own_qkv), first_grad, w_qkv, rows)
+    near_second = after(near_second, own_grad)
+    line_second = line_terms(own_second, other_second, *near_second)
+    others_second = line_send(line_second)
+    far = far_terms(own_qkv, after(other_qkv, *near_second))
+    far_qkv = ring_pair(*far)
+    near = near_terms(own_qkv, after(other_qkv, *line_second), *far_qkv)
+    near_qkv = ring_pair(*near)
+    line_qkv = line_terms(own_qkv, other_qkv, *near_qkv)
+    others_qkv = line_send(line_qkv)
+    down_sum = total_of(line_down[0], others_down)
+    second_sum = total_of(line_second[0], others_second)
+    qkv_sum = total_of(line_qkv[0], others_qkv)
 
     def both(own):
         own = own[:real]

time: 595 us -> 522 us (0.88)
  starting transfers between devices: 114 us -> 75.9 us
  local copies, waits for them, and re-layouts: 61.2 us -> 42.3 us
  waiting for transfers between devices: 197 us -> 188 us
    ppermute x88 -> x68, starting transfers between devices: 114 us -> 75.9 us  [send(): return lax.ppermute(block, axes, list(pairs))]
    unnamed x214 -> x178, local copies, waits for them, and re-layouts: 40.9 us -> 22.1 us
    ppermute x88 -> x68, waiting for transfers between devices: 197 us -> 188 us  [send(): return lax.ppermute(block, axes, list(pairs))]
    convert_element_type x10 -> x2, other arithmetic: 9.39 us -> 1.86 us  [far_terms(): far = chip_term(own, other, 2).astype(LOW)]
  transfers between devices with their start and end apart: 88 -> 68, of which waited for: 31 -> 28; matrix products, arithmetic and copies ran while one was open for 11% -> 10% of each run, Pallas kernels for 12% -> 24%
where the time goes in v1:
time: 522 us; the launch traced here: 513 us
  waiting for transfers between devices  188 us (36%)
  Pallas kernels  156 us (30%)
  starting transfers between devices  75.9 us (15%)
  other arithmetic  43.4 us (8%)
  local copies, waits for them, and re-layouts  42.3 us (8%)
  between operations  8.03 us (2%)
    ppermute x68, waiting for transfers between devices, send(): return lax.ppermute(block, axes, list(pairs))  188 us
    ppermute x68, starting transfers between devices, send(): return lax.ppermute(block, axes, list(pairs))  75.9 us
    pallas_call x1, Pallas kernels, inner_back(): pl.pallas_call(functools.partial(inner_kernel, chunks // 2, len(downs)),...  31.2 us
    pallas_call x1, Pallas kernels, attention_back(): pl.pallas_call(attend_back_kernel, grid=(pairs,), in_specs=pair_specs(tot...  25.2 us
    pallas_call x1, Pallas kernels, up(): pl.pallas_call(functools.partial(up_kernel, per_side), grid=(2 * per_side...  22.3 us
    unnamed x178, local copies, waits for them, and re-layouts  22.1 us
    pallas_call x1, Pallas kernels, down(): pl.pallas_call(functools.partial(down_kernel, chunks // 2, len(pieces)),...  18.8 us
    pallas_call x2, Pallas kernels, weight_grad(): pl.pallas_call(weight_grad_kernel, grid=(chunks,), in_specs=[full(a.shape...  17.6 us
  transfers between devices with their start and end apart: 68, of which 28 were waited for; matrix products, arithmetic and copies ran while one was open for 10% of the time, Pallas kernels for 24%

profile of v1, /device:TPU:0, one launch (start us, length us, event | category | flops | bytes accessed | tf_op | source)
XLA Modules:
  0.0 513.1 jit_solution(10396568183981465977)
XLA Ops:
  1.9 3.1 collective-permute-start
  4.9 2.6 collective-permute-start.1
  9.5 3.7 collective-permute-done.refs_1_
  13.3 8.8 %collective-permute-done.1.refs_2_ = bf16[64,1536]{1,0:T(8,128)(2,1)S(1)} collective-permute-done((bf16[64,1536]{1,0:T(8,128)(2,1)S(1)}, bf16[64,1536]{1,0:T(8,128)(2,1)S(1)}, u32[]{:S(2)}, u32[]{:S(2)}) %collective-permute-start.1) | collective-permute-done | bytes 196640 | tf_op jit(solution)/shard_map/ppermute | solution.py:285
  22.8 2.2 join_column.4.refs_0_
  25.0 1.6 collective-permute-start.6
  27.0 7.8 %constant_dynamic-slice_fusion = (bf16[1,532,1024]{2,0,1:T(2,128)(2,1)}, bf16[1,532,1024]{2,0,1:T(2,128)(2,1)S(1)}) fusion(bf16[2,532,1024]{2,0,1:T(2,128)(2,1)S(1)} %copy-done.41, s32[]{:T(128)S(6)} %select_n.201, bf16[2,532,1024]{2,0,1:T(2,128)(2,1)} %param.25), kind=kLoop, calls=%fused_computation.130 | loop fusion | bytes 4358148 | tf_op jit(solution)/shard_map/jit(dynamic_index_in_dim)/dynamic_slice | solution.py:973
  34.9 2.8 collective-permute-start.3
  41.5 1.6 collective-permute-start.7
  45.2 4.8 collective-permute-done.3.refs_1_
  50.0 14.5 %collective-permute-done.4.refs_2_ = bf16[64,2688]{1,0:T(8,128)(2,1)S(1)} collective-permute-done((bf16[64,2688]{1,0:T(8,128)(2,1)}, bf16[64,2688]{1,0:T(8,128)(2,1)S(1)}, u32[]{:S(2)}, u32[]{:S(2)}) %collective-permute-start.4) | collective-permute-done | bytes 344096 | tf_op jit(solution)/shard_map/ppermute | solution.py:285
  67.8 2.5 join_column.3.refs_0_.refs_10_
  70.4 4.4 collective-permute-start.15
  81.5 5.9 %project.1.q_ref.k_ref.v_ref = bf16[6,544,512]{2,1,0:T(8,128)(2,1)S(1)} custom-call(bf16[544,1024]{1,0:T(8,128)(2,1)S(1)} %pad.15.x_ref.a_ref, bf16[4,64,1536]{2,1,0:T(8,128)(2,1)S(1)} %copy-done.12, bf16[4,64,1536]{2,1,0:T(8,128)(2,1)S(1)} %copy-done.19, bf16[4,64,1536]{2,1,0:T(8,128)(2,1)} %collective-permute-done.8.refs_2_, ...), custom_call_target="tpu_custom_call" | custom-call | flops 6600000000 | bytes 12000000 | tf_op jit(solution)/shard_map/project/pallas_call | solution.py:427
  87.4 1.8 copy-done.26
  89.2 17.6 %attention.1 = (bf16[544,1024]{1,0:T(8,128)(2,1)S(1)}, f32[544,1024]{1,0:T(8,128)S(1)}) custom-call(bf16[6,544,512]{2,1,0:T(8,128)(2,1)} %copy-done.26, bf16[6,544,512]{2,1,0:T(8,128)(2,1)} %copy-done.26, bf16[6,544,512]{2,1,0:T(8,128)(2,1)} %copy-done.26, bf16[544,544]{1,0:T(8,128)(2,1)S(1)} %copy-done.14), custom_call_target="tpu_custom_call" | custom-call | flops 18699999232 | bytes 34000000 | tf_op jit(solution)/shard_map/attention/pallas_call | solution.py:471
  114.8 12.7 %collective-permute-done.20.refs_3_.refs_13_ = bf16[2,64,2688]{2,1,0:T(8,128)(2,1)S(1)} collective-permute-done((bf16[2,64,2688]{2,1,0:T(8,128)(2,1)S(1)}, bf16[2,64,2688]{2,1,0:T(8,128)(2,1)S(1)}, u32[]{:S(2)}, u32[]{:S(2)}) %collective-permute-start.20) | collective-permute-done | bytes 688160 | tf_op jit(solution)/shard_map/ppermute | solution.py:285
  127.5 2.6 collective-permute-done.21.refs_4_.refs_14_
  130.2 2.2 join_column.5.refs_0_
  132.4 1.7 collective-permute-start.27
  134.7 22.3 %up.1 = (bf16[544,1024]{1,0:T(8,128)(2,1)}, f32[544,1024]{1,0:T(8,128)}, f32[544,128]{1,0:T(8,128)}, f32[8,1024]{1,0:T(8,128)}, bf16[8,544,512]{2,1,0:T(8,128)(2,1)}, /*index=5*/bf16[8,544,512]{2,1,0:T(8,128)(2,1)}) custom-call(bf16[544,1024]{1,0:T(8,128)(2,1)} %copy-done.10, bf16[544,1024]{1,0:T(8,128)(2,1)} %copy-done.7, ...), custom_call_target="tpu_custom_call" | custom-call | flops 24199999488 | bytes 44000000 | tf_op jit(solution)/shard_map/up/pallas_call | solution.py:565
  161.4 1.6 collective-permute-start.30
  163.5 9.5 %collective-permute-done.29.refs_3_ = bf16[2,64,2048]{2,1,0:T(8,128)(2,1)S(1)} collective-permute-done((bf16[2,64,2048]{2,1,0:T(8,128)(2,1)S(1)}, bf16[2,64,2048]{2,1,0:T(8,128)(2,1)S(1)}, u32[]{:S(2)}, u32[]{:S(2)}) %collective-permute-start.29) | collective-permute-done | bytes 524320 | tf_op jit(solution)/shard_map/ppermute | solution.py:285
  177.9 18.8 %down.1 = (bf16[544,1024]{1,0:T(8,128)(2,1)}, f32[544,1024]{1,0:T(8,128)}, bf16[544,1024]{1,0:T(8,128)(2,1)}, f32[8,1024]{1,0:T(8,128)}) custom-call(bf16[8,544,512]{2,1,0:T(8,128)(2,1)} %get-tuple-element.84.g_ref.b_ref, f32[544,1024]{1,0:T(8,128)} %get-tuple-element.85.n_ref, f32[8,1024]{1,0:T(8,128)} %get-tuple-element.86.norms_ref, ...), custom_call_target="tpu_custom_call" | custom-call | flops 18699999232 | bytes 34000000 | tf_op jit(solution)/shard_map/down/pallas_call | solution.py:628
  198.0 9.8 %down_grad.1 = (bf16[4,2,2,64,2048]{4,3,2,1,0:T(8,128)(2,1)S(1)}, bf16[4,2,2,64,2048]{4,3,2,1,0:T(8,128)(2,1)S(1)}) custom-call(bf16[544,1024]{1,0:T(8,128)(2,1)S(1)} %copy-done.29, bf16[8,544,512]{2,1,0:T(8,128)(2,1)S(1)} %bitcast.179), custom_call_target="tpu_custom_call" | custom-call | flops 9900000256 | bytes 18000000 | tf_op jit(solution)/shard_map/down_grad/pallas_call | solution.py:669
  207.8 2.5 copy.139
  211.6 7.1 %collective-permute-done.37 = bf16[4,2,2,64,2048]{4,3,0,2,1:T(8,128)(2,1)} collective-permute-done((bf16[4,2,2,64,2048]{4,3,0,2,1:T(8,128)(2,1)}, bf16[4,2,2,64,2048]{4,3,0,2,1:T(8,128)(2,1)}, u32[]{:S(2)}, u32[]{:S(2)}) %collective-permute-start.37) | collective-permute-done | bytes 4194336 | tf_op jit(solution)/shard_map/ppermute | solution.py:285
  218.7 4.1 convert_add_fusion.2
  223.5 1.9 collective-permute-start.39
  225.4 31.2 %inner_back.1 = (bf16[4,2,2,64,2688]{4,3,2,1,0:T(8,128)(2,1)}, bf16[4,2,2,64,2688]{4,3,2,1,0:T(8,128)(2,1)}, f32[544,1024]{1,0:T(8,128)}, bf16[544,1024]{1,0:T(8,128)(2,1)}, f32[8,1024]{1,0:T(8,128)}) custom-call(bf16[544,1024]{1,0:T(8,128)(2,1)} %get-tuple-element.94.a_ref.f_ref, bf16[8,544,512]{2,1,0:T(8,128)(2,1)} %get-tuple-element.95.d_ref, ...), custom_call_target="tpu_custom_call" | custom-call | flops 35200000000 | bytes 64000000 | tf_op jit(solution)/shard_map/inner_back/pallas_call | solution.py:727
  260.6 3.7 out_back.1
  266.5 23.6 %collective-permute-done.42 = bf16[4,64,2048]{2,1,0:T(8,128)(2,1)} collective-permute-done((bf16[4,64,2048]{2,1,0:T(8,128)(2,1)S(1)}, bf16[4,64,2048]{2,1,0:T(8,128)(2,1)}, u32[]{:S(2)}, u32[]{:S(2)}) %collective-permute-start.42) | collective-permute-done | bytes 1048608 | tf_op jit(solution)/shard_map/ppermute | solution.py:285
  291.3 3.0 fusion.2
  295.1 2.3 collective-permute-start.60
  298.9 1.7 add_convert_fusion
  302.7 2.4 convert_add_fusion
  306.6 9.9 %collective-permute-done.60 = bf16[64,2048]{1,0:T(8,128)(2,1)S(1)} collective-permute-done((bf16[64,2048]{1,0:T(8,128)(2,1)S(1)}, bf16[64,2048]{1,0:T(8,128)(2,1)S(1)}, u32[]{:S(2)}, u32[]{:S(2)}) %collective-permute-start.60) | collective-permute-done | bytes 262176 | tf_op jit(solution)/shard_map/ppermute | solution.py:285
  316.5 1.5 multiply_reduce_fusion
  318.1 25.2 %attention_back.1.b_ref.g_ref = bf16[3,544,1024]{2,1,0:T(8,128)(2,1)} custom-call(bf16[6,544,512]{2,1,0:T(8,128)(2,1)} %copy-done.26, bf16[6,544,512]{2,1,0:T(8,128)(2,1)} %copy-done.26, bf16[6,544,512]{2,1,0:T(8,128)(2,1)} %copy-done.26, bf16[544,544]{1,0:T(8,128)(2,1)S(1)} %copy-done.15, f32[544,1024]{1,0:T(8,128)S(1)} %copy-done.31, ...), custom_call_target="tpu_custom_call" | custom-call | flops 27499999232 | bytes 50000000 | tf_op jit(solution)/shard_map/attention_back/pallas_call | solution.py:817
  345.5 1.6 collective-permute-start.47
  347.2 7.8 %qkv_grad.1 = (bf16[4,2,2,64,1536]{4,3,2,1,0:T(8,128)(2,1)S(1)}, bf16[4,2,2,64,1536]{4,3,2,1,0:T(8,128)(2,1)S(1)}) custom-call(bf16[544,1024]{1,0:T(8,128)(2,1)S(1)} %copy-done.11, bf16[3,544,1024]{2,1,0:T(8,128)(2,1)S(1)} %copy-done.27), custom_call_target="tpu_custom_call" | custom-call | flops 9900000256 | bytes 18000000 | tf_op jit(solution)/shard_map/qkv_grad/pallas_call | solution.py:669
  355.1 6.8 %input_back.1 = bf16[544,1024]{1,0:T(8,128)(2,1)S(1)} custom-call(bf16[3,544,1024]{2,1,0:T(8,128)(2,1)S(1)} %copy-done.27, f32[544,1024]{1,0:T(8,128)S(1)} %copy-done.28, bf16[4,64,1536]{2,1,0:T(8,128)(2,1)S(1)} %copy-done.13, bf16[4,64,1536]{2,1,0:T(8,128)(2,1)S(1)} %copy-done.20, bf16[4,64,1536]{2,1,0:T(8,128)(2,1)} %collective-permute-done.8.refs_2_, ...), custom_call_target="tpu_custom_call" | custom-call | flops 7699999744 | bytes 14000000 | tf_op jit(solution)/shard_map/input_back/pallas_call | solution.py:851
  361.9 11.5 %collective-permute-done.48 = bf16[4,64,2688]{2,1,0:T(8,128)(2,1)} collective-permute-done((bf16[4,64,2688]{2,1,0:T(8,128)(2,1)}, bf16[4,64,2688]{2,1,0:T(8,128)(2,1)}, u32[]{:S(2)}, u32[]{:S(2)}) %collective-permute-start.48) | collective-permute-done | bytes 1376288 | tf_op jit(solution)/shard_map/ppermute | solution.py:285
  374.0 3.2 fusion
  377.3 6.2 %collective-permute-start.56 = (bf16[64,2688]{1,0:T(8,128)(2,1)S(1)}, bf16[64,2688]{1,0:T(8,128)(2,1)S(1)}, u32[]{:S(2)}, u32[]{:S(2)}) collective-permute-start(bf16[64,2688]{1,0:T(8,128)(2,1)S(1)} %get-tuple-element.249), channel_id=1, source_target_pairs={{0,8},{8,0},{16,24},{24,16},{1,9},{9,1},{17,25},{25,17},{2,10},{10... | collective-permute-start | bytes 1032200 | tf_op jit(solution)/shard_map/ppermute | solution.py:285
  386.0 7.9 %collective-permute-done.56 = bf16[64,2688]{1,0:T(8,128)(2,1)S(1)} collective-permute-done((bf16[64,2688]{1,0:T(8,128)(2,1)S(1)}, bf16[64,2688]{1,0:T(8,128)(2,1)S(1)}, u32[]{:S(2)}, u32[]{:S(2)}) %collective-permute-start.56) | collective-permute-done | bytes 344096 | tf_op jit(solution)/shard_map/ppermute | solution.py:285
  393.9 15.7 %collective-permute-done.57 = bf16[64,2688]{1,0:T(8,128)(2,1)S(1)} collective-permute-done((bf16[64,2688]{1,0:T(8,128)(2,1)S(1)}, bf16[64,2688]{1,0:T(8,128)(2,1)S(1)}, u32[]{:S(2)}, u32[]{:S(2)}) %collective-permute-start.57) | collective-permute-done | bytes 344096 | tf_op jit(solution)/shard_map/ppermute | solution.py:285
  412.7 9.4 %collective-permute-done.49 = bf16[2,64,1536]{2,1,0:T(8,128)(2,1)S(1)} collective-permute-done((bf16[2,64,1536]{2,1,0:T(8,128)(2,1)S(1)}, bf16[2,64,1536]{2,1,0:T(8,128)(2,1)S(1)}, u32[]{:S(2)}, u32[]{:S(2)}) %collective-permute-start.49) | collective-permute-done | bytes 393248 | tf_op jit(solution)/shard_map/ppermute | solution.py:285
  426.2 1.6 slice_bitcast_fusion.16
  429.2 1.7 slice_bitcast_fusion.15
  432.8 10.0 %collective-permute-done.50 = bf16[4,64,1536]{2,1,0:T(8,128)(2,1)} collective-permute-done((bf16[4,64,1536]{2,1,0:T(8,128)(2,1)}, bf16[4,64,1536]{2,1,0:T(8,128)(2,1)}, u32[]{:S(2)}, u32[]{:S(2)}) %collective-permute-start.50) | collective-permute-done | bytes 786464 | tf_op jit(solution)/shard_map/ppermute | solution.py:285
  442.8 3.5 collective-permute-done.52
  446.4 2.1 fusion.3
  451.2 1.8 collective-permute-start.55
  454.3 6.2 %collective-permute-done.54 = bf16[64,1536]{1,0:T(8,128)(2,1)S(1)} collective-permute-done((bf16[64,1536]{1,0:T(8,128)(2,1)S(1)}, bf16[64,1536]{1,0:T(8,128)(2,1)S(1)}, u32[]{:S(2)}, u32[]{:S(2)}) %collective-permute-start.54) | collective-permute-done | bytes 196640 | tf_op jit(solution)/shard_map/ppermute | solution.py:285
  466.3 2.3 collective-permute-start.65
  468.6 14.6 %collective-permute-done.63 = f32[8,128]{1,0:T(8,128)S(1)} collective-permute-done((f32[8,128]{1,0:T(8,128)S(1)}, f32[8,128]{1,0:T(8,128)S(1)}, u32[]{:S(2)}, u32[]{:S(2)}) %collective-permute-start.63) | collective-permute-done | bytes 4128 | tf_op jit(solution)/shard_map/ppermute | solution.py:285
  483.2 5.1 collective-permute-start.66
  488.3 2.0 maximum_select_fusion
  490.3 3.6 copy.158
  495.2 2.2 fusion.1
  497.5 5.4 %copy.159 = f32[2,532,1024]{2,0,1:T(2,128)} copy(f32[2,532,1024]{2,1,0:T(8,128)S(1)} %fusion.1) | data formatting | bytes 8716288
  505.0 1.6 multiply_add_fusion.1
  507.6 1.6 multiply_add_fusion
  (350 shorter events, 82.6 us)
Async XLA Ops:
  1.9 11.4 %collective-permute-start = (bf16[64,1536]{1,0:T(8,128)(2,1)S(1)}, bf16[64,1536]{1,0:T(8,128)(2,1)S(1)}, u32[]{:S(2)}, u32[]{:S(2)}) collective-permute-start(bf16[64,1536]{1,0:T(8,128)(2,1)S(1)} %pad_maximum_fusion.6.refs_0_), channel_id=1, source_target_pairs={{0,8},{8,0},{16,24},{24,16},{1,9},{9,1},{17,25},{25,17},{2,10},{10... | collective-permute-start | bytes 589832 | tf_op jit(solution)/shard_map/ppermute | solution.py:285
  4.9 17.2 %collective-permute-start.1 = (bf16[64,1536]{1,0:T(8,128)(2,1)S(1)}, bf16[64,1536]{1,0:T(8,128)(2,1)S(1)}, u32[]{:S(2)}, u32[]{:S(2)}) collective-permute-start(bf16[64,1536]{1,0:T(8,128)(2,1)S(1)} %pad_maximum_fusion.6.refs_0_), channel_id=1, source_target_pairs={{0,16},{8,24},{16,0},{24,8},{1,17},{9,25},{17,1},{25,9},{2,18},{10... | collective-permute-start | bytes 589832 | tf_op jit(solution)/shard_map/ppermute | solution.py:285
  7.5 14.6 %collective-permute-start.2 = (bf16[64,1536]{1,0:T(8,128)(2,1)S(1)}, bf16[64,1536]{1,0:T(8,128)(2,1)}, u32[]{:S(2)}, u32[]{:S(2)}) collective-permute-start(bf16[64,1536]{1,0:T(8,128)(2,1)S(1)} %pad_maximum_fusion.6.refs_0_), channel_id=1, source_target_pairs={{0,24},{8,16},{16,8},{24,0},{1,25},{9,17},{17,9},{25,1},{2,26},{10... | collective-permute-start | bytes 589832 | tf_op jit(solution)/shard_map/ppermute | solution.py:285
  25.0 16.5 %collective-permute-start.6 = (bf16[4,64,1536]{2,1,0:T(8,128)(2,1)}, bf16[4,64,1536]{2,1,0:T(8,128)(2,1)S(1)}, u32[]{:S(2)}, u32[]{:S(2)}) collective-permute-start(bf16[4,64,1536]{2,1,0:T(8,128)(2,1)} %join_column.4.refs_0_), channel_id=1, source_target_pairs={{0,1},{1,5},{5,4},{4,0},{2,3},{3,7},{7,6},{6,2},{8,9},{9,13},{13,1... | collective-permute-start | bytes 2359304 | tf_op jit(solution)/shard_map/ppermute | solution.py:285
  26.5 16.6 %collective-permute-start.8 = (bf16[4,64,1536]{2,1,0:T(8,128)(2,1)}, bf16[4,64,1536]{2,1,0:T(8,128)(2,1)}, u32[]{:S(2)}, u32[]{:S(2)}) collective-permute-start(bf16[4,64,1536]{2,1,0:T(8,128)(2,1)} %join_column.4.refs_0_), channel_id=1, source_target_pairs={{1,0},{5,1},{4,5},{0,4},{3,2},{7,3},{6,7},{2,6},{9,8},{13,9},{12,1... | collective-permute-start | bytes 2359304 | tf_op jit(solution)/shard_map/ppermute | solution.py:285
  34.9 15.1 %collective-permute-start.3 = (bf16[64,2688]{1,0:T(8,128)(2,1)}, bf16[64,2688]{1,0:T(8,128)(2,1)S(1)}, u32[]{:S(2)}, u32[]{:S(2)}) collective-permute-start(bf16[64,2688]{1,0:T(8,128)(2,1)} %fusion.31.refs_0_), channel_id=1, source_target_pairs={{0,8},{8,0},{16,24},{24,16},{1,9},{9,1},{17,25},{25,17},{2,10},{10... | collective-permute-start | bytes 1032200 | tf_op jit(solution)/shard_map/ppermute | solution.py:285
  37.7 26.9 %collective-permute-start.4 = (bf16[64,2688]{1,0:T(8,128)(2,1)}, bf16[64,2688]{1,0:T(8,128)(2,1)S(1)}, u32[]{:S(2)}, u32[]{:S(2)}) collective-permute-start(bf16[64,2688]{1,0:T(8,128)(2,1)} %fusion.31.refs_0_), channel_id=1, source_target_pairs={{0,16},{8,24},{16,0},{24,8},{1,17},{9,25},{17,1},{25,9},{2,18},{10... | collective-permute-start | bytes 1032200 | tf_op jit(solution)/shard_map/ppermute | solution.py:285
  38.7 25.9 %collective-permute-start.5 = (bf16[64,2688]{1,0:T(8,128)(2,1)}, bf16[64,2688]{1,0:T(8,128)(2,1)S(1)}, u32[]{:S(2)}, u32[]{:S(2)}) collective-permute-start(bf16[64,2688]{1,0:T(8,128)(2,1)} %fusion.31.refs_0_), channel_id=1, source_target_pairs={{0,24},{8,16},{16,8},{24,0},{1,25},{9,17},{17,9},{25,1},{2,26},{10... | collective-permute-start | bytes 1032200 | tf_op jit(solution)/shard_map/ppermute | solution.py:285
  41.5 25.0 %collective-permute-start.7 = (bf16[2,64,1536]{2,1,0:T(8,128)(2,1)S(1)}, bf16[2,64,1536]{2,1,0:T(8,128)(2,1)S(1)}, u32[]{:S(2)}, u32[]{:S(2)}) collective-permute-start(bf16[2,64,1536]{2,1,0:T(8,128)(2,1)S(1)} %slice.216), channel_id=1, source_target_pairs={{0,1},{1,5},{5,4},{4,0},{2,3},{3,7},{7,6},{6,2},{8,9},{9,13},{13,1... | collective-permute-start | bytes 1179656 | tf_op jit(solution)/shard_map/ppermute | solution.py:285
  44.1 22.5 %collective-permute-start.9 = (bf16[2,64,1536]{2,1,0:T(8,128)(2,1)S(1)}, bf16[2,64,1536]{2,1,0:T(8,128)(2,1)}, u32[]{:S(2)}, u32[]{:S(2)}) collective-permute-start(bf16[2,64,1536]{2,1,0:T(8,128)(2,1)S(1)} %slice.217), channel_id=1, source_target_pairs={{1,0},{5,1},{4,5},{0,4},{3,2},{7,3},{6,7},{2,6},{9,8},{13,9},{12,1... | collective-permute-start | bytes 1179656 | tf_op jit(solution)/shard_map/ppermute | solution.py:285
  50.0 20.4 %collective-permute-start.10 = (bf16[4,64,1536]{2,1,0:T(8,128)(2,1)S(1)}, bf16[4,64,1536]{2,1,0:T(8,128)(2,1)}, u32[]{:S(2)}, u32[]{:S(2)}) collective-permute-start(bf16[4,64,1536]{2,1,0:T(8,128)(2,1)S(1)} %copy-done.12), channel_id=1, source_target_pairs={{0,2},{2,0},{1,3},{3,1},{4,6},{6,4},{5,7},{7,5},{8,10},{10,8},{9,1... | collective-permute-start | bytes 2359304 | tf_op jit(solution)/shard_map/ppermute | solution.py:285
  64.5 12.8 %collective-permute-start.11 = (bf16[4,64,1536]{2,1,0:T(8,128)(2,1)S(1)}, bf16[4,64,1536]{2,1,0:T(8,128)(2,1)}, u32[]{:S(2)}, u32[]{:S(2)}) collective-permute-start(bf16[4,64,1536]{2,1,0:T(8,128)(2,1)S(1)} %collective-permute-done.6.refs_1_), channel_id=1, source_target_pairs={{0,2},{2,0},{1,3},{3,1},{4,6},{6,4},{5,7},{7,5},{8,10},{10,8},{9,1... | collective-permute-start | bytes 2359304 | tf_op jit(solution)/shard_map/ppermute | solution.py:285
  64.6 14.3 %collective-permute-start.12 = (bf16[4,64,1536]{2,1,0:T(8,128)(2,1)}, bf16[4,64,1536]{2,1,0:T(8,128)(2,1)}, u32[]{:S(2)}, u32[]{:S(2)}) collective-permute-start(bf16[4,64,1536]{2,1,0:T(8,128)(2,1)} %collective-permute-done.8.refs_2_), channel_id=1, source_target_pairs={{0,2},{2,0},{1,3},{3,1},{4,6},{6,4},{5,7},{7,5},{8,10},{10,8},{9,1... | collective-permute-start | bytes 2359304 | tf_op jit(solution)/shard_map/ppermute | solution.py:285
  66.6 8.2 %collective-permute-start.13 = (bf16[2,64,1536]{2,1,0:T(8,128)(2,1)S(1)}, bf16[2,64,1536]{2,1,0:T(8,128)(2,1)}, u32[]{:S(2)}, u32[]{:S(2)}) collective-permute-start(bf16[2,64,1536]{2,1,0:T(8,128)(2,1)S(1)} %collective-permute-done.7.refs_3_), channel_id=1, source_target_pairs={{0,2},{2,0},{1,3},{3,1},{4,6},{6,4},{5,7},{7,5},{8,10},{10,8},{9,1... | collective-permute-start | bytes 1179656 | tf_op jit(solution)/shard_map/ppermute | solution.py:285
  66.7 9.2 %collective-permute-start.14 = (bf16[2,64,1536]{2,1,0:T(8,128)(2,1)}, bf16[2,64,1536]{2,1,0:T(8,128)(2,1)}, u32[]{:S(2)}, u32[]{:S(2)}) collective-permute-start(bf16[2,64,1536]{2,1,0:T(8,128)(2,1)} %collective-permute-done.9.refs_4_), channel_id=1, source_target_pairs={{0,2},{2,0},{1,3},{3,1},{4,6},{6,4},{5,7},{7,5},{8,10},{10,8},{9,1... | collective-permute-start | bytes 1179656 | tf_op jit(solution)/shard_map/ppermute | solution.py:285
  70.4 43.3 %collective-permute-start.15 = (bf16[64,2048]{1,0:T(8,128)(2,1)}, bf16[64,2048]{1,0:T(8,128)(2,1)S(1)}, u32[]{:S(2)}, u32[]{:S(2)}) collective-permute-start(bf16[64,2048]{1,0:T(8,128)(2,1)} %convert_bitcast_fusion.refs_0_), channel_id=1, source_target_pairs={{0,8},{8,0},{16,24},{24,16},{1,9},{9,1},{17,25},{25,17},{2,10},{10... | collective-permute-start | bytes 786440 | tf_op jit(solution)/shard_map/ppermute | solution.py:285
  74.8 39.4 %collective-permute-start.16 = (bf16[64,2048]{1,0:T(8,128)(2,1)}, bf16[64,2048]{1,0:T(8,128)(2,1)S(1)}, u32[]{:S(2)}, u32[]{:S(2)}) collective-permute-start(bf16[64,2048]{1,0:T(8,128)(2,1)} %convert_bitcast_fusion.refs_0_), channel_id=1, source_target_pairs={{0,16},{8,24},{16,0},{24,8},{1,17},{9,25},{17,1},{25,9},{2,18},{10... | collective-permute-start | bytes 786440 | tf_op jit(solution)/shard_map/ppermute | solution.py:285
  75.9 38.4 %collective-permute-start.17 = (bf16[64,2048]{1,0:T(8,128)(2,1)}, bf16[64,2048]{1,0:T(8,128)(2,1)S(1)}, u32[]{:S(2)}, u32[]{:S(2)}) collective-permute-start(bf16[64,2048]{1,0:T(8,128)(2,1)} %convert_bitcast_fusion.refs_0_), channel_id=1, source_target_pairs={{0,24},{8,16},{16,8},{24,0},{1,25},{9,17},{17,9},{25,1},{2,26},{10... | collective-permute-start | bytes 786440 | tf_op jit(solution)/shard_map/ppermute | solution.py:285
  77.3 32.2 %collective-permute-start.18 = (bf16[4,64,2688]{2,1,0:T(8,128)(2,1)}, bf16[4,64,2688]{2,1,0:T(8,128)(2,1)S(1)}, u32[]{:S(2)}, u32[]{:S(2)}) collective-permute-start(bf16[4,64,2688]{2,1,0:T(8,128)(2,1)} %join_column.3.refs_0_.refs_10_), channel_id=1, source_target_pairs={{0,1},{1,5},{5,4},{4,0},{2,3},{3,7},{7,6},{6,2},{8,9},{9,13},{13,1... | collective-permute-start | bytes 4128776 | tf_op jit(solution)/shard_map/ppermute | solution.py:285
  78.9 32.0 %collective-permute-start.19 = (bf16[4,64,2688]{2,1,0:T(8,128)(2,1)}, bf16[4,64,2688]{2,1,0:T(8,128)(2,1)}, u32[]{:S(2)}, u32[]{:S(2)}) collective-permute-start(bf16[4,64,2688]{2,1,0:T(8,128)(2,1)} %join_column.3.refs_0_.refs_10_), channel_id=1, source_target_pairs={{1,0},{5,1},{4,5},{0,4},{3,2},{7,3},{6,7},{2,6},{9,8},{13,9},{12,1... | collective-permute-start | bytes 4128776 | tf_op jit(solution)/shard_map/ppermute | solution.py:285
  109.5 22.8 %collective-permute-start.22 = (bf16[4,64,2688]{2,1,0:T(8,128)(2,1)S(1)}, bf16[4,64,2688]{2,1,0:T(8,128)(2,1)}, u32[]{:S(2)}, u32[]{:S(2)}) collective-permute-start(bf16[4,64,2688]{2,1,0:T(8,128)(2,1)S(1)} %copy-done.2), channel_id=1, source_target_pairs={{0,2},{2,0},{1,3},{3,1},{4,6},{6,4},{5,7},{7,5},{8,10},{10,8},{9,1... | collective-permute-start | bytes 4128776 | tf_op jit(solution)/shard_map/ppermute | solution.py:285
  110.9 16.6 %collective-permute-start.20 = (bf16[2,64,2688]{2,1,0:T(8,128)(2,1)S(1)}, bf16[2,64,2688]{2,1,0:T(8,128)(2,1)S(1)}, u32[]{:S(2)}, u32[]{:S(2)}) collective-permute-start(bf16[2,64,2688]{2,1,0:T(8,128)(2,1)S(1)} %slice.167), channel_id=1, source_target_pairs={{0,1},{1,5},{5,4},{4,0},{2,3},{3,7},{7,6},{6,2},{8,9},{9,13},{13,1... | collective-permute-start | bytes 2064392 | tf_op jit(solution)/shard_map/ppermute | solution.py:285
  113.6 16.4 %collective-permute-start.21 = (bf16[2,64,2688]{2,1,0:T(8,128)(2,1)S(1)}, bf16[2,64,2688]{2,1,0:T(8,128)(2,1)}, u32[]{:S(2)}, u32[]{:S(2)}) collective-permute-start(bf16[2,64,2688]{2,1,0:T(8,128)(2,1)S(1)} %slice.168), channel_id=1, source_target_pairs={{1,0},{5,1},{4,5},{0,4},{3,2},{7,3},{6,7},{2,6},{9,8},{13,9},{12,1... | collective-permute-start | bytes 2064392 | tf_op jit(solution)/shard_map/ppermute | solution.py:285
  114.2 20.4 %collective-permute-start.23 = (bf16[4,64,2688]{2,1,0:T(8,128)(2,1)S(1)}, bf16[4,64,2688]{2,1,0:T(8,128)(2,1)}, u32[]{:S(2)}, u32[]{:S(2)}) collective-permute-start(bf16[4,64,2688]{2,1,0:T(8,128)(2,1)S(1)} %collective-permute-done.18.refs_1_.refs_11_), channel_id=1, source_target_pairs={{0,2},{2,0},{1,3},{3,1},{4,6},{6,4},{5,7},{7,5},{8,10},{10,8},{9,1... | collective-permute-start | bytes 4128776 | tf_op jit(solution)/shard_map/ppermute | solution.py:285
  114.3 20.3 %collective-permute-start.24 = (bf16[4,64,2688]{2,1,0:T(8,128)(2,1)}, bf16[4,64,2688]{2,1,0:T(8,128)(2,1)}, u32[]{:S(2)}, u32[]{:S(2)}) collective-permute-start(bf16[4,64,2688]{2,1,0:T(8,128)(2,1)} %collective-permute-done.19.refs_2_.refs_12_), channel_id=1, source_target_pairs={{0,2},{2,0},{1,3},{3,1},{4,6},{6,4},{5,7},{7,5},{8,10},{10,8},{9,1... | collective-permute-start | bytes 4128776 | tf_op jit(solution)/shard_map/ppermute | solution.py:285
  127.5 6.6 %collective-permute-start.25 = (bf16[2,64,2688]{2,1,0:T(8,128)(2,1)S(1)}, bf16[2,64,2688]{2,1,0:T(8,128)(2,1)}, u32[]{:S(2)}, u32[]{:S(2)}) collective-permute-start(bf16[2,64,2688]{2,1,0:T(8,128)(2,1)S(1)} %collective-permute-done.20.refs_3_.refs_13_), channel_id=1, source_target_pairs={{0,2},{2,0},{1,3},{3,1},{4,6},{6,4},{5,7},{7,5},{8,10},{10,8},{9,1... | collective-permute-start | bytes 2064392 | tf_op jit(solution)/shard_map/ppermute | solution.py:285
  132.4 26.0 %collective-permute-start.27 = (bf16[4,64,2048]{2,1,0:T(8,128)(2,1)}, bf16[4,64,2048]{2,1,0:T(8,128)(2,1)S(1)}, u32[]{:S(2)}, u32[]{:S(2)}) collective-permute-start(bf16[4,64,2048]{2,1,0:T(8,128)(2,1)} %join_column.5.refs_0_), channel_id=1, source_target_pairs={{0,1},{1,5},{5,4},{4,0},{2,3},{3,7},{7,6},{6,2},{8,9},{9,13},{13,1... | collective-permute-start | bytes 3145736 | tf_op jit(solution)/shard_map/ppermute | solution.py:285
  134.1 25.6 %collective-permute-start.28 = (bf16[4,64,2048]{2,1,0:T(8,128)(2,1)}, bf16[4,64,2048]{2,1,0:T(8,128)(2,1)}, u32[]{:S(2)}, u32[]{:S(2)}) collective-permute-start(bf16[4,64,2048]{2,1,0:T(8,128)(2,1)} %join_column.5.refs_0_), channel_id=1, source_target_pairs={{1,0},{5,1},{4,5},{0,4},{3,2},{7,3},{6,7},{2,6},{9,8},{13,9},{12,1... | collective-permute-start | bytes 3145736 | tf_op jit(solution)/shard_map/ppermute | solution.py:285
  134.6 41.3 %collective-permute-start.31 = (bf16[4,64,2048]{2,1,0:T(8,128)(2,1)}, bf16[4,64,2048]{2,1,0:T(8,128)(2,1)}, u32[]{:S(2)}, u32[]{:S(2)}) collective-permute-start(bf16[4,64,2048]{2,1,0:T(8,128)(2,1)} %join_column.5.refs_0_), channel_id=1, source_target_pairs={{0,2},{2,0},{1,3},{3,1},{4,6},{6,4},{5,7},{7,5},{8,10},{10,8},{9,1... | collective-permute-start | bytes 3145736 | tf_op jit(solution)/shard_map/ppermute | solution.py:285
  159.7 13.3 %collective-permute-start.29 = (bf16[2,64,2048]{2,1,0:T(8,128)(2,1)S(1)}, bf16[2,64,2048]{2,1,0:T(8,128)(2,1)S(1)}, u32[]{:S(2)}, u32[]{:S(2)}) collective-permute-start(bf16[2,64,2048]{2,1,0:T(8,128)(2,1)S(1)} %slice.169), channel_id=1, source_target_pairs={{0,1},{1,5},{5,4},{4,0},{2,3},{3,7},{7,6},{6,2},{8,9},{9,13},{13,1... | collective-permute-start | bytes 1572872 | tf_op jit(solution)/shard_map/ppermute | solution.py:285
  161.4 13.1 %collective-permute-start.30 = (bf16[2,64,2048]{2,1,0:T(8,128)(2,1)S(1)}, bf16[2,64,2048]{2,1,0:T(8,128)(2,1)S(1)}, u32[]{:S(2)}, u32[]{:S(2)}) collective-permute-start(bf16[2,64,2048]{2,1,0:T(8,128)(2,1)S(1)} %slice.170), channel_id=1, source_target_pairs={{1,0},{5,1},{4,5},{0,4},{3,2},{7,3},{6,7},{2,6},{9,8},{13,9},{12,1... | collective-permute-start | bytes 1572872 | tf_op jit(solution)/shard_map/ppermute | solution.py:285
  162.9 13.4 %collective-permute-start.32 = (bf16[4,64,2048]{2,1,0:T(8,128)(2,1)S(1)}, bf16[4,64,2048]{2,1,0:T(8,128)(2,1)S(1)}, u32[]{:S(2)}, u32[]{:S(2)}) collective-permute-start(bf16[4,64,2048]{2,1,0:T(8,128)(2,1)S(1)} %collective-permute-done.27.refs_1_), channel_id=1, source_target_pairs={{0,2},{2,0},{1,3},{3,1},{4,6},{6,4},{5,7},{7,5},{8,10},{10,8},{9,1... | collective-permute-start | bytes 3145736 | tf_op jit(solution)/shard_map/ppermute | solution.py:285
  162.9 13.4 %collective-permute-start.33 = (bf16[4,64,2048]{2,1,0:T(8,128)(2,1)}, bf16[4,64,2048]{2,1,0:T(8,128)(2,1)S(1)}, u32[]{:S(2)}, u32[]{:S(2)}) collective-permute-start(bf16[4,64,2048]{2,1,0:T(8,128)(2,1)} %collective-permute-done.28.refs_2_), channel_id=1, source_target_pairs={{0,2},{2,0},{1,3},{3,1},{4,6},{6,4},{5,7},{7,5},{8,10},{10,8},{9,1... | collective-permute-start | bytes 3145736 | tf_op jit(solution)/shard_map/ppermute | solution.py:285
  211.2 7.5 %collective-permute-start.37 = (bf16[4,2,2,64,2048]{4,3,0,2,1:T(8,128)(2,1)}, bf16[4,2,2,64,2048]{4,3,0,2,1:T(8,128)(2,1)}, u32[]{:S(2)}, u32[]{:S(2)}) collective-permute-start(bf16[4,2,2,64,2048]{4,3,0,2,1:T(8,128)(2,1)} %copy.139), channel_id=1, source_target_pairs={{0,2},{2,0},{1,3},{3,1},{4,6},{6,4},{5,7},{7,5},{8,10},{10,8},{9,1... | collective-permute-start | bytes 12582920 | tf_op jit(solution)/shard_map/ppermute | solution.py:285
  222.9 33.8 %collective-permute-start.38 = (bf16[2,64,2048]{2,1,0:T(8,128)(2,1)S(1)}, bf16[2,64,2048]{2,1,0:T(8,128)(2,1)S(1)}, u32[]{:S(2)}, u32[]{:S(2)}) collective-permute-start(bf16[2,64,2048]{2,1,0:T(8,128)(2,1)S(1)} %get-tuple-element.263), channel_id=1, source_target_pairs={{0,1},{1,5},{5,4},{4,0},{2,3},{3,7},{7,6},{6,2},{8,9},{9,13},{13,1... | collective-permute-start | bytes 1572872 | tf_op jit(solution)/shard_map/ppermute | solution.py:285
  223.5 33.2 %collective-permute-start.39 = (bf16[2,64,2048]{2,1,0:T(8,128)(2,1)S(1)}, bf16[2,64,2048]{2,1,0:T(8,128)(2,1)}, u32[]{:S(2)}, u32[]{:S(2)}) collective-permute-start(bf16[2,64,2048]{2,1,0:T(8,128)(2,1)S(1)} %get-tuple-element.262), channel_id=1, source_target_pairs={{1,0},{5,1},{4,5},{0,4},{3,2},{7,3},{6,7},{2,6},{9,8},{13,9},{12,1... | collective-permute-start | bytes 1572872 | tf_op jit(solution)/shard_map/ppermute | solution.py:285
  264.3 26.9 %collective-permute-start.40 = (bf16[4,2,2,64,2688]{4,3,2,1,0:T(8,128)(2,1)}, bf16[4,2,2,64,2688]{4,3,2,1,0:T(8,128)(2,1)}, u32[]{:S(2)}, u32[]{:S(2)}) collective-permute-start(bf16[4,2,2,64,2688]{4,3,2,1,0:T(8,128)(2,1)} %get-tuple-element.109), channel_id=1, source_target_pairs={{0,2},{2,0},{1,3},{3,1},{4,6},{6,4},{5,7},{7,5},{8,10},{10,8},{9,1... | collective-permute-start | bytes 16515080 | tf_op jit(solution)/shard_map/ppermute | solution.py:285
  264.4 25.7 %collective-permute-start.42 = (bf16[4,64,2048]{2,1,0:T(8,128)(2,1)S(1)}, bf16[4,64,2048]{2,1,0:T(8,128)(2,1)}, u32[]{:S(2)}, u32[]{:S(2)}) collective-permute-start(bf16[4,64,2048]{2,1,0:T(8,128)(2,1)S(1)} %pad_maximum_fusion.3), channel_id=1, source_target_pairs={{1,0},{5,1},{4,5},{0,4},{3,2},{7,3},{6,7},{2,6},{9,8},{13,9},{12,1... | collective-permute-start | bytes 3145736 | tf_op jit(solution)/shard_map/ppermute | solution.py:285
  265.9 25.3 %collective-permute-start.41 = (bf16[4,64,2048]{2,1,0:T(8,128)(2,1)S(1)}, bf16[4,64,2048]{2,1,0:T(8,128)(2,1)}, u32[]{:S(2)}, u32[]{:S(2)}) collective-permute-start(bf16[4,64,2048]{2,1,0:T(8,128)(2,1)S(1)} %pad_maximum_fusion.2), channel_id=1, source_target_pairs={{0,1},{1,5},{5,4},{4,0},{2,3},{3,7},{7,6},{6,2},{8,9},{9,13},{13,1... | collective-permute-start | bytes 3145736 | tf_op jit(solution)/shard_map/ppermute | solution.py:285
  294.4 12.2 %collective-permute-start.59 = (bf16[64,2048]{1,0:T(8,128)(2,1)S(1)}, bf16[64,2048]{1,0:T(8,128)(2,1)S(1)}, u32[]{:S(2)}, u32[]{:S(2)}) collective-permute-start(bf16[64,2048]{1,0:T(8,128)(2,1)S(1)} %get-tuple-element.252), channel_id=1, source_target_pairs={{0,8},{8,0},{16,24},{24,16},{1,9},{9,1},{17,25},{25,17},{2,10},{10... | collective-permute-start | bytes 786440 | tf_op jit(solution)/shard_map/ppermute | solution.py:285
  295.1 21.4 %collective-permute-start.60 = (bf16[64,2048]{1,0:T(8,128)(2,1)S(1)}, bf16[64,2048]{1,0:T(8,128)(2,1)S(1)}, u32[]{:S(2)}, u32[]{:S(2)}) collective-permute-start(bf16[64,2048]{1,0:T(8,128)(2,1)S(1)} %get-tuple-element.254), channel_id=1, source_target_pairs={{0,16},{8,24},{16,0},{24,8},{1,17},{9,25},{17,1},{25,9},{2,18},{10... | collective-permute-start | bytes 786440 | tf_op jit(solution)/shard_map/ppermute | solution.py:285
  297.4 19.1 %collective-permute-start.61 = (bf16[64,2048]{1,0:T(8,128)(2,1)S(1)}, bf16[64,2048]{1,0:T(8,128)(2,1)S(1)}, u32[]{:S(2)}, u32[]{:S(2)}) collective-permute-start(bf16[64,2048]{1,0:T(8,128)(2,1)S(1)} %get-tuple-element.253), channel_id=1, source_target_pairs={{0,24},{8,16},{16,8},{24,0},{1,25},{9,17},{17,9},{25,1},{2,26},{10... | collective-permute-start | bytes 786440 | tf_op jit(solution)/shard_map/ppermute | solution.py:285
  300.6 42.6 %collective-permute-start.43 = (bf16[2,64,2688]{2,1,0:T(8,128)(2,1)S(1)}, bf16[2,64,2688]{2,1,0:T(8,128)(2,1)S(1)}, u32[]{:S(2)}, u32[]{:S(2)}) collective-permute-start(bf16[2,64,2688]{2,1,0:T(8,128)(2,1)S(1)} %slice_bitcast_fusion.7), channel_id=1, source_target_pairs={{0,1},{1,5},{5,4},{4,0},{2,3},{3,7},{7,6},{6,2},{8,9},{9,13},{13,1... | collective-permute-start | bytes 2064392 | tf_op jit(solution)/shard_map/ppermute | solution.py:285
  301.2 42.0 %collective-permute-start.44 = (bf16[2,64,2688]{2,1,0:T(8,128)(2,1)S(1)}, bf16[2,64,2688]{2,1,0:T(8,128)(2,1)S(1)}, u32[]{:S(2)}, u32[]{:S(2)}) collective-permute-start(bf16[2,64,2688]{2,1,0:T(8,128)(2,1)S(1)} %slice_bitcast_fusion.6), channel_id=1, source_target_pairs={{1,0},{5,1},{4,5},{0,4},{3,2},{7,3},{6,7},{2,6},{9,8},{13,9},{12,1... | collective-permute-start | bytes 2064392 | tf_op jit(solution)/shard_map/ppermute | solution.py:285
  344.8 28.7 %collective-permute-start.48 = (bf16[4,64,2688]{2,1,0:T(8,128)(2,1)}, bf16[4,64,2688]{2,1,0:T(8,128)(2,1)}, u32[]{:S(2)}, u32[]{:S(2)}) collective-permute-start(bf16[4,64,2688]{2,1,0:T(8,128)(2,1)} %pad_maximum_fusion.1), channel_id=1, source_target_pairs={{1,0},{5,1},{4,5},{0,4},{3,2},{7,3},{6,7},{2,6},{9,8},{13,9},{12,1... | collective-permute-start | bytes 4128776 | tf_op jit(solution)/shard_map/ppermute | solution.py:285
  345.5 28.5 %collective-permute-start.47 = (bf16[4,64,2688]{2,1,0:T(8,128)(2,1)S(1)}, bf16[4,64,2688]{2,1,0:T(8,128)(2,1)}, u32[]{:S(2)}, u32[]{:S(2)}) collective-permute-start(bf16[4,64,2688]{2,1,0:T(8,128)(2,1)S(1)} %pad_maximum_fusion), channel_id=1, source_target_pairs={{0,1},{1,5},{5,4},{4,0},{2,3},{3,7},{7,6},{6,2},{8,9},{9,13},{13,1... | collective-permute-start | bytes 4128776 | tf_op jit(solution)/shard_map/ppermute | solution.py:285
  355.0 54.7 %collective-permute-start.46 = (bf16[4,2,2,64,1536]{4,3,2,1,0:T(8,128)(2,1)S(1)}, bf16[4,2,2,64,1536]{4,3,2,1,0:T(8,128)(2,1)S(1)}, u32[]{:S(2)}, u32[]{:S(2)}) collective-permute-start(bf16[4,2,2,64,1536]{4,3,2,1,0:T(8,128)(2,1)S(1)} %get-tuple-element.120), channel_id=1, source_target_pairs={{0,2},{2,0},{1,3},{3,1},{4,6},{6,4},{5,7},{7,5},{8,10},{10,8},{9,1... | collective-permute-start | bytes 9437192 | tf_op jit(solution)/shard_map/ppermute | solution.py:285
  377.3 16.6 %collective-permute-start.56 = (bf16[64,2688]{1,0:T(8,128)(2,1)S(1)}, bf16[64,2688]{1,0:T(8,128)(2,1)S(1)}, u32[]{:S(2)}, u32[]{:S(2)}) collective-permute-start(bf16[64,2688]{1,0:T(8,128)(2,1)S(1)} %get-tuple-element.249), channel_id=1, source_target_pairs={{0,8},{8,0},{16,24},{24,16},{1,9},{9,1},{17,25},{25,17},{2,10},{10... | collective-permute-start | bytes 1032200 | tf_op jit(solution)/shard_map/ppermute | solution.py:285
  383.6 26.0 %collective-permute-start.57 = (bf16[64,2688]{1,0:T(8,128)(2,1)S(1)}, bf16[64,2688]{1,0:T(8,128)(2,1)S(1)}, u32[]{:S(2)}, u32[]{:S(2)}) collective-permute-start(bf16[64,2688]{1,0:T(8,128)(2,1)S(1)} %get-tuple-element.251), channel_id=1, source_target_pairs={{0,16},{8,24},{16,0},{24,8},{1,17},{9,25},{17,1},{25,9},{2,18},{10... | collective-permute-start | bytes 1032200 | tf_op jit(solution)/shard_map/ppermute | solution.py:285
  384.6 25.0 %collective-permute-start.58 = (bf16[64,2688]{1,0:T(8,128)(2,1)S(1)}, bf16[64,2688]{1,0:T(8,128)(2,1)S(1)}, u32[]{:S(2)}, u32[]{:S(2)}) collective-permute-start(bf16[64,2688]{1,0:T(8,128)(2,1)S(1)} %get-tuple-element.250), channel_id=1, source_target_pairs={{0,24},{8,16},{16,8},{24,0},{1,25},{9,17},{17,9},{25,1},{2,26},{10... | collective-permute-start | bytes 1032200 | tf_op jit(solution)/shard_map/ppermute | solution.py:285
  410.1 12.0 %collective-permute-start.49 = (bf16[2,64,1536]{2,1,0:T(8,128)(2,1)S(1)}, bf16[2,64,1536]{2,1,0:T(8,128)(2,1)S(1)}, u32[]{:S(2)}, u32[]{:S(2)}) collective-permute-start(bf16[2,64,1536]{2,1,0:T(8,128)(2,1)S(1)} %slice_bitcast_fusion.11), channel_id=1, source_target_pairs={{0,1},{1,5},{5,4},{4,0},{2,3},{3,7},{7,6},{6,2},{8,9},{9,13},{13,1... | collective-permute-start | bytes 1179656 | tf_op jit(solution)/shard_map/ppermute | solution.py:285
  412.0 12.6 %collective-permute-start.51 = (bf16[2,64,1536]{2,1,0:T(8,128)(2,1)S(1)}, bf16[2,64,1536]{2,1,0:T(8,128)(2,1)S(1)}, u32[]{:S(2)}, u32[]{:S(2)}) collective-permute-start(bf16[2,64,1536]{2,1,0:T(8,128)(2,1)S(1)} %slice_bitcast_fusion.10), channel_id=1, source_target_pairs={{1,0},{5,1},{4,5},{0,4},{3,2},{7,3},{6,7},{2,6},{9,8},{13,9},{12,1... | collective-permute-start | bytes 1179656 | tf_op jit(solution)/shard_map/ppermute | solution.py:285
  423.1 19.7 %collective-permute-start.50 = (bf16[4,64,1536]{2,1,0:T(8,128)(2,1)}, bf16[4,64,1536]{2,1,0:T(8,128)(2,1)}, u32[]{:S(2)}, u32[]{:S(2)}) collective-permute-start(bf16[4,64,1536]{2,1,0:T(8,128)(2,1)} %pad_maximum_fusion.4), channel_id=1, source_target_pairs={{0,1},{1,5},{5,4},{4,0},{2,3},{3,7},{7,6},{6,2},{8,9},{9,13},{13,1... | collective-permute-start | bytes 2359304 | tf_op jit(solution)/shard_map/ppermute | solution.py:285
  425.6 20.8 %collective-permute-start.52 = (bf16[4,64,1536]{2,1,0:T(8,128)(2,1)}, bf16[4,64,1536]{2,1,0:T(8,128)(2,1)}, u32[]{:S(2)}, u32[]{:S(2)}) collective-permute-start(bf16[4,64,1536]{2,1,0:T(8,128)(2,1)} %pad_maximum_fusion.5), channel_id=1, source_target_pairs={{1,0},{5,1},{4,5},{0,4},{3,2},{7,3},{6,7},{2,6},{9,8},{13,9},{12,1... | collective-permute-start | bytes 2359304 | tf_op jit(solution)/shard_map/ppermute | solution.py:285
  427.8 60.5 %collective-permute-start.36 = (bf16[532,1024]{1,0:T(8,128)(2,1)}, bf16[532,1024]{1,0:T(8,128)(2,1)}, u32[]{:S(2)}, u32[]{:S(2)}) collective-permute-start(bf16[532,1024]{1,0:T(8,128)(2,1)} %get-tuple-element.261), channel_id=1, source_target_pairs={{0,1},{1,0},{2,3},{3,2},{4,5},{5,4},{6,7},{7,6},{8,9},{9,8},{10,11... | collective-permute-start | bytes 3268616 | tf_op jit(solution)/shard_map/ppermute | solution.py:285
  430.9 64.3 %collective-permute-start.45 = (bf16[532,1024]{1,0:T(8,128)(2,1)}, bf16[532,1024]{1,0:T(8,128)(2,1)}, u32[]{:S(2)}, u32[]{:S(2)}) collective-permute-start(bf16[532,1024]{1,0:T(8,128)(2,1)} %get-tuple-element.259), channel_id=1, source_target_pairs={{0,1},{1,0},{2,3},{3,2},{4,5},{5,4},{6,7},{7,6},{8,9},{9,8},{10,11... | collective-permute-start | bytes 3268616 | tf_op jit(solution)/shard_map/ppermute | solution.py:285
  448.5 5.8 %collective-permute-start.53 = (bf16[64,1536]{1,0:T(8,128)(2,1)S(1)}, bf16[64,1536]{1,0:T(8,128)(2,1)S(1)}, u32[]{:S(2)}, u32[]{:S(2)}) collective-permute-start(bf16[64,1536]{1,0:T(8,128)(2,1)S(1)} %get-tuple-element.255), channel_id=1, source_target_pairs={{0,8},{8,0},{16,24},{24,16},{1,9},{9,1},{17,25},{25,17},{2,10},{10... | collective-permute-start | bytes 589832 | tf_op jit(solution)/shard_map/ppermute | solution.py:285
  449.8 10.8 %collective-permute-start.54 = (bf16[64,1536]{1,0:T(8,128)(2,1)S(1)}, bf16[64,1536]{1,0:T(8,128)(2,1)S(1)}, u32[]{:S(2)}, u32[]{:S(2)}) collective-permute-start(bf16[64,1536]{1,0:T(8,128)(2,1)S(1)} %get-tuple-element.257), channel_id=1, source_target_pairs={{0,16},{8,24},{16,0},{24,8},{1,17},{9,25},{17,1},{25,9},{2,18},{10... | collective-permute-start | bytes 589832 | tf_op jit(solution)/shard_map/ppermute | solution.py:285
  451.2 9.4 %collective-permute-start.55 = (bf16[64,1536]{1,0:T(8,128)(2,1)S(1)}, bf16[64,1536]{1,0:T(8,128)(2,1)S(1)}, u32[]{:S(2)}, u32[]{:S(2)}) collective-permute-start(bf16[64,1536]{1,0:T(8,128)(2,1)S(1)} %get-tuple-element.256), channel_id=1, source_target_pairs={{0,24},{8,16},{16,8},{24,0},{1,25},{9,17},{17,9},{25,1},{2,26},{10... | collective-permute-start | bytes 589832 | tf_op jit(solution)/shard_map/ppermute | solution.py:285
  465.1 18.1 %collective-permute-start.63 = (f32[8,128]{1,0:T(8,128)S(1)}, f32[8,128]{1,0:T(8,128)S(1)}, u32[]{:S(2)}, u32[]{:S(2)}) collective-permute-start(f32[8,128]{1,0:T(8,128)S(1)} %broadcast_add_fusion), channel_id=1, source_target_pairs={{0,1},{1,0},{4,5},{5,4},{2,3},{3,2},{6,7},{7,6},{8,9},{9,8},{12,13... | collective-permute-start | bytes 12296 | tf_op jit(solution)/shard_map/ppermute | solution.py:285
  465.1 18.1 %collective-permute-start.64 = (f32[8,128]{1,0:T(8,128)S(1)}, f32[8,128]{1,0:T(8,128)S(1)}, u32[]{:S(2)}, u32[]{:S(2)}) collective-permute-start(f32[8,128]{1,0:T(8,128)S(1)} %broadcast_add_fusion), channel_id=1, source_target_pairs={{0,4},{1,5},{4,0},{5,1},{2,6},{3,7},{6,2},{7,3},{8,12},{9,13},{12,... | collective-permute-start | bytes 12296 | tf_op jit(solution)/shard_map/ppermute | solution.py:285
  466.3 16.9 %collective-permute-start.65 = (f32[8,128]{1,0:T(8,128)S(1)}, f32[8,128]{1,0:T(8,128)S(1)}, u32[]{:S(2)}, u32[]{:S(2)}) collective-permute-start(f32[8,128]{1,0:T(8,128)S(1)} %broadcast_add_fusion), channel_id=1, source_target_pairs={{0,5},{1,4},{4,1},{5,0},{2,7},{3,6},{6,3},{7,2},{8,13},{9,12},{12,... | collective-permute-start | bytes 12296 | tf_op jit(solution)/shard_map/ppermute | solution.py:285
  483.2 10.7 %collective-permute-start.66 = (f32[8,128]{1,0:T(8,128)S(1)}, f32[8,128]{1,0:T(8,128)S(1)}, u32[]{:S(2)}, u32[]{:S(2)}) collective-permute-start(f32[8,128]{1,0:T(8,128)S(1)} %add_add_fusion), channel_id=1, source_target_pairs={{0,8},{8,0},{16,24},{24,16},{1,9},{9,1},{17,25},{25,17},{2,10},{10... | collective-permute-start | bytes 12296 | tf_op jit(solution)/shard_map/ppermute | solution.py:285
  493.9 9.0 %collective-permute-start.67 = (f32[8,128]{1,0:T(8,128)S(1)}, f32[8,128]{1,0:T(8,128)S(1)}, u32[]{:S(2)}, u32[]{:S(2)}) collective-permute-start(f32[8,128]{1,0:T(8,128)S(1)} %add.572), channel_id=1, source_target_pairs={{0,16},{8,24},{16,0},{24,8},{1,17},{9,25},{17,1},{25,9},{2,18},{10... | collective-permute-start | bytes 12296 | tf_op jit(solution)/shard_map/ppermute | solution.py:285
  (91 other events, 775.1 us)

commit v2 on v1

--- a/solution.py
+++ b/solution.py
@@ -315,7 +315,7 @@
 TN = (((0,), (0,)), ((), ()))
 NN = (((1,), (0,)), ((), ()))
 F32, LOW = jnp.float32, jnp.bfloat16
-ANYWHERE = pl.BlockSpec(memory_space=pl.ANY)
+ANYWHERE = pl.BlockSpec(memory_space=pltpu.HBM)
 
 
 def params(mib):
@@ -365,8 +365,31 @@
         out_specs=pl.BlockSpec(memory_space=pltpu.VMEM),
         out_shape=shaped(shape, pieces[0].dtype),
         scratch_shapes=[pltpu.SemaphoreType.DMA((count,))],
+        compiler_params=params(60),
         name="join_column",
     )(*pieces)
+
+
+def join_pair_kernel(axis, own, other, out, sem):
+    place = lax.axis_index(axis)
+    copies = [pltpu.make_async_copy(own, out.at[place], sem.at[0])]
+    copies.append(pltpu.make_async_copy(other, out.at[1 - place], sem.at[1]))
+    for copy in copies:
+        copy.start()
+    for copy in copies:
+        copy.wait()
+
+
+def join_pair(own, other, axis):
+    return pl.pallas_call(
+        functools.partial(join_pair_kernel, axis),
+        in_specs=[ANYWHERE] * 2,
+        out_specs=pl.BlockSpec(memory_space=pltpu.VMEM),
+        out_shape=shaped((2,) + own.shape, own.dtype),
+        scratch_shapes=[pltpu.SemaphoreType.DMA((2,))],
+        compiler_params=params(60),
+        name="join_pair",
+    )(own, other)
 
 
 def both_cores(pieces):
@@ -389,6 +412,19 @@
                 ).start()
 
 
+def load_lines(pieces, w, sem, width, per_side):
+    z, core = lax.axis_index("z"), lax.axis_index("c")
+    count = len(pieces) // 2
+    for k in range(per_side):
+        for group, core_at in ((pieces[:count], core), (pieces[count:], 1 - core)):
+            for i, ref in enumerate(group):
+                for y in range(2):
+                    chunk = y * per_side + k
+                    pltpu.make_async_copy(
+                        ref.at[:, y, :, pl.ds(k * width, width)], w.at[chunk, z ^ i, :, core_at], sem.at[chunk]
+                    ).start()
+
+
 def ready(w, sem, chunk):
     pltpu.make_async_copy(w.at[chunk], w.at[chunk], sem.at[chunk]).wait()
 
@@ -431,7 +467,7 @@
         out_specs=pl.BlockSpec((1, x.shape[0], width), lambda j: (at(j), 0, 0)),
         out_shape=shaped((2 * per_side, x.shape[0], width), LOW),
         scratch_shapes=chunk_buffer((count, rows), 2 * per_side, width),
-        compiler_params=params(32),
+        compiler_params=params(60),
         cost_estimate=cost(6 * 1.1e9, 6 * 2e6),
         name="project",
     )(x, *pieces)
@@ -474,7 +510,7 @@
         in_specs=pair_specs(total, pairs // 2) + [full(bias.shape)],
         out_specs=[pl.BlockSpec((total, 128), lambda g: (0, g))] * 2,
         out_shape=[shaped((total, width), LOW), shaped((total, width), F32)],
-        compiler_params=params(48),
+        compiler_params=params(60),
         cost_estimate=cost(17 * 1.1e9, 17 * 2e6),
         name="attention",
     )(qkv, qkv, qkv, bias)
@@ -579,7 +615,7 @@
         + chunk_buffer((count, rows), 2, width)
         + chunk_buffer((count, 16), 2, 128)
         + [pltpu.VMEM(x.shape, F32)],
-        compiler_params=params(56),
+        compiler_params=params(60),
         cost_estimate=cost(22 * 1.1e9, 22 * 2e6),
         name="up",
     )(x, context, *pieces)
@@ -592,7 +628,7 @@
 
     @pl.when(j == 0)
     def _():
-        load_weights(pieces, w, sem, 0, g_ref.shape[2], per_side)
+        load_lines(pieces, w, sem, g_ref.shape[2], per_side)
         acc[...] = jnp.zeros_like(acc)
 
     chunk = alternate(per_side)(j)
@@ -624,7 +660,7 @@
     chunks, total = active.shape[0], active.shape[1]
     at = alternate(chunks // 2)
     shape = normed.shape
-    count = pieces[0].shape[0]
+    count = len(pieces) // 2
     return pl.pallas_call(
         functools.partial(down_kernel, chunks // 2, len(pieces)),
         grid=(chunks,),
@@ -633,46 +669,65 @@
         out_specs=[full(shape), full(shape), full(shape), full(norms.shape)],
         out_shape=[shaped(shape, LOW), shaped(shape, F32), shaped(shape, LOW), shaped(norms.shape, F32)],
         scratch_shapes=chunk_buffer((count, rows), chunks, width) + [pltpu.VMEM(shape, F32)],
-        compiler_params=params(56),
+        compiler_params=params(60),
         cost_estimate=cost(17 * 1.1e9, 17 * 2e6),
         name="down",
     )(active, normed, norms, cot, *pieces)
 
 
-def share_out(value, own_ref, other_ref):
+def share_out(value, own_ref, other_ref, lines_first=False):
     core = lax.axis_index("c")
-    z, x, _, rows, width = own_ref.shape
-    value = value.reshape(z, x, 2, rows, width)
+    if lines_first:
+        z, x, _, rows, width = own_ref.shape
+        value = value.reshape(z, x, 2, rows, width)
+        for parity in range(2):
+
+            @pl.when(core == parity)
+            def _(parity=parity):
+                own_ref[:, :, 0] = value[:, :, parity]
+
+            @pl.when(core != parity)
+            def _(parity=parity):
+                other_ref[:, :, 0] = value[:, :, parity]
+
+        return
+    squares, _, z, rows, width = own_ref.shape
+    value = value.reshape(z, squares, 2, rows, width)
     for parity in range(2):
-        part = value[:, :, parity]
 
         @pl.when(core == parity)
-        def _(part=part):
-            own_ref[:, :, 0] = part
+        def _(parity=parity):
+            for x in range(squares):
+                own_ref[x, 0] = value[:, x, parity]
 
         @pl.when(core != parity)
-        def _(part=part):
-            other_ref[:, :, 0] = part
+        def _(parity=parity):
+            for x in range(squares):
+                other_ref[x, 0] = value[:, x, parity]
 
 
 def share_specs(count, rows, per_side, columns):
-    spec = pl.BlockSpec((count, 2, 1, rows, STEP_WIDTH), lambda j: (0, 0, j // per_side, 0, j % per_side))
-    return [spec] * 2, [shaped((count, 2, 2, rows, columns), LOW)] * 2
-
-
-def weight_grad_kernel(a_ref, b_ref, own_ref, other_ref):
-    share_out(mm(a_ref[...], b_ref[0], TN).astype(LOW), own_ref, other_ref)
-
-
-def weight_grad(a, b, spec, chunks, count, rows, name):
-    out_specs, out_shape = share_specs(count, rows, chunks // 2, chunks // 2 * STEP_WIDTH)
+    spec = pl.BlockSpec((2, 1, count, rows, STEP_WIDTH), lambda j: (0, j // per_side, 0, 0, j % per_side))
+    return [spec] * 2, [shaped((2, 2, count, rows, columns), LOW)] * 2
+
+
+def weight_grad_kernel(lines_first, a_ref, b_ref, own_ref, other_ref):
+    share_out(mm(a_ref[...], b_ref[0], TN).astype(LOW), own_ref, other_ref, lines_first)
+
+
+def weight_grad(a, b, spec, chunks, count, rows, name, lines_first=False):
+    per_side = chunks // 2
+    out_specs, out_shape = share_specs(count, rows, per_side, per_side * STEP_WIDTH)
+    if lines_first:
+        spec_out = pl.BlockSpec((count, 2, 1, rows, STEP_WIDTH), lambda j: (0, 0, j // per_side, 0, j % per_side))
+        out_specs, out_shape = [spec_out] * 2, [shaped((count, 2, 2, rows, per_side * STEP_WIDTH), LOW)] * 2
     return pl.pallas_call(
-        weight_grad_kernel,
+        functools.partial(weight_grad_kernel, lines_first),
         grid=(chunks,),
         in_specs=[full(a.shape), spec],
         out_specs=out_specs,
         out_shape=out_shape,
-        compiler_params=params(32),
+        compiler_params=params(60),
         cost_estimate=cost(9 * 1.1e9, 9 * 2e6),
         name=name,
     )(a, b)
@@ -686,7 +741,7 @@
 
     @pl.when(j == 0)
     def _():
-        load_weights(downs, wd, ds, 0, width, per_side)
+        load_lines(downs, wd, ds, width, per_side)
         load_weights(ups, wu, us, 0, width, per_side)
         acc[...] = r_ref[...]
 
@@ -733,7 +788,7 @@
         out_specs=out_specs + [full(shape), full(shape), full(norms.shape)],
         out_shape=out_shape + [shaped(shape, F32), shaped(shape, LOW), shaped(norms.shape, F32)],
         scratch_shapes=chunk_buffer((count, rows), chunks, width) * 2 + [pltpu.VMEM(shape, F32)],
-        compiler_params=params(58),
+        compiler_params=params(60),
         cost_estimate=cost(32 * 1.1e9, 32 * 2e6),
         name="inner_back",
     )(feed_grad, slope, hidden, second_grad, normed, inverse, norms, *downs, *ups)
@@ -742,7 +797,7 @@
 def out_kernel(column, a_ref, ctx_ref, one_ref, two_ref, own_in, other_in, *refs):
     pieces = refs[:10]
     own_ref, other_ref, o_ref, w, sem, tiles, out_sem = refs[10:]
-    _, _, z, x, rows, _ = tiles.shape
+    _, _, x, z, rows, _ = tiles.shape
     width = w.shape[5]
     core = lax.axis_index("c")
     load_weights(pieces, w, sem, column, width, 1)
@@ -751,18 +806,19 @@
         grad = mm(a_ref[...], ctx_ref[:, y * width : (y + 1) * width], TN).astype(LOW).reshape(z, x, 2, rows, width)
         for parity in range(2):
             slot = (parity + core) % 2
-            tiles[slot, y, :, :, :, :width] = grad[:, :, parity]
+            for at_x in range(x):
+                tiles[slot, y, at_x, :, :, :width] = grad[:, at_x, parity]
             for at in range(z * x):
                 cell = norm_grads[:, (at * 2 + parity) * rows : (at * 2 + parity + 1) * rows]
                 cell = jnp.concatenate([cell, jnp.zeros((8, 128 - rows), F32)], axis=1)
                 cell = jnp.concatenate([cell, jnp.zeros((rows - 8, 128), F32)], axis=0)
-                tiles[slot, y, at // x, at % x, :, width:] = cell.astype(LOW)
+                tiles[slot, y, at % x, at // x, :, width:] = cell.astype(LOW)
     copies = []
     for slot, ref in enumerate((own_ref, other_ref)):
         for y in range(2):
             copies.append(
                 pltpu.make_async_copy(
-                    tiles.at[slot, y], ref.at[:, :, y, :, pl.ds(column, width + 128)], out_sem.at[slot, y]
+                    tiles.at[slot, y], ref.at[:, y, :, :, pl.ds(column, width + 128)], out_sem.at[slot, y]
                 )
             )
     for copy in copies:
@@ -783,9 +839,9 @@
         out_specs=[ANYWHERE, ANYWHERE, inside],
         out_shape=[shaped(own.shape, LOW), shaped(other.shape, LOW), shaped(context.shape, LOW)],
         scratch_shapes=chunk_buffer((count, rows), 2, width)
-        + [pltpu.VMEM((2, 2, count, 2, rows, width + 128), LOW), pltpu.SemaphoreType.DMA((2, 2))],
+        + [pltpu.VMEM((2, 2, 2, count, rows, width + 128), LOW), pltpu.SemaphoreType.DMA((2, 2))],
         input_output_aliases={4: 0, 5: 1},
-        compiler_params=params(40),
+        compiler_params=params(60),
         cost_estimate=cost(4 * 1.1e9, 4 * 2e6),
         name="out_back",
     )(branch_grad, context, one, two, own, other, *pieces)
@@ -810,6 +866,31 @@
         o_ref[i] = jnp.where(lane < HEAD, outs[0][i], outs[1][i]).astype(LOW)
 
 
+def final_rows_kernel(own_ref, other_ref, o_ref):
+    y = lax.axis_index("y")
+    for place in range(2):
+
+        @pl.when(y == place)
+        def _(place=place):
+            o_ref[:, place] = own_ref[...]
+            o_ref[:, 1 - place] = other_ref[...]
+
+
+def final_rows(own, other):
+    total, width = own.shape
+    block = pl.BlockSpec((ROWS_AT_ONCE, width), lambda i: (i, 0))
+    both = pl.pallas_call(
+        final_rows_kernel,
+        grid=(pl.cdiv(total, ROWS_AT_ONCE),),
+        in_specs=[block, block],
+        out_specs=pl.BlockSpec((ROWS_AT_ONCE, 2, width), lambda i: (i, 0, 0)),
+        out_shape=shaped((total, 2, width), own.dtype),
+        compiler_params=params(60),
+        name="final_rows",
+    )(own, other)
+    return both.transpose(1, 0, 2)
+
+
 def attention_back(qkv, bias, logs, grad):
     total, width = grad.shape
     pairs = width // 128
@@ -820,45 +901,55 @@
         in_specs=pair_specs(total, pairs // 2) + [full(bias.shape), column, column],
         out_specs=pl.BlockSpec((3, total, 128), lambda g: (0, 0, g)),
         out_shape=shaped((3, total, width), LOW),
-        compiler_params=params(48),
+        compiler_params=params(60),
         cost_estimate=cost(25 * 1.1e9, 25 * 2e6),
         name="attention_back",
     )(qkv, qkv, qkv, bias, logs, grad)
 
 
-def input_kernel(per_side, g_ref, r_ref, *refs):
-    pieces, (o_ref, w, sem, acc) = refs[:10], refs[10:]
+def qkv_back_kernel(per_side, x_ref, g_ref, r_ref, *refs):
+    pieces, (own_ref, other_ref, o_ref, w, sem, acc) = refs[:10], refs[10:]
     j = pl.program_id(0)
 
     @pl.when(j == 0)
     def _():
         load_weights(pieces, w, sem, 0, g_ref.shape[2], per_side)
-        acc[...] = r_ref[...]
-
-    chunk = alternate(per_side)(j)
-    ready(w, sem, chunk)
-    acc[...] += mm(g_ref[0], matrix(w, chunk), NT)
+
+    grad = g_ref[0]
+    share_out(mm(x_ref[...], grad, TN).astype(LOW), own_ref, other_ref)
+    ready(w, sem, j)
+    term = mm(grad, matrix(w, j), NT)
+
+    @pl.when(j == 0)
+    def _():
+        acc[...] = r_ref[...] + term
+
+    @pl.when(j > 0)
+    def _():
+        acc[...] += term
 
     @pl.when(j == 2 * per_side - 1)
     def _():
         o_ref[...] = acc[...].astype(LOW)
 
 
-def input_back(grads, first_grad, pieces, rows):
+def qkv_back(x, grads, first_grad, pieces, rows):
     count, width = pieces[0].shape[0], STEP_WIDTH
     per_side = grads.shape[0]
     shape = first_grad.shape
+    out_specs, out_shape = share_specs(count, rows, per_side, per_side * width)
     return pl.pallas_call(
-        functools.partial(input_kernel, per_side),
+        functools.partial(qkv_back_kernel, per_side),
         grid=(2 * per_side,),
-        in_specs=[pl.BlockSpec((1, shape[0], width), lambda j: (j // 2, 0, j % 2)), full(shape)] + [ANYWHERE] * 10,
-        out_specs=full(shape),
-        out_shape=shaped(shape, LOW),
+        in_specs=[full(shape), pl.BlockSpec((1, shape[0], width), lambda j: (j % per_side, 0, j // per_side)), full(shape)]
+        + [ANYWHERE] * 10,
+        out_specs=out_specs + [full(shape)],
+        out_shape=out_shape + [shaped(shape, LOW)],
         scratch_shapes=chunk_buffer((count, rows), 2 * per_side, width) + [pltpu.VMEM(shape, F32)],
-        compiler_params=params(40),
-        cost_estimate=cost(7 * 1.1e9, 7 * 2e6),
-        name="input_back",
-    )(grads, first_grad, *pieces)
+        compiler_params=params(60),
+        cost_estimate=cost(16 * 1.1e9, 16 * 2e6),
+        name="qkv_back",
+    )(x, grads, first_grad, *pieces)
 
 
 def at(a, index, axis):
@@ -867,25 +958,37 @@
 
 def chip_term(own, other, shift):
     x, y = place_xy(ring_place() + shift)
-    return at(at(own, x, 1), y, 1).astype(F32) + at(at(other, x, 1), y, 1).astype(F32)
+    return at(at(own, x, 0), y, 0).astype(F32) + at(at(other, x, 0), y, 0).astype(F32)
 
 
 def ring_pair(to_right, to_left):
     return send(to_right, ("x", "y"), RING), send(to_left, ("x", "y"), RING_BACK)
 
 
-def far_terms(own, other):
-    far = chip_term(own, other, 2).astype(LOW)
+def far_terms(take):
+    far = take(2).astype(LOW)
     half = far.shape[0] // 2
     return far[:half], far[half:]
 
 
-def near_terms(own, other, from_left, from_right):
+def near_terms(take, from_left, from_right):
     half = from_left.shape[0]
-    right, left = chip_term(own, other, 1), chip_term(own, other, -1)
+    right, left = take(1).astype(F32), take(-1).astype(F32)
     to_right = jnp.concatenate([right[:half] + from_left.astype(F32), right[half:]]).astype(LOW)
     to_left = jnp.concatenate([left[:half], left[half:] + from_right.astype(F32)]).astype(LOW)
     return to_right, to_left
+
+
+def chip_terms(own, other):
+    return lambda shift: chip_term(own, other, shift)
+
+
+def square_terms(square):
+    def take(shift):
+        x, y = place_xy(ring_place() + shift)
+        return at(at(square, x, 0), y, 0)
+
+    return take
 
 
 def line_terms(own, other, from_left, from_right):
@@ -977,19 +1080,25 @@
     second_block = jnp.concatenate([up_weight.astype(LOW), out_weight.T.astype(LOW), norm_block], axis=1)
     down_block = down_weight.T.astype(LOW)
 
+    pair_down = join_pair(down_block, send(down_block, "y", SWAP), "y")
+    qkv_block = after(qkv_block, down_block)
+    tokens, cotangent, doc_ids = after((tokens, cotangent, doc_ids), pair_down)
     x = pad_rows(mine(tokens), total)
     cot = pad_rows(mine(cotangent), total)
     bias = mask_bias(mine(doc_ids), mine(reset_flags), mine(mem_live), total)
 
     z_qkv = line_pieces(qkv_block)
+    other_pair = send(pair_down, "x", SWAP)
     z_second = line_pieces(after(second_block, *z_qkv))
-    column_qkv = join_column(z_qkv)
+    column_qkv = join_column(after(tuple(z_qkv), x, cot, bias, other_pair))
+    square_down = join_pair(pair_down, other_pair, "x")
     near_qkv = ring_near(column_qkv)
     far_qkv = ring_far(*near_qkv)
     w_qkv = both_cores((column_qkv,) + near_qkv + far_qkv)
-    z_down = line_pieces(after(down_block, *z_second))
     column_second = after(join_column(z_second), *far_qkv)
     near_second = ring_near(column_second)
+    square_down = after(square_down, column_second)
+    down_one, down_two = send(square_down, "z", partners(1)), send(square_down, "z", partners(2))
 
     qkv = project(after(x, column_second), w_qkv, rows)
     context, logs = attention(qkv, bias)
@@ -997,14 +1106,12 @@
     near_second = after(near_second, context)
     far_second = ring_far(*near_second)
     w_second = both_cores((column_second,) + near_second + far_second)
-    column_down = after(join_column([after(z_down[0], context)] + z_down[1:]), *far_second)
-    near_down = ring_near(column_down)
-
-    hidden, normed, inverse, norms, active, slope = up(x, after(context, column_down), w_second, rows, inner_part)
-
-    near_down = after(near_down, active)
-    far_down = ring_far(*near_down)
-    w_down = both_cores((column_down,) + near_down + far_down)
+    down_two = after(down_two, near_second[0])
+    down_three = send(down_two, "z", partners(1))
+
+    hidden, normed, inverse, norms, active, slope = up(x, after(context, down_two), w_second, rows, inner_part)
+
+    w_down = both_cores((square_down, down_one, down_two, after(down_three, active)))
     result, second_grad, feed_grad, norm_two = down(active, normed, norms, cot, w_down, rows)
 
     chunks = active.shape[0]
@@ -1016,13 +1123,26 @@
         count,
         rows,
         "down_grad",
-    )
+        lines_first=True,
+    )
+    z, place_x = lax.axis_index("z"), lax.axis_index("x")
+
+    def pair(own, other):
+        own, other = jnp.where(y == 0, own, other), jnp.where(y == 0, other, own)
+        return jnp.stack([own, other], axis=1).transpose(1, 0, 2)
+
+    def term(own, other):
+        return lambda k: at(own, z ^ k, 0).astype(F32) + at(other, z ^ k, 0).astype(F32)
+
     other_down = send(other, "c", SWAP)
-    far = far_terms(own_down, other_down)
-    far_down = ring_pair(*far)
+    down_term = term(own_down, other_down)
+    crossing = down_term(3).astype(LOW)
+    crossed = send(crossing, "z", partners(1))
+    own_result = result[:real]
+    shared_result = send(own_result, "y", SWAP)
     columns = inner_part + part + 128
     own, other, first_grad, branch_grad, norm_one = inner_back(
-        after(feed_grad, *far),
+        after(feed_grad, crossing, own_result),
         slope,
         hidden,
         second_grad,
@@ -1034,55 +1154,65 @@
         rows,
         columns,
     )
-    far_down = after(far_down, branch_grad)
-    near = near_terms(own_down, other_down, *far_down)
-    near_down = ring_pair(*near)
+    crossed, shared_result = after(crossed, branch_grad), after(shared_result, branch_grad)
+    one, two = down_term(1).astype(LOW), (down_term(2) + crossed.astype(F32)).astype(LOW)
+    from_one, from_two = send(one, "z", partners(1)), send(two, "z", partners(2))
     own_second, other, context_grad = out_back(
-        after(branch_grad, *near), context, norm_one, norm_two, own, other, w_second, rows, inner_part
+        after(branch_grad, one, two, shared_result),
+        context,
+        norm_one,
+        norm_two,
+        own,
+        other,
+        w_second,
+        rows,
+        inner_part,
     )
     other_second = send(other, "c", SWAP)
-    near_down = after(near_down, context_grad, other_second)
-    line_down = line_terms(own_down, other_down, *near_down)
-    others_down = line_send(line_down)
-    far = far_terms(own_second, after(other_second, *near_down))
+    take_second = chip_terms(own_second, other_second)
+    far = far_terms(take_second)
     far_second = ring_pair(*far)
-
-    grads = attention_back(qkv, bias, logs, after(context_grad, *far, *line_down))
+    grads = attention_back(qkv, bias, logs, after(context_grad, *far))
 
     far_second = after(far_second, grads)
-    near = near_terms(own_second, other_second, *far_second)
+    near = near_terms(take_second, *far_second)
     near_second = ring_pair(*near)
-    own_qkv, other = weight_grad(
-        after(x, *near),
-        grads,
-        pl.BlockSpec((1, total, STEP_WIDTH), lambda j: (j % 3, 0, j // 3)),
-        6,
-        count,
-        rows,
-        "qkv_grad",
-    )
-    other_qkv = send(other, "c", SWAP)
-    own_grad = input_back(after(grads, own_qkv), first_grad, w_qkv, rows)
-    near_second = after(near_second, own_grad)
-    line_second = line_terms(own_second, other_second, *near_second)
-    others_second = line_send(line_second)
-    far = far_terms(own_qkv, after(other_qkv, *near_second))
+    from_one, from_two = after(from_one, *near), after(from_two, *near)
+    square = down_term(0) + from_one.astype(F32) + from_two.astype(F32)
+    to_x = at(square, 1 - place_x, 0).astype(LOW)
+    own_qkv, other, own_grad = qkv_back(after(x, to_x), grads, first_grad, w_qkv, rows)
+    near_second = after(near_second, own_qkv)
+    from_x = send(after(to_x, *near_second), "x", SWAP)
+    other_qkv = send(after(other, *near_second), "c", SWAP)
+    shared_grad = send(after(own_grad[: total // 2], *near_second), "y", SWAP)
+    column = chip_term(own_second, other_second, 0) + near_second[0].astype(F32) + near_second[1].astype(F32)
+    crossing = at(column, z ^ 3, 0).astype(LOW)
+    crossed = send(crossing, "z", partners(1))
+    take_qkv = chip_terms(own_qkv, after(other_qkv, crossing))
+    far = far_terms(take_qkv)
     far_qkv = ring_pair(*far)
-    near = near_terms(own_qkv, after(other_qkv, *line_second), *far_qkv)
+    from_x, shared_grad = after(from_x, *far), after(shared_grad, *far)
+    half = at(square, place_x, 0) + from_x.astype(F32)
+    to_y = at(half, 1 - y, 0).astype(LOW)
+    crossed = after(crossed, *far)
+    one, two = at(column, z ^ 1, 0).astype(LOW), (at(column, z ^ 2, 0) + crossed.astype(F32)).astype(LOW)
+    from_one, from_two = send(one, "z", partners(1)), send(two, "z", partners(2))
+    far_qkv = after(far_qkv, one, two, to_y, shared_grad)
+    near = near_terms(take_qkv, *far_qkv)
     near_qkv = ring_pair(*near)
-    line_qkv = line_terms(own_qkv, other_qkv, *near_qkv)
+    output = final_rows(own_result, after(shared_result, *near))
+    near_qkv = after(near_qkv, output)
+    from_one, from_two = after(from_one, *near), after(from_two, *near)
+    second_sum = at(column, z, 0) + from_one.astype(F32) + from_two.astype(F32)
+    line_qkv = line_terms(own_qkv, other_qkv, *after(near_qkv, second_sum))
     others_qkv = line_send(line_qkv)
-    down_sum = total_of(line_down[0], others_down)
-    second_sum = total_of(line_second[0], others_second)
+    from_y = send(after(to_y, *line_qkv), "y", SWAP)
+    last_rows = after(own_grad[total // 2 : real], *line_qkv)
+    shared_grad = jnp.concatenate([shared_grad, send(last_rows, "y", SWAP)])
+    down_sum = at(half, y, 0) + from_y.astype(F32)
+    others_qkv = after(tuple(others_qkv), down_sum, shared_grad)
+    input_grad = pair(own_grad[:real], shared_grad).astype(F32)
     qkv_sum = total_of(line_qkv[0], others_qkv)
-
-    def both(own):
-        own = own[:real]
-        other = send(own, "y", SWAP)
-        return jnp.where(y == 0, jnp.stack([own, other]), jnp.stack([other, own]))
-
-    output = both(result)
-    input_grad = both(own_grad).astype(F32)
 
     qkv_sum = qkv_sum.reshape(rows, 3, part).transpose(1, 0, 2)
     up_sum = second_sum[:, :inner_part]
@@ -1118,7 +1248,7 @@
         )
 
     def run(*args):
-        if narrow == 2 and wide % 8 == 0 and args[0].shape[0] == wide * narrow:
+        if narrow == 2 and wide == 16 and args[0].shape[0] == wide * narrow:
             body = whole_segment
             grid = jax.sharding.Mesh(mesh.devices.reshape(wide // 4, 2, 2, 2), ("z", "x", "c", "y"))
             ins, outs = placed(("z", "x", "c"), "y")

time: 522 us -> 438 us (0.84)
  waiting for transfers between devices: 188 us -> 95.3 us
  Pallas kernels: 156 us -> 179 us
  local copies, waits for them, and re-layouts: 42.3 us -> 30.5 us
  starting transfers between devices: 75.9 us -> 66.9 us
  other arithmetic: 43.4 us -> 50.3 us
    ppermute x68 -> x64, waiting for transfers between devices: 188 us -> 95.3 us  [send(): return lax.ppermute(block, axes, list(pairs))]
    pallas_call x3 -> x5, Pallas kernels: 24.4 us -> 44.3 us  [the longest x1 17.4 us: qkv_back(): pl.pallas_call(functools.partial(qkv_back_kernel, per_side), grid=(2 * pe...]
    unnamed x178 -> x126, local copies, waits for them, and re-layouts: 22.1 us -> 13 us
    ppermute x68 -> x64, starting transfers between devices: 75.9 us -> 66.9 us  [send(): return lax.ppermute(block, axes, list(pairs))]
    dynamic_slice x3 -> x2, local copies, waits for them, and re-layouts: 8.42 us -> 0.59 us  [mine(): return lax.dynamic_index_in_dim(a, y, 0, keepdims=False)]
    add x4 -> x6, other arithmetic: 7.04 us -> 14 us  [the longest x2 6.61 us: chip_term(): at(at(own, x, 0), y, 0).astype(F32) + at(at(other, x, 0), y, 0).astype(F32)]
    add x3 -> x1, other arithmetic: 8.29 us -> 2.24 us  [line_terms(): chip_term(own, other, 0) + from_left.astype(F32) + from_right.astype(F32)]
  transfers between devices with their start and end apart: 68 -> 64, of which waited for: 28 -> 30; matrix products, arithmetic and copies ran while one was open for 10% -> 13% of each run, Pallas kernels for 24% -> 32%
where the time goes in v2:
time: 438 us; the launch traced here: 430 us
  Pallas kernels  179 us (41%)
  waiting for transfers between devices  95.3 us (22%)
  starting transfers between devices  66.9 us (15%)
  other arithmetic  50.3 us (11%)
  local copies, waits for them, and re-layouts  30.5 us (7%)
  between operations  7.89 us (2%)
    ppermute x64, waiting for transfers between devices, send(): return lax.ppermute(block, axes, list(pairs))  95.3 us
    ppermute x64, starting transfers between devices, send(): return lax.ppermute(block, axes, list(pairs))  66.9 us
    pallas_call x1, Pallas kernels, inner_back(): pl.pallas_call(functools.partial(inner_kernel, chunks // 2, len(downs)),...  31.4 us
    pallas_call x1, Pallas kernels, attention_back(): pl.pallas_call(attend_back_kernel, grid=(pairs,), in_specs=pair_specs(tot...  25.2 us
    pallas_call x1, Pallas kernels, up(): pl.pallas_call(functools.partial(up_kernel, per_side), grid=(2 * per_side...  22.2 us
    pallas_call x1, Pallas kernels, down(): pl.pallas_call(functools.partial(down_kernel, chunks // 2, len(pieces)),...  18.8 us
    pallas_call x1, Pallas kernels, attention(): pl.pallas_call(attend_kernel, grid=(pairs,), in_specs=pair_specs(total, p...  18.1 us
    pallas_call x1, Pallas kernels, qkv_back(): pl.pallas_call(functools.partial(qkv_back_kernel, per_side), grid=(2 * pe...  17.4 us
  transfers between devices with their start and end apart: 64, of which 30 were waited for; matrix products, arithmetic and copies ran while one was open for 13% of the time, Pallas kernels for 32%

profile of v2, /device:TPU:0, one launch (start us, length us, event | category | flops | bytes accessed | tf_op | source)
XLA Modules:
  0.0 430.1 jit_solution(3111483105044572178)
XLA Ops:
  1.9 3.0 collective-permute-start
  6.1 1.6 collective-permute-start.1
  7.7 2.6 collective-permute-start.2
  12.5 1.8 join_pair.2.own
  22.3 2.7 collective-permute-done.2.refs_2_
  25.0 2.4 collective-permute-done.7.other
  27.3 2.3 join_column.3.refs_0_
  33.4 2.5 collective-permute-start.5
  36.3 12.2 %collective-permute-done.8.refs_1_ = bf16[4,64,1536]{2,1,0:T(8,128)(2,1)} collective-permute-done((bf16[4,64,1536]{2,1,0:T(8,128)(2,1)}, bf16[4,64,1536]{2,1,0:T(8,128)(2,1)}, u32[]{:S(2)}, u32[]{:S(2)}) %collective-permute-start.8) | collective-permute-done | bytes 786464 | tf_op jit(solution)/shard_map/ppermute | solution.py:285
  52.8 7.3 %collective-permute-done.5.refs_2_ = bf16[64,2688]{1,0:T(8,128)(2,1)S(1)} collective-permute-done((bf16[64,2688]{1,0:T(8,128)(2,1)S(1)}, bf16[64,2688]{1,0:T(8,128)(2,1)S(1)}, u32[]{:S(2)}, u32[]{:S(2)}) %collective-permute-start.5) | collective-permute-done | bytes 344096 | tf_op jit(solution)/shard_map/ppermute | solution.py:285
  62.7 2.4 join_column.2.refs_0_.refs_8_
  65.2 2.3 join_pair.3.refs_0_
  67.5 1.7 collective-permute-start.18
  69.6 3.5 collective-permute-start.17
  73.8 8.2 %project.1.q_ref.k_ref.v_ref = bf16[6,544,512]{2,1,0:T(8,128)(2,1)} custom-call(bf16[544,1024]{1,0:T(8,128)(2,1)} %pad.15.x_ref, bf16[4,64,1536]{2,1,0:T(8,128)(2,1)} %join_column.3.refs_0_, bf16[4,64,1536]{2,1,0:T(8,128)(2,1)} %collective-permute-done.8.refs_1_, bf16[4,64,1536]{2,1,0:T(8,128)(2,1)} %collective-permute-done.10.refs_2_, ...), custom_call_target="tpu_custom_call" | custom-call | flops 6600000000 | bytes 12000000 | tf_op jit(solution)/shard_map/project/pallas_call | solution.py:463
  82.0 18.1 %attention.1 = (bf16[544,1024]{1,0:T(8,128)(2,1)}, f32[544,1024]{1,0:T(8,128)}) custom-call(bf16[6,544,512]{2,1,0:T(8,128)(2,1)} %project.1.q_ref.k_ref.v_ref, bf16[6,544,512]{2,1,0:T(8,128)(2,1)} %project.1.q_ref.k_ref.v_ref, bf16[6,544,512]{2,1,0:T(8,128)(2,1)} %project.1.q_ref.k_ref.v_ref, bf16[544,544]{1,0:T(8,128)(2,1)} %select_convert_fusion.bias_ref), custom_call_target="tpu_custom_call" | custom-call | flops 18699999232 | bytes 34000000 | tf_op jit(solution)/shard_map/attention/pallas_call | solution.py:507
  105.5 14.3 %collective-permute-done.17.refs_2_ = bf16[2,2,64,2048]{3,2,1,0:T(8,128)(2,1)} collective-permute-done((bf16[2,2,64,2048]{3,2,1,0:T(8,128)(2,1)}, bf16[2,2,64,2048]{3,2,1,0:T(8,128)(2,1)}, u32[]{:S(2)}, u32[]{:S(2)}) %collective-permute-start.17) | collective-permute-done | bytes 1048608 | tf_op jit(solution)/shard_map/ppermute | solution.py:285
  121.9 3.0 collective-permute-done.25.refs_8_.refs_16_
  125.1 1.8 collective-permute-done.26.refs_9_.refs_17_
  128.2 22.2 %up.1 = (bf16[544,1024]{1,0:T(8,128)(2,1)}, f32[544,1024]{1,0:T(8,128)}, f32[544,128]{1,0:T(8,128)}, f32[8,1024]{1,0:T(8,128)}, bf16[8,544,512]{2,1,0:T(8,128)(2,1)}, /*index=5*/bf16[8,544,512]{2,1,0:T(8,128)(2,1)}) custom-call(bf16[544,1024]{1,0:T(8,128)(2,1)} %pad.15.x_ref, bf16[544,1024]{1,0:T(8,128)(2,1)} %get-tuple-element.113.ctx_ref, ...), custom_call_target="tpu_custom_call" | custom-call | flops 24199999488 | bytes 44000000 | tf_op jit(solution)/shard_map/up/pallas_call | solution.py:601
  150.4 2.0 collective-permute-done.28.refs_3_
  152.4 2.8 collective-permute-done.32.refs_7_
  156.2 18.8 %down.1 = (bf16[544,1024]{1,0:T(8,128)(2,1)}, f32[544,1024]{1,0:T(8,128)}, bf16[544,1024]{1,0:T(8,128)(2,1)}, f32[8,1024]{1,0:T(8,128)}) custom-call(bf16[8,544,512]{2,1,0:T(8,128)(2,1)} %get-tuple-element.115.g_ref.b_ref, f32[544,1024]{1,0:T(8,128)} %get-tuple-element.116.n_ref, f32[8,1024]{1,0:T(8,128)} %get-tuple-element.117.norms_ref, ...), custom_call_target="tpu_custom_call" | custom-call | flops 18699999232 | bytes 34000000 | tf_op jit(solution)/shard_map/down/pallas_call | solution.py:664
  175.0 12.7 %down_grad.1 = (bf16[4,2,2,64,2048]{4,3,2,1,0:T(8,128)(2,1)}, bf16[4,2,2,64,2048]{4,3,2,1,0:T(8,128)(2,1)}) custom-call(bf16[544,1024]{1,0:T(8,128)(2,1)} %get-tuple-element.123.a_ref.f_ref, bf16[8,544,512]{2,1,0:T(8,128)(2,1)} %get-tuple-element.115.g_ref.b_ref), custom_call_target="tpu_custom_call" | custom-call | flops 9900000256 | bytes 18000000 | tf_op jit(solution)/shard_map/down_grad/pallas_call | solution.py:724
  189.5 5.7 %collective-permute-done.34 = bf16[4,2,2,64,2048]{4,3,2,1,0:T(8,128)(2,1)} collective-permute-done((bf16[4,2,2,64,2048]{4,3,2,1,0:T(8,128)(2,1)}, bf16[4,2,2,64,2048]{4,3,2,1,0:T(8,128)(2,1)}, u32[]{:S(2)}, u32[]{:S(2)}) %collective-permute-start.34) | collective-permute-done | bytes 4194336 | tf_op jit(solution)/shard_map/ppermute | solution.py:285
  195.2 4.4 %fusion.9 = (bf16[2,2,64,2048]{3,2,1,0:T(8,128)(2,1)}, bf16[2,2,64,2048]{3,2,1,0:T(8,128)(2,1)}) fusion(bf16[4,2,2,64,2048]{4,3,2,1,0:T(8,128)(2,1)} %collective-permute-done.34, s32[]{:T(128)S(6)} %select_n.192, bf16[4,2,2,64,2048]{4,3,2,1,0:T(8,128)(2,1)} %get-tuple-element.121, s32[]{:T(128)S(6)} %select_n.190), kind=kLoop, calls=%fused_computation.33 | loop fusion | flops 4194304 | bytes 6291464 | tf_op jit(solution)/shard_map/convert_element_type | solution.py:1158
  199.8 31.4 %inner_back.1 = (bf16[2,2,4,64,2688]{4,3,2,1,0:T(8,128)(2,1)}, bf16[2,2,4,64,2688]{4,3,2,1,0:T(8,128)(2,1)}, f32[544,1024]{1,0:T(8,128)}, bf16[544,1024]{1,0:T(8,128)(2,1)}, f32[8,1024]{1,0:T(8,128)}) custom-call(bf16[544,1024]{1,0:T(8,128)(2,1)} %get-tuple-element.123.a_ref.f_ref, bf16[8,544,512]{2,1,0:T(8,128)(2,1)} %get-tuple-element.124.d_ref, ...), custom_call_target="tpu_custom_call" | custom-call | flops 35200000000 | bytes 64000000 | tf_op jit(solution)/shard_map/inner_back/pallas_call | solution.py:782
  231.3 3.5 fusion.1
  234.8 6.1 %out_back.1 = (bf16[2,2,4,64,2688]{4,3,2,1,0:T(8,128)(2,1)}, bf16[2,2,4,64,2688]{4,3,2,1,0:T(8,128)(2,1)}, bf16[544,1024]{1,0:T(8,128)(2,1)}) custom-call(bf16[544,1024]{1,0:T(8,128)(2,1)} %get-tuple-element.131.a_ref, bf16[544,1024]{1,0:T(8,128)(2,1)} %get-tuple-element.113.ctx_ref, ...), custom_call_target="tpu_custom_call", output_to_operand_aliasing={{0}: (4, {}), {1}: (5, {})} | custom-call | flops 4400000000 | bytes 8000000 | tf_op jit(solution)/shard_map/out_back/pallas_call | solution.py:836
  241.1 1.8 collective-permute-start.35
  244.4 6.0 %collective-permute-done.37 = bf16[2,2,4,64,2688]{4,3,2,1,0:T(8,128)(2,1)} collective-permute-done((bf16[2,2,4,64,2688]{4,3,2,1,0:T(8,128)(2,1)}, bf16[2,2,4,64,2688]{4,3,2,1,0:T(8,128)(2,1)}, u32[]{:S(2)}, u32[]{:S(2)}) %collective-permute-start.37) | collective-permute-done | bytes 5505056 | tf_op jit(solution)/shard_map/ppermute | solution.py:285
  250.3 4.3 convert_add_fusion
  255.9 1.7 collective-permute-start.38
  258.0 25.2 %attention_back.1.g_ref = bf16[3,544,1024]{2,1,0:T(8,128)(2,1)} custom-call(bf16[6,544,512]{2,1,0:T(8,128)(2,1)} %project.1.q_ref.k_ref.v_ref, bf16[6,544,512]{2,1,0:T(8,128)(2,1)} %project.1.q_ref.k_ref.v_ref, bf16[6,544,512]{2,1,0:T(8,128)(2,1)} %project.1.q_ref.k_ref.v_ref, bf16[544,544]{1,0:T(8,128)(2,1)} %select_convert_fusion.bias_ref, ...), custom_call_target="tpu_custom_call" | custom-call | flops 27499999232 | bytes 50000000 | tf_op jit(solution)/shard_map/attention_back/pallas_call | solution.py:898
  283.4 1.6 fusion.5
  289.7 2.9 fusion.2
  294.8 17.4 %qkv_back.1 = (bf16[2,2,4,64,1536]{4,3,2,1,0:T(8,128)(2,1)}, bf16[2,2,4,64,1536]{4,3,2,1,0:T(8,128)(2,1)}, bf16[544,1024]{1,0:T(8,128)(2,1)}) custom-call(bf16[544,1024]{1,0:T(8,128)(2,1)} %pad.15.x_ref, bf16[3,544,1024]{2,1,0:T(8,128)(2,1)} %attention_back.1.g_ref, f32[544,1024]{1,0:T(8,128)} %get-tuple-element.146.r_ref, ...), custom_call_target="tpu_custom_call" | custom-call | flops 17600000000 | bytes 32000000 | tf_op jit(solution)/shard_map/qkv_back/pallas_call | solution.py:941
  312.1 6.1 %collective-permute-done.42 = bf16[4,64,2688]{2,1,0:T(8,128)(2,1)} collective-permute-done((bf16[4,64,2688]{2,1,0:T(8,128)(2,1)}, bf16[4,64,2688]{2,1,0:T(8,128)(2,1)}, u32[]{:S(2)}, u32[]{:S(2)}) %collective-permute-start.42) | collective-permute-done | bytes 1376288 | tf_op jit(solution)/shard_map/ppermute | solution.py:285
  318.2 2.5 collective-permute-done.41
  322.1 1.9 slice.158
  324.5 1.7 collective-permute-start.47
  326.2 3.4 fusion
  329.6 1.8 collective-permute-start.46
  331.7 2.3 convert_add_fusion.2
  335.7 3.0 collective-permute-done.48
  338.7 2.4 collective-permute-start.45
  341.2 3.2 collective-permute-start.52
  346.8 2.2 collective-permute-done.45
  354.0 4.3 collective-permute-done.52
  359.0 10.1 %final_rows.1 = bf16[532,2,1024]{2,1,0:T(2,128)(2,1)} custom-call(bf16[532,1024]{1,0:T(8,128)(2,1)} %copy-done.6, bf16[532,1024]{1,0:T(8,128)(2,1)} %copy-done.21), custom_call_target="tpu_custom_call" | custom-call | tf_op jit(solution)/shard_map/final_rows/pallas_call | solution.py:882
  370.2 2.2 fusion.3
  379.2 1.7 collective-permute-start.55
  382.9 2.6 multiply_reduce_fusion
  385.5 4.2 collective-permute-done.53
  389.6 1.9 constant_dynamic-update-slice_fusion
  391.5 2.0 collective-permute-done.55
  398.8 1.7 collective-permute-start.59
  400.6 1.7 collective-permute-start.61
  402.4 1.7 collective-permute-done.60
  405.2 2.6 collective-permute-start.62
  409.4 3.2 collective-permute-start.63
  412.9 5.4 %copy.79 = f32[2,532,1024]{2,0,1:T(2,128)} copy(f32[2,532,1024]{2,1,0:T(8,128)S(1)} %convert_bitcast_fusion) | data formatting | bytes 8716288
  421.4 3.2 multiply_add_fusion
  424.7 1.6 multiply_add_fusion.1
  (284 shorter events, 77.3 us)
Async XLA Ops:
  1.9 9.9 %collective-permute-start = (bf16[64,2048]{1,0:T(8,128)(2,1)S(1)}, bf16[64,2048]{1,0:T(8,128)(2,1)S(1)}, u32[]{:S(2)}, u32[]{:S(2)}) collective-permute-start(bf16[64,2048]{1,0:T(8,128)(2,1)S(1)} %convert_bitcast_fusion.1.own), channel_id=1, source_target_pairs={{0,1},{1,0},{2,3},{3,2},{4,5},{5,4},{6,7},{7,6},{8,9},{9,8},{10,11... | collective-permute-start | bytes 786440 | tf_op jit(solution)/shard_map/ppermute | solution.py:285
  6.1 16.3 %collective-permute-start.1 = (bf16[64,1536]{1,0:T(8,128)(2,1)S(1)}, bf16[64,1536]{1,0:T(8,128)(2,1)}, u32[]{:S(2)}, u32[]{:S(2)}) collective-permute-start(bf16[64,1536]{1,0:T(8,128)(2,1)S(1)} %pad_maximum_fusion.4.refs_0_), channel_id=1, source_target_pairs={{0,8},{8,0},{16,24},{24,16},{1,9},{9,1},{17,25},{25,17},{2,10},{10... | collective-permute-start | bytes 589832 | tf_op jit(solution)/shard_map/ppermute | solution.py:285
  7.7 17.3 %collective-permute-start.2 = (bf16[64,1536]{1,0:T(8,128)(2,1)S(1)}, bf16[64,1536]{1,0:T(8,128)(2,1)}, u32[]{:S(2)}, u32[]{:S(2)}) collective-permute-start(bf16[64,1536]{1,0:T(8,128)(2,1)S(1)} %pad_maximum_fusion.4.refs_0_), channel_id=1, source_target_pairs={{0,16},{8,24},{16,0},{24,8},{1,17},{9,25},{17,1},{25,9},{2,18},{10... | collective-permute-start | bytes 589832 | tf_op jit(solution)/shard_map/ppermute | solution.py:285
  10.3 14.7 %collective-permute-start.3 = (bf16[64,1536]{1,0:T(8,128)(2,1)S(1)}, bf16[64,1536]{1,0:T(8,128)(2,1)}, u32[]{:S(2)}, u32[]{:S(2)}) collective-permute-start(bf16[64,1536]{1,0:T(8,128)(2,1)S(1)} %pad_maximum_fusion.4.refs_0_), channel_id=1, source_target_pairs={{0,24},{8,16},{16,8},{24,0},{1,25},{9,17},{17,9},{25,1},{2,26},{10... | collective-permute-start | bytes 589832 | tf_op jit(solution)/shard_map/ppermute | solution.py:285
  14.4 13.0 %collective-permute-start.7 = (bf16[2,64,2048]{2,1,0:T(8,128)(2,1)}, bf16[2,64,2048]{2,1,0:T(8,128)(2,1)S(1)}, u32[]{:S(2)}, u32[]{:S(2)}) collective-permute-start(bf16[2,64,2048]{2,1,0:T(8,128)(2,1)} %join_pair.2.own), channel_id=1, source_target_pairs={{0,4},{4,0},{1,5},{5,1},{2,6},{6,2},{3,7},{7,3},{8,12},{12,8},{9,1... | collective-permute-start | bytes 1572872 | tf_op jit(solution)/shard_map/ppermute | solution.py:285
  29.7 19.9 %collective-permute-start.10 = (bf16[4,64,1536]{2,1,0:T(8,128)(2,1)}, bf16[4,64,1536]{2,1,0:T(8,128)(2,1)}, u32[]{:S(2)}, u32[]{:S(2)}) collective-permute-start(bf16[4,64,1536]{2,1,0:T(8,128)(2,1)} %join_column.3.refs_0_), channel_id=1, source_target_pairs={{1,0},{5,1},{4,5},{0,4},{3,2},{7,3},{6,7},{2,6},{9,8},{13,9},{12,1... | collective-permute-start | bytes 2359304 | tf_op jit(solution)/shard_map/ppermute | solution.py:285
  31.1 17.4 %collective-permute-start.8 = (bf16[4,64,1536]{2,1,0:T(8,128)(2,1)}, bf16[4,64,1536]{2,1,0:T(8,128)(2,1)}, u32[]{:S(2)}, u32[]{:S(2)}) collective-permute-start(bf16[4,64,1536]{2,1,0:T(8,128)(2,1)} %join_column.3.refs_0_), channel_id=1, source_target_pairs={{0,1},{1,5},{5,4},{4,0},{2,3},{3,7},{7,6},{6,2},{8,9},{9,13},{13,1... | collective-permute-start | bytes 2359304 | tf_op jit(solution)/shard_map/ppermute | solution.py:285
  31.9 19.4 %collective-permute-start.4 = (bf16[64,2688]{1,0:T(8,128)(2,1)S(1)}, bf16[64,2688]{1,0:T(8,128)(2,1)S(1)}, u32[]{:S(2)}, u32[]{:S(2)}) collective-permute-start(bf16[64,2688]{1,0:T(8,128)(2,1)S(1)} %fusion.28.refs_0_), channel_id=1, source_target_pairs={{0,8},{8,0},{16,24},{24,16},{1,9},{9,1},{17,25},{25,17},{2,10},{10... | collective-permute-start | bytes 1032200 | tf_op jit(solution)/shard_map/ppermute | solution.py:285
  33.4 26.6 %collective-permute-start.5 = (bf16[64,2688]{1,0:T(8,128)(2,1)S(1)}, bf16[64,2688]{1,0:T(8,128)(2,1)S(1)}, u32[]{:S(2)}, u32[]{:S(2)}) collective-permute-start(bf16[64,2688]{1,0:T(8,128)(2,1)S(1)} %fusion.28.refs_0_), channel_id=1, source_target_pairs={{0,16},{8,24},{16,0},{24,8},{1,17},{9,25},{17,1},{25,9},{2,18},{10... | collective-permute-start | bytes 1032200 | tf_op jit(solution)/shard_map/ppermute | solution.py:285
  36.0 24.1 %collective-permute-start.6 = (bf16[64,2688]{1,0:T(8,128)(2,1)S(1)}, bf16[64,2688]{1,0:T(8,128)(2,1)S(1)}, u32[]{:S(2)}, u32[]{:S(2)}) collective-permute-start(bf16[64,2688]{1,0:T(8,128)(2,1)S(1)} %fusion.28.refs_0_), channel_id=1, source_target_pairs={{0,24},{8,16},{16,8},{24,0},{1,25},{9,17},{17,9},{25,1},{2,26},{10... | collective-permute-start | bytes 1032200 | tf_op jit(solution)/shard_map/ppermute | solution.py:285
  48.5 19.0 %collective-permute-start.12 = (bf16[4,64,1536]{2,1,0:T(8,128)(2,1)S(1)}, bf16[4,64,1536]{2,1,0:T(8,128)(2,1)}, u32[]{:S(2)}, u32[]{:S(2)}) collective-permute-start(bf16[4,64,1536]{2,1,0:T(8,128)(2,1)S(1)} %copy-done.26), channel_id=1, source_target_pairs={{0,2},{2,0},{1,3},{3,1},{4,6},{6,4},{5,7},{7,5},{8,10},{10,8},{9,1... | collective-permute-start | bytes 2359304 | tf_op jit(solution)/shard_map/ppermute | solution.py:285
  49.6 11.6 %collective-permute-start.9 = (bf16[2,64,1536]{2,1,0:T(8,128)(2,1)S(1)}, bf16[2,64,1536]{2,1,0:T(8,128)(2,1)S(1)}, u32[]{:S(2)}, u32[]{:S(2)}) collective-permute-start(bf16[2,64,1536]{2,1,0:T(8,128)(2,1)S(1)} %slice.166), channel_id=1, source_target_pairs={{0,1},{1,5},{5,4},{4,0},{2,3},{3,7},{7,6},{6,2},{8,9},{9,13},{13,1... | collective-permute-start | bytes 1179656 | tf_op jit(solution)/shard_map/ppermute | solution.py:285
  51.3 11.4 %collective-permute-start.11 = (bf16[2,64,1536]{2,1,0:T(8,128)(2,1)S(1)}, bf16[2,64,1536]{2,1,0:T(8,128)(2,1)}, u32[]{:S(2)}, u32[]{:S(2)}) collective-permute-start(bf16[2,64,1536]{2,1,0:T(8,128)(2,1)S(1)} %slice.167), channel_id=1, source_target_pairs={{1,0},{5,1},{4,5},{0,4},{3,2},{7,3},{6,7},{2,6},{9,8},{13,9},{12,1... | collective-permute-start | bytes 1179656 | tf_op jit(solution)/shard_map/ppermute | solution.py:285
  60.1 9.5 %collective-permute-start.13 = (bf16[4,64,1536]{2,1,0:T(8,128)(2,1)}, bf16[4,64,1536]{2,1,0:T(8,128)(2,1)}, u32[]{:S(2)}, u32[]{:S(2)}) collective-permute-start(bf16[4,64,1536]{2,1,0:T(8,128)(2,1)} %collective-permute-done.8.refs_1_), channel_id=1, source_target_pairs={{0,2},{2,0},{1,3},{3,1},{4,6},{6,4},{5,7},{7,5},{8,10},{10,8},{9,1... | collective-permute-start | bytes 2359304 | tf_op jit(solution)/shard_map/ppermute | solution.py:285
  60.1 13.0 %collective-permute-start.14 = (bf16[4,64,1536]{2,1,0:T(8,128)(2,1)}, bf16[4,64,1536]{2,1,0:T(8,128)(2,1)}, u32[]{:S(2)}, u32[]{:S(2)}) collective-permute-start(bf16[4,64,1536]{2,1,0:T(8,128)(2,1)} %collective-permute-done.10.refs_2_), channel_id=1, source_target_pairs={{0,2},{2,0},{1,3},{3,1},{4,6},{6,4},{5,7},{7,5},{8,10},{10,8},{9,1... | collective-permute-start | bytes 2359304 | tf_op jit(solution)/shard_map/ppermute | solution.py:285
  61.2 8.1 %collective-permute-start.15 = (bf16[2,64,1536]{2,1,0:T(8,128)(2,1)S(1)}, bf16[2,64,1536]{2,1,0:T(8,128)(2,1)}, u32[]{:S(2)}, u32[]{:S(2)}) collective-permute-start(bf16[2,64,1536]{2,1,0:T(8,128)(2,1)S(1)} %collective-permute-done.9.refs_3_), channel_id=1, source_target_pairs={{0,2},{2,0},{1,3},{3,1},{4,6},{6,4},{5,7},{7,5},{8,10},{10,8},{9,1... | collective-permute-start | bytes 1179656 | tf_op jit(solution)/shard_map/ppermute | solution.py:285
  62.7 6.9 %collective-permute-start.16 = (bf16[2,64,1536]{2,1,0:T(8,128)(2,1)}, bf16[2,64,1536]{2,1,0:T(8,128)(2,1)}, u32[]{:S(2)}, u32[]{:S(2)}) collective-permute-start(bf16[2,64,1536]{2,1,0:T(8,128)(2,1)} %collective-permute-done.11.refs_4_), channel_id=1, source_target_pairs={{0,2},{2,0},{1,3},{3,1},{4,6},{6,4},{5,7},{7,5},{8,10},{10,8},{9,1... | collective-permute-start | bytes 1179656 | tf_op jit(solution)/shard_map/ppermute | solution.py:285
  67.5 32.6 %collective-permute-start.18 = (bf16[4,64,2688]{2,1,0:T(8,128)(2,1)S(1)}, bf16[4,64,2688]{2,1,0:T(8,128)(2,1)S(1)}, u32[]{:S(2)}, u32[]{:S(2)}) collective-permute-start(bf16[4,64,2688]{2,1,0:T(8,128)(2,1)S(1)} %copy-done.5), channel_id=1, source_target_pairs={{0,1},{1,5},{5,4},{4,0},{2,3},{3,7},{7,6},{6,2},{8,9},{9,13},{13,1... | collective-permute-start | bytes 4128776 | tf_op jit(solution)/shard_map/ppermute | solution.py:285
  69.2 32.4 %collective-permute-start.19 = (bf16[4,64,2688]{2,1,0:T(8,128)(2,1)S(1)}, bf16[4,64,2688]{2,1,0:T(8,128)(2,1)}, u32[]{:S(2)}, u32[]{:S(2)}) collective-permute-start(bf16[4,64,2688]{2,1,0:T(8,128)(2,1)S(1)} %copy-done.5), channel_id=1, source_target_pairs={{1,0},{5,1},{4,5},{0,4},{3,2},{7,3},{6,7},{2,6},{9,8},{13,9},{12,1... | collective-permute-start | bytes 4128776 | tf_op jit(solution)/shard_map/ppermute | solution.py:285
  69.6 51.8 %collective-permute-start.22 = (bf16[4,64,2688]{2,1,0:T(8,128)(2,1)S(1)}, bf16[4,64,2688]{2,1,0:T(8,128)(2,1)}, u32[]{:S(2)}, u32[]{:S(2)}) collective-permute-start(bf16[4,64,2688]{2,1,0:T(8,128)(2,1)S(1)} %copy-done.5), channel_id=1, source_target_pairs={{0,2},{2,0},{1,3},{3,1},{4,6},{6,4},{5,7},{7,5},{8,10},{10,8},{9,1... | collective-permute-start | bytes 4128776 | tf_op jit(solution)/shard_map/ppermute | solution.py:285
  69.6 50.2 %collective-permute-start.17 = (bf16[2,2,64,2048]{3,2,1,0:T(8,128)(2,1)}, bf16[2,2,64,2048]{3,2,1,0:T(8,128)(2,1)}, u32[]{:S(2)}, u32[]{:S(2)}) collective-permute-start(bf16[2,2,64,2048]{3,2,1,0:T(8,128)(2,1)} %join_pair.3.refs_0_), channel_id=1, source_target_pairs={{0,16},{8,24},{16,0},{24,8},{1,17},{9,25},{17,1},{25,9},{2,18},{10... | collective-permute-start | bytes 3145736 | tf_op jit(solution)/shard_map/ppermute | solution.py:285
  73.1 46.8 %collective-permute-start.27 = (bf16[2,2,64,2048]{3,2,1,0:T(8,128)(2,1)}, bf16[2,2,64,2048]{3,2,1,0:T(8,128)(2,1)}, u32[]{:S(2)}, u32[]{:S(2)}) collective-permute-start(bf16[2,2,64,2048]{3,2,1,0:T(8,128)(2,1)} %join_pair.3.refs_0_), channel_id=1, source_target_pairs={{0,8},{8,0},{16,24},{24,16},{1,9},{9,1},{17,25},{25,17},{2,10},{10... | collective-permute-start | bytes 3145736 | tf_op jit(solution)/shard_map/ppermute | solution.py:285
  101.7 18.6 %collective-permute-start.20 = (bf16[2,64,2688]{2,1,0:T(8,128)(2,1)S(1)}, bf16[2,64,2688]{2,1,0:T(8,128)(2,1)S(1)}, u32[]{:S(2)}, u32[]{:S(2)}) collective-permute-start(bf16[2,64,2688]{2,1,0:T(8,128)(2,1)S(1)} %slice.129), channel_id=1, source_target_pairs={{0,1},{1,5},{5,4},{4,0},{2,3},{3,7},{7,6},{6,2},{8,9},{9,13},{13,1... | collective-permute-start | bytes 2064392 | tf_op jit(solution)/shard_map/ppermute | solution.py:285
  104.4 17.0 %collective-permute-start.21 = (bf16[2,64,2688]{2,1,0:T(8,128)(2,1)S(1)}, bf16[2,64,2688]{2,1,0:T(8,128)(2,1)S(1)}, u32[]{:S(2)}, u32[]{:S(2)}) collective-permute-start(bf16[2,64,2688]{2,1,0:T(8,128)(2,1)S(1)} %slice.130), channel_id=1, source_target_pairs={{1,0},{5,1},{4,5},{0,4},{3,2},{7,3},{6,7},{2,6},{9,8},{13,9},{12,1... | collective-permute-start | bytes 2064392 | tf_op jit(solution)/shard_map/ppermute | solution.py:285
  119.8 7.1 %collective-permute-start.23 = (bf16[4,64,2688]{2,1,0:T(8,128)(2,1)S(1)}, bf16[4,64,2688]{2,1,0:T(8,128)(2,1)S(1)}, u32[]{:S(2)}, u32[]{:S(2)}) collective-permute-start(bf16[4,64,2688]{2,1,0:T(8,128)(2,1)S(1)} %collective-permute-done.18.refs_1_.refs_9_), channel_id=1, source_target_pairs={{0,2},{2,0},{1,3},{3,1},{4,6},{6,4},{5,7},{7,5},{8,10},{10,8},{9,1... | collective-permute-start | bytes 4128776 | tf_op jit(solution)/shard_map/ppermute | solution.py:285
  120.0 8.2 %collective-permute-start.24 = (bf16[4,64,2688]{2,1,0:T(8,128)(2,1)}, bf16[4,64,2688]{2,1,0:T(8,128)(2,1)}, u32[]{:S(2)}, u32[]{:S(2)}) collective-permute-start(bf16[4,64,2688]{2,1,0:T(8,128)(2,1)} %collective-permute-done.19.refs_2_.refs_10_), channel_id=1, source_target_pairs={{0,2},{2,0},{1,3},{3,1},{4,6},{6,4},{5,7},{7,5},{8,10},{10,8},{9,1... | collective-permute-start | bytes 4128776 | tf_op jit(solution)/shard_map/ppermute | solution.py:285
  120.3 4.6 %collective-permute-start.25 = (bf16[2,64,2688]{2,1,0:T(8,128)(2,1)S(1)}, bf16[2,64,2688]{2,1,0:T(8,128)(2,1)S(1)}, u32[]{:S(2)}, u32[]{:S(2)}) collective-permute-start(bf16[2,64,2688]{2,1,0:T(8,128)(2,1)S(1)} %collective-permute-done.20.refs_3_.refs_11_), channel_id=1, source_target_pairs={{0,2},{2,0},{1,3},{3,1},{4,6},{6,4},{5,7},{7,5},{8,10},{10,8},{9,1... | collective-permute-start | bytes 2064392 | tf_op jit(solution)/shard_map/ppermute | solution.py:285
  121.4 5.5 %collective-permute-start.26 = (bf16[2,64,2688]{2,1,0:T(8,128)(2,1)S(1)}, bf16[2,64,2688]{2,1,0:T(8,128)(2,1)S(1)}, u32[]{:S(2)}, u32[]{:S(2)}) collective-permute-start(bf16[2,64,2688]{2,1,0:T(8,128)(2,1)S(1)} %collective-permute-done.21.refs_4_.refs_12_), channel_id=1, source_target_pairs={{0,2},{2,0},{1,3},{3,1},{4,6},{6,4},{5,7},{7,5},{8,10},{10,8},{9,1... | collective-permute-start | bytes 2064392 | tf_op jit(solution)/shard_map/ppermute | solution.py:285
  121.4 31.0 %collective-permute-start.29 = (bf16[2,2,64,2048]{3,2,1,0:T(8,128)(2,1)S(1)}, bf16[2,2,64,2048]{3,2,1,0:T(8,128)(2,1)S(1)}, u32[]{:S(2)}, u32[]{:S(2)}) collective-permute-start(bf16[2,2,64,2048]{3,2,1,0:T(8,128)(2,1)S(1)} %copy-done.23), channel_id=1, source_target_pairs={{0,2},{2,0},{1,3},{3,1},{4,6},{6,4},{5,7},{7,5},{8,10},{10,8},{9,1... | collective-permute-start | bytes 3145736 | tf_op jit(solution)/shard_map/ppermute | solution.py:285
  124.9 27.5 %collective-permute-start.30 = (bf16[2,2,64,2048]{3,2,1,0:T(8,128)(2,1)}, bf16[2,2,64,2048]{3,2,1,0:T(8,128)(2,1)}, u32[]{:S(2)}, u32[]{:S(2)}) collective-permute-start(bf16[2,2,64,2048]{3,2,1,0:T(8,128)(2,1)} %collective-permute-done.27.refs_1_), channel_id=1, source_target_pairs={{0,2},{2,0},{1,3},{3,1},{4,6},{6,4},{5,7},{7,5},{8,10},{10,8},{9,1... | collective-permute-start | bytes 3145736 | tf_op jit(solution)/shard_map/ppermute | solution.py:285
  126.9 25.5 %collective-permute-start.28 = (bf16[2,2,64,2048]{3,2,1,0:T(8,128)(2,1)}, bf16[2,2,64,2048]{3,2,1,0:T(8,128)(2,1)}, u32[]{:S(2)}, u32[]{:S(2)}) collective-permute-start(bf16[2,2,64,2048]{3,2,1,0:T(8,128)(2,1)} %collective-permute-done.17.refs_2_), channel_id=1, source_target_pairs={{0,8},{8,0},{16,24},{24,16},{1,9},{9,1},{17,25},{25,17},{2,10},{10... | collective-permute-start | bytes 3145736 | tf_op jit(solution)/shard_map/ppermute | solution.py:285
  128.0 24.4 %collective-permute-start.31 = (bf16[2,2,64,2048]{3,2,1,0:T(8,128)(2,1)}, bf16[2,2,64,2048]{3,2,1,0:T(8,128)(2,1)}, u32[]{:S(2)}, u32[]{:S(2)}) collective-permute-start(bf16[2,2,64,2048]{3,2,1,0:T(8,128)(2,1)} %collective-permute-done.17.refs_2_), channel_id=1, source_target_pairs={{0,2},{2,0},{1,3},{3,1},{4,6},{6,4},{5,7},{7,5},{8,10},{10,8},{9,1... | collective-permute-start | bytes 3145736 | tf_op jit(solution)/shard_map/ppermute | solution.py:285
  152.4 2.9 collective-permute-start.32
  187.7 7.5 %collective-permute-start.34 = (bf16[4,2,2,64,2048]{4,3,2,1,0:T(8,128)(2,1)}, bf16[4,2,2,64,2048]{4,3,2,1,0:T(8,128)(2,1)}, u32[]{:S(2)}, u32[]{:S(2)}) collective-permute-start(bf16[4,2,2,64,2048]{4,3,2,1,0:T(8,128)(2,1)} %get-tuple-element.122), channel_id=1, source_target_pairs={{0,2},{2,0},{1,3},{3,1},{4,6},{6,4},{5,7},{7,5},{8,10},{10,8},{9,1... | collective-permute-start | bytes 12582920 | tf_op jit(solution)/shard_map/ppermute | solution.py:285
  187.9 43.4 %collective-permute-start.33 = (bf16[532,1024]{1,0:T(8,128)(2,1)S(1)}, bf16[532,1024]{1,0:T(8,128)(2,1)S(1)}, u32[]{:S(2)}, u32[]{:S(2)}) collective-permute-start(bf16[532,1024]{1,0:T(8,128)(2,1)S(1)} %slice.131.own_ref), channel_id=1, source_target_pairs={{0,1},{1,0},{2,3},{3,2},{4,5},{5,4},{6,7},{7,6},{8,9},{9,8},{10,11... | collective-permute-start | bytes 3268616 | tf_op jit(solution)/shard_map/ppermute | solution.py:285
  199.6 31.7 %collective-permute-start.36 = (bf16[2,2,64,2048]{3,2,1,0:T(8,128)(2,1)}, bf16[2,2,64,2048]{3,2,1,0:T(8,128)(2,1)S(1)}, u32[]{:S(2)}, u32[]{:S(2)}) collective-permute-start(bf16[2,2,64,2048]{3,2,1,0:T(8,128)(2,1)} %get-tuple-element.291), channel_id=1, source_target_pairs={{0,8},{8,0},{16,24},{24,16},{1,9},{9,1},{17,25},{25,17},{2,10},{10... | collective-permute-start | bytes 3145736 | tf_op jit(solution)/shard_map/ppermute | solution.py:285
  240.9 9.4 %collective-permute-start.37 = (bf16[2,2,4,64,2688]{4,3,2,1,0:T(8,128)(2,1)}, bf16[2,2,4,64,2688]{4,3,2,1,0:T(8,128)(2,1)}, u32[]{:S(2)}, u32[]{:S(2)}) collective-permute-start(bf16[2,2,4,64,2688]{4,3,2,1,0:T(8,128)(2,1)} %get-tuple-element.137), channel_id=1, source_target_pairs={{0,2},{2,0},{1,3},{3,1},{4,6},{6,4},{5,7},{7,5},{8,10},{10,8},{9,1... | collective-permute-start | bytes 16515080 | tf_op jit(solution)/shard_map/ppermute | solution.py:285
  241.1 48.6 %collective-permute-start.35 = (bf16[2,2,64,2048]{3,2,1,0:T(8,128)(2,1)}, bf16[2,2,64,2048]{3,2,1,0:T(8,128)(2,1)}, u32[]{:S(2)}, u32[]{:S(2)}) collective-permute-start(bf16[2,2,64,2048]{3,2,1,0:T(8,128)(2,1)} %get-tuple-element.290), channel_id=1, source_target_pairs={{0,8},{8,0},{16,24},{24,16},{1,9},{9,1},{17,25},{25,17},{2,10},{10... | collective-permute-start | bytes 3145736 | tf_op jit(solution)/shard_map/ppermute | solution.py:285
  242.9 46.8 %collective-permute-start.40 = (bf16[2,2,64,2048]{3,2,1,0:T(8,128)(2,1)}, bf16[2,2,64,2048]{3,2,1,0:T(8,128)(2,1)}, u32[]{:S(2)}, u32[]{:S(2)}) collective-permute-start(bf16[2,2,64,2048]{3,2,1,0:T(8,128)(2,1)} %fusion.1), channel_id=1, source_target_pairs={{0,16},{8,24},{16,0},{24,8},{1,17},{9,25},{17,1},{25,9},{2,18},{10... | collective-permute-start | bytes 3145736 | tf_op jit(solution)/shard_map/ppermute | solution.py:285
  255.9 27.4 %collective-permute-start.38 = (bf16[2,64,2688]{2,1,0:T(8,128)(2,1)}, bf16[2,64,2688]{2,1,0:T(8,128)(2,1)}, u32[]{:S(2)}, u32[]{:S(2)}) collective-permute-start(bf16[2,64,2688]{2,1,0:T(8,128)(2,1)} %get-tuple-element.303), channel_id=1, source_target_pairs={{0,1},{1,5},{5,4},{4,0},{2,3},{3,7},{7,6},{6,2},{8,9},{9,13},{13,1... | collective-permute-start | bytes 2064392 | tf_op jit(solution)/shard_map/ppermute | solution.py:285
  257.6 25.7 %collective-permute-start.39 = (bf16[2,64,2688]{2,1,0:T(8,128)(2,1)}, bf16[2,64,2688]{2,1,0:T(8,128)(2,1)}, u32[]{:S(2)}, u32[]{:S(2)}) collective-permute-start(bf16[2,64,2688]{2,1,0:T(8,128)(2,1)} %get-tuple-element.302), channel_id=1, source_target_pairs={{1,0},{5,1},{4,5},{0,4},{3,2},{7,3},{6,7},{2,6},{9,8},{13,9},{12,1... | collective-permute-start | bytes 2064392 | tf_op jit(solution)/shard_map/ppermute | solution.py:285
  286.2 32.0 %collective-permute-start.42 = (bf16[4,64,2688]{2,1,0:T(8,128)(2,1)}, bf16[4,64,2688]{2,1,0:T(8,128)(2,1)}, u32[]{:S(2)}, u32[]{:S(2)}) collective-permute-start(bf16[4,64,2688]{2,1,0:T(8,128)(2,1)} %pad_maximum_fusion.1), channel_id=1, source_target_pairs={{1,0},{5,1},{4,5},{0,4},{3,2},{7,3},{6,7},{2,6},{9,8},{13,9},{12,1... | collective-permute-start | bytes 4128776 | tf_op jit(solution)/shard_map/ppermute | solution.py:285
  289.2 31.4 %collective-permute-start.41 = (bf16[4,64,2688]{2,1,0:T(8,128)(2,1)S(1)}, bf16[4,64,2688]{2,1,0:T(8,128)(2,1)S(1)}, u32[]{:S(2)}, u32[]{:S(2)}) collective-permute-start(bf16[4,64,2688]{2,1,0:T(8,128)(2,1)S(1)} %pad_maximum_fusion), channel_id=1, source_target_pairs={{0,1},{1,5},{5,4},{4,0},{2,3},{3,7},{7,6},{6,2},{8,9},{9,13},{13,1... | collective-permute-start | bytes 4128776 | tf_op jit(solution)/shard_map/ppermute | solution.py:285
  320.7 11.1 %collective-permute-start.43 = (bf16[2,2,4,64,1536]{4,3,2,1,0:T(8,128)(2,1)}, bf16[2,2,4,64,1536]{4,3,2,1,0:T(8,128)(2,1)}, u32[]{:S(2)}, u32[]{:S(2)}) collective-permute-start(bf16[2,2,4,64,1536]{4,3,2,1,0:T(8,128)(2,1)} %get-tuple-element.151), channel_id=1, source_target_pairs={{0,2},{2,0},{1,3},{3,1},{4,6},{6,4},{5,7},{7,5},{8,10},{10,8},{9,1... | collective-permute-start | bytes 9437192 | tf_op jit(solution)/shard_map/ppermute | solution.py:285
  324.1 14.7 %collective-permute-start.48 = (bf16[272,1024]{1,0:T(8,128)(2,1)S(1)}, bf16[272,1024]{1,0:T(8,128)(2,1)S(1)}, u32[]{:S(2)}, u32[]{:S(2)}) collective-permute-start(bf16[272,1024]{1,0:T(8,128)(2,1)S(1)} %slice.150), channel_id=1, source_target_pairs={{0,1},{1,0},{2,3},{3,2},{4,5},{5,4},{6,7},{7,6},{8,9},{9,8},{10,11... | collective-permute-start | bytes 1671176 | tf_op jit(solution)/shard_map/ppermute | solution.py:285
  324.5 16.6 %collective-permute-start.47 = (bf16[2,64,2048]{2,1,0:T(8,128)(2,1)}, bf16[2,64,2048]{2,1,0:T(8,128)(2,1)S(1)}, u32[]{:S(2)}, u32[]{:S(2)}) collective-permute-start(bf16[2,64,2048]{2,1,0:T(8,128)(2,1)} %fusion.21), channel_id=1, source_target_pairs={{0,4},{4,0},{1,5},{5,1},{2,6},{6,2},{3,7},{7,3},{8,12},{12,8},{9,1... | collective-permute-start | bytes 1572872 | tf_op jit(solution)/shard_map/ppermute | solution.py:285
  329.6 11.5 %collective-permute-start.46 = (bf16[64,2688]{1,0:T(8,128)(2,1)S(1)}, bf16[64,2688]{1,0:T(8,128)(2,1)S(1)}, u32[]{:S(2)}, u32[]{:S(2)}) collective-permute-start(bf16[64,2688]{1,0:T(8,128)(2,1)S(1)} %get-tuple-element.296), channel_id=1, source_target_pairs={{0,8},{8,0},{16,24},{24,16},{1,9},{9,1},{17,25},{25,17},{2,10},{10... | collective-permute-start | bytes 1032200 | tf_op jit(solution)/shard_map/ppermute | solution.py:285
  331.4 22.5 %collective-permute-start.51 = (bf16[64,2688]{1,0:T(8,128)(2,1)S(1)}, bf16[64,2688]{1,0:T(8,128)(2,1)S(1)}, u32[]{:S(2)}, u32[]{:S(2)}) collective-permute-start(bf16[64,2688]{1,0:T(8,128)(2,1)S(1)} %get-tuple-element.295), channel_id=1, source_target_pairs={{0,8},{8,0},{16,24},{24,16},{1,9},{9,1},{17,25},{25,17},{2,10},{10... | collective-permute-start | bytes 1032200 | tf_op jit(solution)/shard_map/ppermute | solution.py:285
  334.1 12.6 %collective-permute-start.44 = (bf16[2,64,1536]{2,1,0:T(8,128)(2,1)S(1)}, bf16[2,64,1536]{2,1,0:T(8,128)(2,1)S(1)}, u32[]{:S(2)}, u32[]{:S(2)}) collective-permute-start(bf16[2,64,1536]{2,1,0:T(8,128)(2,1)S(1)} %get-tuple-element.305), channel_id=1, source_target_pairs={{0,1},{1,5},{5,4},{4,0},{2,3},{3,7},{7,6},{6,2},{8,9},{9,13},{13,1... | collective-permute-start | bytes 1179656 | tf_op jit(solution)/shard_map/ppermute | solution.py:285
  338.7 10.3 %collective-permute-start.45 = (bf16[2,64,1536]{2,1,0:T(8,128)(2,1)S(1)}, bf16[2,64,1536]{2,1,0:T(8,128)(2,1)S(1)}, u32[]{:S(2)}, u32[]{:S(2)}) collective-permute-start(bf16[2,64,1536]{2,1,0:T(8,128)(2,1)S(1)} %get-tuple-element.304), channel_id=1, source_target_pairs={{1,0},{5,1},{4,5},{0,4},{3,2},{7,3},{6,7},{2,6},{9,8},{13,9},{12,1... | collective-permute-start | bytes 1179656 | tf_op jit(solution)/shard_map/ppermute | solution.py:285
  341.2 17.0 %collective-permute-start.52 = (bf16[64,2688]{1,0:T(8,128)(2,1)S(1)}, bf16[64,2688]{1,0:T(8,128)(2,1)S(1)}, u32[]{:S(2)}, u32[]{:S(2)}) collective-permute-start(bf16[64,2688]{1,0:T(8,128)(2,1)S(1)} %fusion.17), channel_id=1, source_target_pairs={{0,16},{8,24},{16,0},{24,8},{1,17},{9,25},{17,1},{25,9},{2,18},{10... | collective-permute-start | bytes 1032200 | tf_op jit(solution)/shard_map/ppermute | solution.py:285
  350.1 20.1 %collective-permute-start.50 = (bf16[4,64,1536]{2,1,0:T(8,128)(2,1)}, bf16[4,64,1536]{2,1,0:T(8,128)(2,1)}, u32[]{:S(2)}, u32[]{:S(2)}) collective-permute-start(bf16[4,64,1536]{2,1,0:T(8,128)(2,1)} %pad_maximum_fusion.3), channel_id=1, source_target_pairs={{1,0},{5,1},{4,5},{0,4},{3,2},{7,3},{6,7},{2,6},{9,8},{13,9},{12,1... | collective-permute-start | bytes 2359304 | tf_op jit(solution)/shard_map/ppermute | solution.py:285
  352.7 17.5 %collective-permute-start.49 = (bf16[4,64,1536]{2,1,0:T(8,128)(2,1)}, bf16[4,64,1536]{2,1,0:T(8,128)(2,1)}, u32[]{:S(2)}, u32[]{:S(2)}) collective-permute-start(bf16[4,64,1536]{2,1,0:T(8,128)(2,1)} %pad_maximum_fusion.2), channel_id=1, source_target_pairs={{0,1},{1,5},{5,4},{4,0},{2,3},{3,7},{7,6},{6,2},{8,9},{9,13},{13,1... | collective-permute-start | bytes 2359304 | tf_op jit(solution)/shard_map/ppermute | solution.py:285
  373.3 9.6 %collective-permute-start.57 = (bf16[64,2048]{1,0:T(8,128)(2,1)}, bf16[64,2048]{1,0:T(8,128)(2,1)}, u32[]{:S(2)}, u32[]{:S(2)}) collective-permute-start(bf16[64,2048]{1,0:T(8,128)(2,1)} %fusion.31), channel_id=1, source_target_pairs={{0,1},{1,0},{2,3},{3,2},{4,5},{5,4},{6,7},{7,6},{8,9},{9,8},{10,11... | collective-permute-start | bytes 786440 | tf_op jit(solution)/shard_map/ppermute | solution.py:285
  374.1 15.5 %collective-permute-start.53 = (bf16[260,1024]{1,0:T(8,128)(2,1)}, bf16[260,1024]{1,0:T(8,128)(2,1)}, u32[]{:S(2)}, u32[]{:S(2)}) collective-permute-start(bf16[260,1024]{1,0:T(8,128)(2,1)} %slice.158), channel_id=1, source_target_pairs={{0,1},{1,0},{2,3},{3,2},{4,5},{5,4},{6,7},{7,6},{8,9},{9,8},{10,11... | collective-permute-start | bytes 1597448 | tf_op jit(solution)/shard_map/ppermute | solution.py:285
  378.0 13.6 %collective-permute-start.54 = (bf16[64,1536]{1,0:T(8,128)(2,1)}, bf16[64,1536]{1,0:T(8,128)(2,1)S(1)}, u32[]{:S(2)}, u32[]{:S(2)}) collective-permute-start(bf16[64,1536]{1,0:T(8,128)(2,1)} %get-tuple-element.301), channel_id=1, source_target_pairs={{0,8},{8,0},{16,24},{24,16},{1,9},{9,1},{17,25},{25,17},{2,10},{10... | collective-permute-start | bytes 589832 | tf_op jit(solution)/shard_map/ppermute | solution.py:285
  379.2 14.4 %collective-permute-start.55 = (bf16[64,1536]{1,0:T(8,128)(2,1)}, bf16[64,1536]{1,0:T(8,128)(2,1)S(1)}, u32[]{:S(2)}, u32[]{:S(2)}) collective-permute-start(bf16[64,1536]{1,0:T(8,128)(2,1)} %get-tuple-element.300), channel_id=1, source_target_pairs={{0,16},{8,24},{16,0},{24,8},{1,17},{9,25},{17,1},{25,9},{2,18},{10... | collective-permute-start | bytes 589832 | tf_op jit(solution)/shard_map/ppermute | solution.py:285
  380.9 12.7 %collective-permute-start.56 = (bf16[64,1536]{1,0:T(8,128)(2,1)}, bf16[64,1536]{1,0:T(8,128)(2,1)S(1)}, u32[]{:S(2)}, u32[]{:S(2)}) collective-permute-start(bf16[64,1536]{1,0:T(8,128)(2,1)} %get-tuple-element.299), channel_id=1, source_target_pairs={{0,24},{8,16},{16,8},{24,0},{1,25},{9,17},{17,9},{25,1},{2,26},{10... | collective-permute-start | bytes 589832 | tf_op jit(solution)/shard_map/ppermute | solution.py:285
  397.6 1.2 collective-permute-start.58
  398.8 3.6 collective-permute-start.59
  400.5 3.6 collective-permute-start.60
  400.6 4.5 %collective-permute-start.61 = (f32[8,128]{1,0:T(8,128)S(1)}, f32[8,128]{1,0:T(8,128)S(1)}, u32[]{:S(2)}, u32[]{:S(2)}) collective-permute-start(f32[8,128]{1,0:T(8,128)S(1)} %broadcast_add_fusion), channel_id=1, source_target_pairs={{0,5},{1,4},{4,1},{5,0},{2,7},{3,6},{6,3},{7,2},{8,13},{9,12},{12,... | collective-permute-start | bytes 12296 | tf_op jit(solution)/shard_map/ppermute | solution.py:285
  405.2 4.2 collective-permute-start.62
  409.4 9.0 %collective-permute-start.63 = (f32[8,128]{1,0:T(8,128)S(1)}, f32[8,128]{1,0:T(8,128)S(1)}, u32[]{:S(2)}, u32[]{:S(2)}) collective-permute-start(f32[8,128]{1,0:T(8,128)S(1)} %add.520), channel_id=1, source_target_pairs={{0,16},{8,24},{16,0},{24,8},{1,17},{9,25},{17,1},{25,9},{2,18},{10... | collective-permute-start | bytes 12296 | tf_op jit(solution)/shard_map/ppermute | solution.py:285
  (62 other events, 426.4 us)

commit v3 on v2

--- a/solution.py
+++ b/solution.py
@@ -523,7 +523,7 @@
     def step(i, held):
         return body(pl.ds(pl.multiple_of(i * ROWS_AT_ONCE, ROWS_AT_ONCE), ROWS_AT_ONCE), held)
 
-    return lax.fori_loop(0, total // ROWS_AT_ONCE, step, carry)
+    return lax.fori_loop(0, total // ROWS_AT_ONCE, step, carry, unroll=True)
 
 
 def normalize(v):
@@ -545,12 +545,8 @@
 
 
 def gelu_parts(u):
-    expo = jnp.exp(-0.5 * (u * u))
-    t = 1.0 / (1.0 + 0.3275911 * 0.7071067811865476 * jnp.abs(u))
-    poly = ((((1.061405429 * t - 1.453152027) * t + 1.421413741) * t - 0.284496736) * t + 0.254829592) * t
-    tail = 0.5 * poly * expo
-    phi = jnp.where(u < 0, tail, 1.0 - tail)
-    return u * phi, phi + u * expo * 0.3989422804014327
+    phi = 0.5 + 0.5 * lax.erf(u * math.sqrt(0.5))
+    return u * phi, phi + u * (jnp.exp(-0.5 * (u * u)) * (1.0 / math.sqrt(2.0 * math.pi)))
 
 
 def up_kernel(per_side, x_ref, ctx_ref, *refs):
@@ -1011,11 +1007,8 @@
     value = value + send(value, "c", SWAP)
     square = [send(value, ("x", "y"), tuple((i, i ^ k) for i in range(4))) for k in (1, 2, 3)]
     value = (value + square[0]) + (square[1] + square[2])
-    count, k = lax.axis_size("z"), 1
-    while k < count:
-        value = value + send(value, "z", tuple((i, i ^ k) for i in range(count)))
-        k *= 2
-    return value
+    column = [send(value, "z", partners(k)) for k in (1, 2, 3)]
+    return (value + column[0]) + (column[1] + column[2])
 
 
 def pad_rows(a, total):
@@ -1095,9 +1088,9 @@
     near_qkv = ring_near(column_qkv)
     far_qkv = ring_far(*near_qkv)
     w_qkv = both_cores((column_qkv,) + near_qkv + far_qkv)
-    column_second = after(join_column(z_second), *far_qkv)
+    column_second = after(join_column(after(tuple(z_second), square_down)), *far_qkv)
     near_second = ring_near(column_second)
-    square_down = after(square_down, column_second)
+    square_down = after(square_down, *z_second)
     down_one, down_two = send(square_down, "z", partners(1)), send(square_down, "z", partners(2))
 
     qkv = project(after(x, column_second), w_qkv, rows)
@@ -1155,10 +1148,8 @@
         columns,
     )
     crossed, shared_result = after(crossed, branch_grad), after(shared_result, branch_grad)
-    one, two = down_term(1).astype(LOW), (down_term(2) + crossed.astype(F32)).astype(LOW)
-    from_one, from_two = send(one, "z", partners(1)), send(two, "z", partners(2))
     own_second, other, context_grad = out_back(
-        after(branch_grad, one, two, shared_result),
+        after(branch_grad, crossed, shared_result),
         context,
         norm_one,
         norm_two,
@@ -1169,7 +1160,10 @@
         inner_part,
     )
     other_second = send(other, "c", SWAP)
-    take_second = chip_terms(own_second, other_second)
+    crossed = after(crossed, own_second)
+    one, two = down_term(1).astype(LOW), (down_term(2) + crossed.astype(F32)).astype(LOW)
+    from_one, from_two = send(one, "z", partners(1)), send(two, "z", partners(2))
+    take_second = chip_terms(own_second, after(other_second, one, two))
     far = far_terms(take_second)
     far_second = ring_pair(*far)
     grads = attention_back(qkv, bias, logs, after(context_grad, *far))

time: 438 us -> 428 us (0.977)
  Pallas kernels: 179 us -> 169 us
    pallas_call x1, Pallas kernels: 22.2 us -> 16.1 us  [up(): pl.pallas_call(functools.partial(up_kernel, per_side), grid=(2 * per_side...]
    ppermute x64 -> x65, starting transfers between devices: 66.9 us -> 69.4 us  [send(): return lax.ppermute(block, axes, list(pairs))]
    ppermute x64 -> x65, waiting for transfers between devices: 95.3 us -> 93.6 us  [send(): return lax.ppermute(block, axes, list(pairs))]
    unnamed x126 -> x128, local copies, waits for them, and re-layouts: 13 us -> 13.6 us
  transfers between devices with their start and end apart: 64 -> 65, of which waited for: 30 -> 31; matrix products, arithmetic and copies ran while one was open for 13% -> 14% of each run, Pallas kernels for 32% -> 31%
where the time goes in v3:
time: 428 us; the launch traced here: 420 us
  Pallas kernels  169 us (39%)
  waiting for transfers between devices  93.6 us (22%)
  starting transfers between devices  69.4 us (16%)
  other arithmetic  50 us (12%)
  local copies, waits for them, and re-layouts  30 us (7%)
  between operations  8.13 us (2%)
    ppermute x65, waiting for transfers between devices, send(): return lax.ppermute(block, axes, list(pairs))  93.6 us
    ppermute x65, starting transfers between devices, send(): return lax.ppermute(block, axes, list(pairs))  69.4 us
    pallas_call x1, Pallas kernels, inner_back(): pl.pallas_call(functools.partial(inner_kernel, chunks // 2, len(downs)),...  29.9 us
    pallas_call x1, Pallas kernels, attention_back(): pl.pallas_call(attend_back_kernel, grid=(pairs,), in_specs=pair_specs(tot...  25.2 us
    pallas_call x1, Pallas kernels, attention(): pl.pallas_call(attend_kernel, grid=(pairs,), in_specs=pair_specs(total, p...  18.1 us
    pallas_call x1, Pallas kernels, qkv_back(): pl.pallas_call(functools.partial(qkv_back_kernel, per_side), grid=(2 * pe...  17.2 us
    pallas_call x1, Pallas kernels, up(): pl.pallas_call(functools.partial(up_kernel, per_side), grid=(2 * per_side...  16.1 us
    pallas_call x1, Pallas kernels, down(): pl.pallas_call(functools.partial(down_kernel, chunks // 2, len(pieces)),...  15.5 us
  transfers between devices with their start and end apart: 65, of which 31 were waited for; matrix products, arithmetic and copies ran while one was open for 14% of the time, Pallas kernels for 31%

profile of v3, /device:TPU:0, one launch (start us, length us, event | category | flops | bytes accessed | tf_op | source)
XLA Modules:
  0.0 419.7 jit_solution(11715990565517701736)
XLA Ops:
  1.9 3.0 collective-permute-start
  6.1 1.6 collective-permute-start.1
  7.7 2.6 collective-permute-start.2
  12.5 1.8 join_pair.2.own
  22.8 2.1 collective-permute-done.2.refs_2_
  25.0 2.3 collective-permute-done.7.other
  27.3 2.3 join_column.3.refs_0_
  33.3 2.7 collective-permute-start.5
  36.3 12.2 %collective-permute-done.8.refs_1_ = bf16[4,64,1536]{2,1,0:T(8,128)(2,1)} collective-permute-done((bf16[4,64,1536]{2,1,0:T(8,128)(2,1)}, bf16[4,64,1536]{2,1,0:T(8,128)(2,1)}, u32[]{:S(2)}, u32[]{:S(2)}) %collective-permute-start.8) | collective-permute-done | bytes 786464 | tf_op jit(solution)/shard_map/ppermute | solution.py:285
  52.7 7.3 %collective-permute-done.5.refs_2_ = bf16[64,2688]{1,0:T(8,128)(2,1)S(1)} collective-permute-done((bf16[64,2688]{1,0:T(8,128)(2,1)S(1)}, bf16[64,2688]{1,0:T(8,128)(2,1)S(1)}, u32[]{:S(2)}, u32[]{:S(2)}) %collective-permute-start.5) | collective-permute-done | bytes 344096 | tf_op jit(solution)/shard_map/ppermute | solution.py:285
  62.5 2.4 join_pair.3.refs_0_
  64.9 2.4 join_column.2.refs_0_.refs_8_
  67.3 3.4 collective-permute-start.17
  71.7 1.7 collective-permute-start.18
  73.7 8.2 %project.1.q_ref.k_ref.v_ref = bf16[6,544,512]{2,1,0:T(8,128)(2,1)} custom-call(bf16[544,1024]{1,0:T(8,128)(2,1)} %pad.15.x_ref, bf16[4,64,1536]{2,1,0:T(8,128)(2,1)} %join_column.3.refs_0_, bf16[4,64,1536]{2,1,0:T(8,128)(2,1)} %collective-permute-done.8.refs_1_, bf16[4,64,1536]{2,1,0:T(8,128)(2,1)} %collective-permute-done.10.refs_2_, ...), custom_call_target="tpu_custom_call" | custom-call | flops 6600000000 | bytes 12000000 | tf_op jit(solution)/shard_map/project/pallas_call | solution.py:463
  81.9 18.1 %attention.1 = (bf16[544,1024]{1,0:T(8,128)(2,1)}, f32[544,1024]{1,0:T(8,128)}) custom-call(bf16[6,544,512]{2,1,0:T(8,128)(2,1)} %project.1.q_ref.k_ref.v_ref, bf16[6,544,512]{2,1,0:T(8,128)(2,1)} %project.1.q_ref.k_ref.v_ref, bf16[6,544,512]{2,1,0:T(8,128)(2,1)} %project.1.q_ref.k_ref.v_ref, bf16[544,544]{1,0:T(8,128)(2,1)} %select_convert_fusion.bias_ref), custom_call_target="tpu_custom_call" | custom-call | flops 18699999232 | bytes 34000000 | tf_op jit(solution)/shard_map/attention/pallas_call | solution.py:507
  100.1 3.7 collective-permute-done.18.refs_1_.refs_9_
  107.4 9.9 %collective-permute-done.17.refs_2_ = bf16[2,2,64,2048]{3,2,1,0:T(8,128)(2,1)} collective-permute-done((bf16[2,2,64,2048]{3,2,1,0:T(8,128)(2,1)}, bf16[2,2,64,2048]{3,2,1,0:T(8,128)(2,1)}, u32[]{:S(2)}, u32[]{:S(2)}) %collective-permute-start.17) | collective-permute-done | bytes 1048608 | tf_op jit(solution)/shard_map/ppermute | solution.py:285
  117.8 3.5 collective-permute-done.20.refs_3_.refs_11_
  127.1 16.1 %up.1 = (bf16[544,1024]{1,0:T(8,128)(2,1)}, f32[544,1024]{1,0:T(8,128)}, f32[544,128]{1,0:T(8,128)}, f32[8,1024]{1,0:T(8,128)}, bf16[8,544,512]{2,1,0:T(8,128)(2,1)}, /*index=5*/bf16[8,544,512]{2,1,0:T(8,128)(2,1)}) custom-call(bf16[544,1024]{1,0:T(8,128)(2,1)} %pad.15.x_ref, bf16[544,1024]{1,0:T(8,128)(2,1)} %get-tuple-element.123.ctx_ref, ...), custom_call_target="tpu_custom_call" | custom-call | flops 24199999488 | bytes 44000000 | tf_op jit(solution)/shard_map/up/pallas_call | solution.py:597
  143.2 7.4 %collective-permute-done.28.refs_3_ = bf16[2,2,64,2048]{3,2,1,0:T(8,128)(2,1)} collective-permute-done((bf16[2,2,64,2048]{3,2,1,0:T(8,128)(2,1)}, bf16[2,2,64,2048]{3,2,1,0:T(8,128)(2,1)}, u32[]{:S(2)}, u32[]{:S(2)}) %collective-permute-start.28) | collective-permute-done | bytes 1048608 | tf_op jit(solution)/shard_map/ppermute | solution.py:285
  150.6 2.8 collective-permute-done.32.refs_7_
  154.4 15.5 %down.1 = (bf16[544,1024]{1,0:T(8,128)(2,1)}, f32[544,1024]{1,0:T(8,128)}, bf16[544,1024]{1,0:T(8,128)(2,1)}, f32[8,1024]{1,0:T(8,128)}) custom-call(bf16[8,544,512]{2,1,0:T(8,128)(2,1)} %get-tuple-element.125.g_ref.b_ref, f32[544,1024]{1,0:T(8,128)} %get-tuple-element.126.n_ref, f32[8,1024]{1,0:T(8,128)} %get-tuple-element.127.norms_ref, ...), custom_call_target="tpu_custom_call" | custom-call | flops 18699999232 | bytes 34000000 | tf_op jit(solution)/shard_map/down/pallas_call | solution.py:660
  170.0 12.7 %down_grad.1 = (bf16[4,2,2,64,2048]{4,3,2,1,0:T(8,128)(2,1)}, bf16[4,2,2,64,2048]{4,3,2,1,0:T(8,128)(2,1)}) custom-call(bf16[544,1024]{1,0:T(8,128)(2,1)} %get-tuple-element.133.a_ref.f_ref, bf16[8,544,512]{2,1,0:T(8,128)(2,1)} %get-tuple-element.125.g_ref.b_ref), custom_call_target="tpu_custom_call" | custom-call | flops 9900000256 | bytes 18000000 | tf_op jit(solution)/shard_map/down_grad/pallas_call | solution.py:720
  182.9 2.0 collective-permute-start.33
  184.9 5.3 %collective-permute-done.34 = bf16[4,2,2,64,2048]{4,3,2,1,0:T(8,128)(2,1)} collective-permute-done((bf16[4,2,2,64,2048]{4,3,2,1,0:T(8,128)(2,1)}, bf16[4,2,2,64,2048]{4,3,2,1,0:T(8,128)(2,1)}, u32[]{:S(2)}, u32[]{:S(2)}) %collective-permute-start.34) | collective-permute-done | bytes 4194336 | tf_op jit(solution)/shard_map/ppermute | solution.py:285
  190.2 4.4 %fusion.9 = (bf16[2,2,64,2048]{3,2,1,0:T(8,128)(2,1)}, bf16[2,2,64,2048]{3,2,1,0:T(8,128)(2,1)}) fusion(bf16[4,2,2,64,2048]{4,3,2,1,0:T(8,128)(2,1)} %collective-permute-done.34, s32[]{:T(128)S(6)} %select_n.192, bf16[4,2,2,64,2048]{4,3,2,1,0:T(8,128)(2,1)} %get-tuple-element.131, s32[]{:T(128)S(6)} %select_n.190), kind=kLoop, calls=%fused_computation.33 | loop fusion | flops 4194304 | bytes 6291464 | tf_op jit(solution)/shard_map/convert_element_type | solution.py:1164
  195.5 29.9 %inner_back.1 = (bf16[2,2,4,64,2688]{4,3,2,1,0:T(8,128)(2,1)}, bf16[2,2,4,64,2688]{4,3,2,1,0:T(8,128)(2,1)}, f32[544,1024]{1,0:T(8,128)}, bf16[544,1024]{1,0:T(8,128)(2,1)}, f32[8,1024]{1,0:T(8,128)}) custom-call(bf16[544,1024]{1,0:T(8,128)(2,1)} %get-tuple-element.133.a_ref.f_ref, bf16[8,544,512]{2,1,0:T(8,128)(2,1)} %get-tuple-element.134.d_ref, ...), custom_call_target="tpu_custom_call" | custom-call | flops 35200000000 | bytes 64000000 | tf_op jit(solution)/shard_map/inner_back/pallas_call | solution.py:778
  225.4 6.5 %out_back.1 = (bf16[2,2,4,64,2688]{4,3,2,1,0:T(8,128)(2,1)}, bf16[2,2,4,64,2688]{4,3,2,1,0:T(8,128)(2,1)}, bf16[544,1024]{1,0:T(8,128)(2,1)}) custom-call(bf16[544,1024]{1,0:T(8,128)(2,1)} %get-tuple-element.141.a_ref, bf16[544,1024]{1,0:T(8,128)(2,1)} %get-tuple-element.123.ctx_ref, ...), custom_call_target="tpu_custom_call", output_to_operand_aliasing={{0}: (4, {}), {1}: (5, {})} | custom-call | flops 4400000000 | bytes 8000000 | tf_op jit(solution)/shard_map/out_back/pallas_call | solution.py:832
  233.4 3.1 fusion.1
  236.5 3.0 collective-permute-start.40
  239.4 2.0 collective-permute-done.37
  241.4 4.3 %convert_add_fusion = (f32[1,1,4,64,2688]{4,3,2,1,0:T(8,128)S(1)}, bf16[1,1,4,64,2688]{4,3,2,1,0:T(8,128)(2,1)S(1)}, f32[1,1,4,64,2688]{4,3,2,1,0:T(8,128)S(1)}) fusion(bf16[2,2,4,64,2688]{4,3,2,1,0:T(8,128)(2,1)} %collective-permute-done.37, s32[]{:T(128)S(6)} %select_n.209, s32[]{:T(128)S(6)} %select_n.212, ...), kind=kLoop, calls=%fused_computation.3 | loop fusion | flops 6881280 | bytes 15138840 | tf_op jit(solution)/shard_map/add | solution.py:957
  247.0 2.0 collective-permute-start.38
  249.1 25.2 %attention_back.1.g_ref = bf16[3,544,1024]{2,1,0:T(8,128)(2,1)} custom-call(bf16[6,544,512]{2,1,0:T(8,128)(2,1)} %project.1.q_ref.k_ref.v_ref, bf16[6,544,512]{2,1,0:T(8,128)(2,1)} %project.1.q_ref.k_ref.v_ref, bf16[6,544,512]{2,1,0:T(8,128)(2,1)} %project.1.q_ref.k_ref.v_ref, bf16[544,544]{1,0:T(8,128)(2,1)} %select_convert_fusion.bias_ref, ...), custom_call_target="tpu_custom_call" | custom-call | flops 27499999232 | bytes 50000000 | tf_op jit(solution)/shard_map/attention_back/pallas_call | solution.py:894
  274.5 1.6 fusion.5
  280.9 4.8 %collective-permute-done.40 = bf16[2,2,64,2048]{3,2,1,0:T(8,128)(2,1)} collective-permute-done((bf16[2,2,64,2048]{3,2,1,0:T(8,128)(2,1)}, bf16[2,2,64,2048]{3,2,1,0:T(8,128)(2,1)}, u32[]{:S(2)}, u32[]{:S(2)}) %collective-permute-start.40) | collective-permute-done | bytes 1048608 | tf_op jit(solution)/shard_map/ppermute | solution.py:285
  285.6 2.9 fusion.2
  290.7 17.2 %qkv_back.1 = (bf16[2,2,4,64,1536]{4,3,2,1,0:T(8,128)(2,1)}, bf16[2,2,4,64,1536]{4,3,2,1,0:T(8,128)(2,1)}, bf16[544,1024]{1,0:T(8,128)(2,1)}) custom-call(bf16[544,1024]{1,0:T(8,128)(2,1)} %pad.15.x_ref, bf16[3,544,1024]{2,1,0:T(8,128)(2,1)} %attention_back.1.g_ref, f32[544,1024]{1,0:T(8,128)} %get-tuple-element.158.r_ref, ...), custom_call_target="tpu_custom_call" | custom-call | flops 17600000000 | bytes 32000000 | tf_op jit(solution)/shard_map/qkv_back/pallas_call | solution.py:937
  307.9 1.8 collective-permute-done.42
  309.6 2.2 collective-permute-done.41
  313.3 1.9 slice.158
  315.9 1.7 collective-permute-start.47
  317.6 3.4 fusion
  323.2 2.3 convert_add_fusion.2
  327.0 2.9 collective-permute-done.48
  329.9 2.6 collective-permute-start.45
  332.5 3.4 collective-permute-start.52
  338.2 2.0 collective-permute-done.45
  341.3 1.7 collective-permute-start.50
  345.1 4.7 %collective-permute-done.52 = bf16[64,2688]{1,0:T(8,128)(2,1)S(1)} collective-permute-done((bf16[64,2688]{1,0:T(8,128)(2,1)S(1)}, bf16[64,2688]{1,0:T(8,128)(2,1)S(1)}, u32[]{:S(2)}, u32[]{:S(2)}) %collective-permute-start.52) | collective-permute-done | bytes 344096 | tf_op jit(solution)/shard_map/ppermute | solution.py:285
  350.5 10.1 %final_rows.1 = bf16[532,2,1024]{2,1,0:T(2,128)(2,1)} custom-call(bf16[532,1024]{1,0:T(8,128)(2,1)} %copy-done.5, bf16[532,1024]{1,0:T(8,128)(2,1)} %copy-done.21), custom_call_target="tpu_custom_call" | custom-call | tf_op jit(solution)/shard_map/final_rows/pallas_call | solution.py:878
  361.8 2.2 fusion.3
  365.2 1.7 collective-permute-start.53
  370.5 1.9 collective-permute-start.55
  374.4 2.6 multiply_reduce_fusion
  377.0 3.7 collective-permute-done.53
  380.7 1.9 constant_dynamic-update-slice_fusion
  382.6 2.3 collective-permute-done.55
  392.0 1.8 collective-permute-start.61
  396.5 2.6 collective-permute-start.62
  402.3 5.4 %copy.79 = f32[2,532,1024]{2,0,1:T(2,128)} copy(f32[2,532,1024]{2,1,0:T(8,128)S(1)} %convert_bitcast_fusion) | data formatting | bytes 8716288
  410.9 3.2 multiply_add_fusion
  414.2 1.6 multiply_add_fusion.1
  (288 shorter events, 80.0 us)
Async XLA Ops:
  1.9 9.9 %collective-permute-start = (bf16[64,2048]{1,0:T(8,128)(2,1)S(1)}, bf16[64,2048]{1,0:T(8,128)(2,1)S(1)}, u32[]{:S(2)}, u32[]{:S(2)}) collective-permute-start(bf16[64,2048]{1,0:T(8,128)(2,1)S(1)} %convert_bitcast_fusion.1.own), channel_id=1, source_target_pairs={{0,1},{1,0},{2,3},{3,2},{4,5},{5,4},{6,7},{7,6},{8,9},{9,8},{10,11... | collective-permute-start | bytes 786440 | tf_op jit(solution)/shard_map/ppermute | solution.py:285
  6.1 16.8 %collective-permute-start.1 = (bf16[64,1536]{1,0:T(8,128)(2,1)S(1)}, bf16[64,1536]{1,0:T(8,128)(2,1)S(1)}, u32[]{:S(2)}, u32[]{:S(2)}) collective-permute-start(bf16[64,1536]{1,0:T(8,128)(2,1)S(1)} %pad_maximum_fusion.4.refs_0_), channel_id=1, source_target_pairs={{0,8},{8,0},{16,24},{24,16},{1,9},{9,1},{17,25},{25,17},{2,10},{10... | collective-permute-start | bytes 589832 | tf_op jit(solution)/shard_map/ppermute | solution.py:285
  7.7 17.3 %collective-permute-start.2 = (bf16[64,1536]{1,0:T(8,128)(2,1)S(1)}, bf16[64,1536]{1,0:T(8,128)(2,1)}, u32[]{:S(2)}, u32[]{:S(2)}) collective-permute-start(bf16[64,1536]{1,0:T(8,128)(2,1)S(1)} %pad_maximum_fusion.4.refs_0_), channel_id=1, source_target_pairs={{0,16},{8,24},{16,0},{24,8},{1,17},{9,25},{17,1},{25,9},{2,18},{10... | collective-permute-start | bytes 589832 | tf_op jit(solution)/shard_map/ppermute | solution.py:285
  10.3 14.7 %collective-permute-start.3 = (bf16[64,1536]{1,0:T(8,128)(2,1)S(1)}, bf16[64,1536]{1,0:T(8,128)(2,1)}, u32[]{:S(2)}, u32[]{:S(2)}) collective-permute-start(bf16[64,1536]{1,0:T(8,128)(2,1)S(1)} %pad_maximum_fusion.4.refs_0_), channel_id=1, source_target_pairs={{0,24},{8,16},{16,8},{24,0},{1,25},{9,17},{17,9},{25,1},{2,26},{10... | collective-permute-start | bytes 589832 | tf_op jit(solution)/shard_map/ppermute | solution.py:285
  14.4 12.9 %collective-permute-start.7 = (bf16[2,64,2048]{2,1,0:T(8,128)(2,1)}, bf16[2,64,2048]{2,1,0:T(8,128)(2,1)S(1)}, u32[]{:S(2)}, u32[]{:S(2)}) collective-permute-start(bf16[2,64,2048]{2,1,0:T(8,128)(2,1)} %join_pair.2.own), channel_id=1, source_target_pairs={{0,4},{4,0},{1,5},{5,1},{2,6},{6,2},{3,7},{7,3},{8,12},{12,8},{9,1... | collective-permute-start | bytes 1572872 | tf_op jit(solution)/shard_map/ppermute | solution.py:285
  29.6 19.9 %collective-permute-start.10 = (bf16[4,64,1536]{2,1,0:T(8,128)(2,1)}, bf16[4,64,1536]{2,1,0:T(8,128)(2,1)}, u32[]{:S(2)}, u32[]{:S(2)}) collective-permute-start(bf16[4,64,1536]{2,1,0:T(8,128)(2,1)} %join_column.3.refs_0_), channel_id=1, source_target_pairs={{1,0},{5,1},{4,5},{0,4},{3,2},{7,3},{6,7},{2,6},{9,8},{13,9},{12,1... | collective-permute-start | bytes 2359304 | tf_op jit(solution)/shard_map/ppermute | solution.py:285
  31.1 17.3 %collective-permute-start.8 = (bf16[4,64,1536]{2,1,0:T(8,128)(2,1)}, bf16[4,64,1536]{2,1,0:T(8,128)(2,1)}, u32[]{:S(2)}, u32[]{:S(2)}) collective-permute-start(bf16[4,64,1536]{2,1,0:T(8,128)(2,1)} %join_column.3.refs_0_), channel_id=1, source_target_pairs={{0,1},{1,5},{5,4},{4,0},{2,3},{3,7},{7,6},{6,2},{8,9},{9,13},{13,1... | collective-permute-start | bytes 2359304 | tf_op jit(solution)/shard_map/ppermute | solution.py:285
  31.8 19.3 %collective-permute-start.4 = (bf16[64,2688]{1,0:T(8,128)(2,1)S(1)}, bf16[64,2688]{1,0:T(8,128)(2,1)S(1)}, u32[]{:S(2)}, u32[]{:S(2)}) collective-permute-start(bf16[64,2688]{1,0:T(8,128)(2,1)S(1)} %fusion.28.refs_0_), channel_id=1, source_target_pairs={{0,8},{8,0},{16,24},{24,16},{1,9},{9,1},{17,25},{25,17},{2,10},{10... | collective-permute-start | bytes 1032200 | tf_op jit(solution)/shard_map/ppermute | solution.py:285
  33.3 26.6 %collective-permute-start.5 = (bf16[64,2688]{1,0:T(8,128)(2,1)S(1)}, bf16[64,2688]{1,0:T(8,128)(2,1)S(1)}, u32[]{:S(2)}, u32[]{:S(2)}) collective-permute-start(bf16[64,2688]{1,0:T(8,128)(2,1)S(1)} %fusion.28.refs_0_), channel_id=1, source_target_pairs={{0,16},{8,24},{16,0},{24,8},{1,17},{9,25},{17,1},{25,9},{2,18},{10... | collective-permute-start | bytes 1032200 | tf_op jit(solution)/shard_map/ppermute | solution.py:285
  36.0 24.0 %collective-permute-start.6 = (bf16[64,2688]{1,0:T(8,128)(2,1)S(1)}, bf16[64,2688]{1,0:T(8,128)(2,1)S(1)}, u32[]{:S(2)}, u32[]{:S(2)}) collective-permute-start(bf16[64,2688]{1,0:T(8,128)(2,1)S(1)} %fusion.28.refs_0_), channel_id=1, source_target_pairs={{0,24},{8,16},{16,8},{24,0},{1,25},{9,17},{17,9},{25,1},{2,26},{10... | collective-permute-start | bytes 1032200 | tf_op jit(solution)/shard_map/ppermute | solution.py:285
  48.5 18.8 %collective-permute-start.12 = (bf16[4,64,1536]{2,1,0:T(8,128)(2,1)S(1)}, bf16[4,64,1536]{2,1,0:T(8,128)(2,1)S(1)}, u32[]{:S(2)}, u32[]{:S(2)}) collective-permute-start(bf16[4,64,1536]{2,1,0:T(8,128)(2,1)S(1)} %copy-done.25), channel_id=1, source_target_pairs={{0,2},{2,0},{1,3},{3,1},{4,6},{6,4},{5,7},{7,5},{8,10},{10,8},{9,1... | collective-permute-start | bytes 2359304 | tf_op jit(solution)/shard_map/ppermute | solution.py:285
  49.5 11.6 %collective-permute-start.9 = (bf16[2,64,1536]{2,1,0:T(8,128)(2,1)S(1)}, bf16[2,64,1536]{2,1,0:T(8,128)(2,1)S(1)}, u32[]{:S(2)}, u32[]{:S(2)}) collective-permute-start(bf16[2,64,1536]{2,1,0:T(8,128)(2,1)S(1)} %slice.166), channel_id=1, source_target_pairs={{0,1},{1,5},{5,4},{4,0},{2,3},{3,7},{7,6},{6,2},{8,9},{9,13},{13,1... | collective-permute-start | bytes 1179656 | tf_op jit(solution)/shard_map/ppermute | solution.py:285
  51.2 11.3 %collective-permute-start.11 = (bf16[2,64,1536]{2,1,0:T(8,128)(2,1)S(1)}, bf16[2,64,1536]{2,1,0:T(8,128)(2,1)S(1)}, u32[]{:S(2)}, u32[]{:S(2)}) collective-permute-start(bf16[2,64,1536]{2,1,0:T(8,128)(2,1)S(1)} %slice.167), channel_id=1, source_target_pairs={{1,0},{5,1},{4,5},{0,4},{3,2},{7,3},{6,7},{2,6},{9,8},{13,9},{12,1... | collective-permute-start | bytes 1179656 | tf_op jit(solution)/shard_map/ppermute | solution.py:285
  60.0 13.4 %collective-permute-start.13 = (bf16[4,64,1536]{2,1,0:T(8,128)(2,1)}, bf16[4,64,1536]{2,1,0:T(8,128)(2,1)}, u32[]{:S(2)}, u32[]{:S(2)}) collective-permute-start(bf16[4,64,1536]{2,1,0:T(8,128)(2,1)} %collective-permute-done.8.refs_1_), channel_id=1, source_target_pairs={{0,2},{2,0},{1,3},{3,1},{4,6},{6,4},{5,7},{7,5},{8,10},{10,8},{9,1... | collective-permute-start | bytes 2359304 | tf_op jit(solution)/shard_map/ppermute | solution.py:285
  60.0 13.7 %collective-permute-start.14 = (bf16[4,64,1536]{2,1,0:T(8,128)(2,1)}, bf16[4,64,1536]{2,1,0:T(8,128)(2,1)}, u32[]{:S(2)}, u32[]{:S(2)}) collective-permute-start(bf16[4,64,1536]{2,1,0:T(8,128)(2,1)} %collective-permute-done.10.refs_2_), channel_id=1, source_target_pairs={{0,2},{2,0},{1,3},{3,1},{4,6},{6,4},{5,7},{7,5},{8,10},{10,8},{9,1... | collective-permute-start | bytes 2359304 | tf_op jit(solution)/shard_map/ppermute | solution.py:285
  61.1 9.6 %collective-permute-start.15 = (bf16[2,64,1536]{2,1,0:T(8,128)(2,1)S(1)}, bf16[2,64,1536]{2,1,0:T(8,128)(2,1)}, u32[]{:S(2)}, u32[]{:S(2)}) collective-permute-start(bf16[2,64,1536]{2,1,0:T(8,128)(2,1)S(1)} %collective-permute-done.9.refs_3_), channel_id=1, source_target_pairs={{0,2},{2,0},{1,3},{3,1},{4,6},{6,4},{5,7},{7,5},{8,10},{10,8},{9,1... | collective-permute-start | bytes 1179656 | tf_op jit(solution)/shard_map/ppermute | solution.py:285
  62.5 9.2 %collective-permute-start.16 = (bf16[2,64,1536]{2,1,0:T(8,128)(2,1)S(1)}, bf16[2,64,1536]{2,1,0:T(8,128)(2,1)}, u32[]{:S(2)}, u32[]{:S(2)}) collective-permute-start(bf16[2,64,1536]{2,1,0:T(8,128)(2,1)S(1)} %collective-permute-done.11.refs_4_), channel_id=1, source_target_pairs={{0,2},{2,0},{1,3},{3,1},{4,6},{6,4},{5,7},{7,5},{8,10},{10,8},{9,1... | collective-permute-start | bytes 1179656 | tf_op jit(solution)/shard_map/ppermute | solution.py:285
  67.3 50.0 %collective-permute-start.17 = (bf16[2,2,64,2048]{3,2,1,0:T(8,128)(2,1)}, bf16[2,2,64,2048]{3,2,1,0:T(8,128)(2,1)}, u32[]{:S(2)}, u32[]{:S(2)}) collective-permute-start(bf16[2,2,64,2048]{3,2,1,0:T(8,128)(2,1)} %join_pair.3.refs_0_), channel_id=1, source_target_pairs={{0,16},{8,24},{16,0},{24,8},{1,17},{9,25},{17,1},{25,9},{2,18},{10... | collective-permute-start | bytes 3145736 | tf_op jit(solution)/shard_map/ppermute | solution.py:285
  70.7 46.8 %collective-permute-start.27 = (bf16[2,2,64,2048]{3,2,1,0:T(8,128)(2,1)}, bf16[2,2,64,2048]{3,2,1,0:T(8,128)(2,1)}, u32[]{:S(2)}, u32[]{:S(2)}) collective-permute-start(bf16[2,2,64,2048]{3,2,1,0:T(8,128)(2,1)} %join_pair.3.refs_0_), channel_id=1, source_target_pairs={{0,8},{8,0},{16,24},{24,16},{1,9},{9,1},{17,25},{25,17},{2,10},{10... | collective-permute-start | bytes 3145736 | tf_op jit(solution)/shard_map/ppermute | solution.py:285
  71.7 32.1 %collective-permute-start.18 = (bf16[4,64,2688]{2,1,0:T(8,128)(2,1)}, bf16[4,64,2688]{2,1,0:T(8,128)(2,1)S(1)}, u32[]{:S(2)}, u32[]{:S(2)}) collective-permute-start(bf16[4,64,2688]{2,1,0:T(8,128)(2,1)} %join_column.2.refs_0_.refs_8_), channel_id=1, source_target_pairs={{0,1},{1,5},{5,4},{4,0},{2,3},{3,7},{7,6},{6,2},{8,9},{9,13},{13,1... | collective-permute-start | bytes 4128776 | tf_op jit(solution)/shard_map/ppermute | solution.py:285
  73.4 31.8 %collective-permute-start.19 = (bf16[4,64,2688]{2,1,0:T(8,128)(2,1)}, bf16[4,64,2688]{2,1,0:T(8,128)(2,1)S(1)}, u32[]{:S(2)}, u32[]{:S(2)}) collective-permute-start(bf16[4,64,2688]{2,1,0:T(8,128)(2,1)} %join_column.2.refs_0_.refs_8_), channel_id=1, source_target_pairs={{1,0},{5,1},{4,5},{0,4},{3,2},{7,3},{6,7},{2,6},{9,8},{13,9},{12,1... | collective-permute-start | bytes 4128776 | tf_op jit(solution)/shard_map/ppermute | solution.py:285
  73.7 48.9 %collective-permute-start.22 = (bf16[4,64,2688]{2,1,0:T(8,128)(2,1)}, bf16[4,64,2688]{2,1,0:T(8,128)(2,1)}, u32[]{:S(2)}, u32[]{:S(2)}) collective-permute-start(bf16[4,64,2688]{2,1,0:T(8,128)(2,1)} %join_column.2.refs_0_.refs_8_), channel_id=1, source_target_pairs={{0,2},{2,0},{1,3},{3,1},{4,6},{6,4},{5,7},{7,5},{8,10},{10,8},{9,1... | collective-permute-start | bytes 4128776 | tf_op jit(solution)/shard_map/ppermute | solution.py:285
  105.2 16.1 %collective-permute-start.20 = (bf16[2,64,2688]{2,1,0:T(8,128)(2,1)S(1)}, bf16[2,64,2688]{2,1,0:T(8,128)(2,1)S(1)}, u32[]{:S(2)}, u32[]{:S(2)}) collective-permute-start(bf16[2,64,2688]{2,1,0:T(8,128)(2,1)S(1)} %slice.129), channel_id=1, source_target_pairs={{0,1},{1,5},{5,4},{4,0},{2,3},{3,7},{7,6},{6,2},{8,9},{9,13},{13,1... | collective-permute-start | bytes 2064392 | tf_op jit(solution)/shard_map/ppermute | solution.py:285
  106.8 15.8 %collective-permute-start.21 = (bf16[2,64,2688]{2,1,0:T(8,128)(2,1)S(1)}, bf16[2,64,2688]{2,1,0:T(8,128)(2,1)S(1)}, u32[]{:S(2)}, u32[]{:S(2)}) collective-permute-start(bf16[2,64,2688]{2,1,0:T(8,128)(2,1)S(1)} %slice.130), channel_id=1, source_target_pairs={{1,0},{5,1},{4,5},{0,4},{3,2},{7,3},{6,7},{2,6},{9,8},{13,9},{12,1... | collective-permute-start | bytes 2064392 | tf_op jit(solution)/shard_map/ppermute | solution.py:285
  117.3 8.7 %collective-permute-start.23 = (bf16[4,64,2688]{2,1,0:T(8,128)(2,1)S(1)}, bf16[4,64,2688]{2,1,0:T(8,128)(2,1)S(1)}, u32[]{:S(2)}, u32[]{:S(2)}) collective-permute-start(bf16[4,64,2688]{2,1,0:T(8,128)(2,1)S(1)} %collective-permute-done.18.refs_1_.refs_9_), channel_id=1, source_target_pairs={{0,2},{2,0},{1,3},{3,1},{4,6},{6,4},{5,7},{7,5},{8,10},{10,8},{9,1... | collective-permute-start | bytes 4128776 | tf_op jit(solution)/shard_map/ppermute | solution.py:285
  117.5 9.6 %collective-permute-start.24 = (bf16[4,64,2688]{2,1,0:T(8,128)(2,1)S(1)}, bf16[4,64,2688]{2,1,0:T(8,128)(2,1)}, u32[]{:S(2)}, u32[]{:S(2)}) collective-permute-start(bf16[4,64,2688]{2,1,0:T(8,128)(2,1)S(1)} %collective-permute-done.19.refs_2_.refs_10_), channel_id=1, source_target_pairs={{0,2},{2,0},{1,3},{3,1},{4,6},{6,4},{5,7},{7,5},{8,10},{10,8},{9,1... | collective-permute-start | bytes 4128776 | tf_op jit(solution)/shard_map/ppermute | solution.py:285
  121.3 2.1 collective-permute-start.25
  122.6 2.4 collective-permute-start.26
  122.6 27.9 %collective-permute-start.29 = (bf16[2,2,64,2048]{3,2,1,0:T(8,128)(2,1)}, bf16[2,2,64,2048]{3,2,1,0:T(8,128)(2,1)}, u32[]{:S(2)}, u32[]{:S(2)}) collective-permute-start(bf16[2,2,64,2048]{3,2,1,0:T(8,128)(2,1)} %join_pair.3.refs_0_), channel_id=1, source_target_pairs={{0,2},{2,0},{1,3},{3,1},{4,6},{6,4},{5,7},{7,5},{8,10},{10,8},{9,1... | collective-permute-start | bytes 3145736 | tf_op jit(solution)/shard_map/ppermute | solution.py:285
  123.5 27.1 %collective-permute-start.30 = (bf16[2,2,64,2048]{3,2,1,0:T(8,128)(2,1)}, bf16[2,2,64,2048]{3,2,1,0:T(8,128)(2,1)}, u32[]{:S(2)}, u32[]{:S(2)}) collective-permute-start(bf16[2,2,64,2048]{3,2,1,0:T(8,128)(2,1)} %collective-permute-done.27.refs_1_), channel_id=1, source_target_pairs={{0,2},{2,0},{1,3},{3,1},{4,6},{6,4},{5,7},{7,5},{8,10},{10,8},{9,1... | collective-permute-start | bytes 3145736 | tf_op jit(solution)/shard_map/ppermute | solution.py:285
  125.0 25.5 %collective-permute-start.28 = (bf16[2,2,64,2048]{3,2,1,0:T(8,128)(2,1)}, bf16[2,2,64,2048]{3,2,1,0:T(8,128)(2,1)}, u32[]{:S(2)}, u32[]{:S(2)}) collective-permute-start(bf16[2,2,64,2048]{3,2,1,0:T(8,128)(2,1)} %collective-permute-done.17.refs_2_), channel_id=1, source_target_pairs={{0,8},{8,0},{16,24},{24,16},{1,9},{9,1},{17,25},{25,17},{2,10},{10... | collective-permute-start | bytes 3145736 | tf_op jit(solution)/shard_map/ppermute | solution.py:285
  127.0 23.5 %collective-permute-start.31 = (bf16[2,2,64,2048]{3,2,1,0:T(8,128)(2,1)}, bf16[2,2,64,2048]{3,2,1,0:T(8,128)(2,1)}, u32[]{:S(2)}, u32[]{:S(2)}) collective-permute-start(bf16[2,2,64,2048]{3,2,1,0:T(8,128)(2,1)} %collective-permute-done.17.refs_2_), channel_id=1, source_target_pairs={{0,2},{2,0},{1,3},{3,1},{4,6},{6,4},{5,7},{7,5},{8,10},{10,8},{9,1... | collective-permute-start | bytes 3145736 | tf_op jit(solution)/shard_map/ppermute | solution.py:285
  150.5 2.9 collective-permute-start.32
  182.6 7.5 %collective-permute-start.34 = (bf16[4,2,2,64,2048]{4,3,2,1,0:T(8,128)(2,1)}, bf16[4,2,2,64,2048]{4,3,2,1,0:T(8,128)(2,1)}, u32[]{:S(2)}, u32[]{:S(2)}) collective-permute-start(bf16[4,2,2,64,2048]{4,3,2,1,0:T(8,128)(2,1)} %get-tuple-element.132), channel_id=1, source_target_pairs={{0,2},{2,0},{1,3},{3,1},{4,6},{6,4},{5,7},{7,5},{8,10},{10,8},{9,1... | collective-permute-start | bytes 12582920 | tf_op jit(solution)/shard_map/ppermute | solution.py:285
  182.9 42.6 %collective-permute-start.33 = (bf16[532,1024]{1,0:T(8,128)(2,1)S(1)}, bf16[532,1024]{1,0:T(8,128)(2,1)S(1)}, u32[]{:S(2)}, u32[]{:S(2)}) collective-permute-start(bf16[532,1024]{1,0:T(8,128)(2,1)S(1)} %slice.131.own_ref), channel_id=1, source_target_pairs={{0,1},{1,0},{2,3},{3,2},{4,5},{5,4},{6,7},{7,6},{8,9},{9,8},{10,11... | collective-permute-start | bytes 3268616 | tf_op jit(solution)/shard_map/ppermute | solution.py:285
  194.6 30.9 %collective-permute-start.36 = (bf16[2,2,64,2048]{3,2,1,0:T(8,128)(2,1)}, bf16[2,2,64,2048]{3,2,1,0:T(8,128)(2,1)S(1)}, u32[]{:S(2)}, u32[]{:S(2)}) collective-permute-start(bf16[2,2,64,2048]{3,2,1,0:T(8,128)(2,1)} %get-tuple-element.303), channel_id=1, source_target_pairs={{0,8},{8,0},{16,24},{24,16},{1,9},{9,1},{17,25},{25,17},{2,10},{10... | collective-permute-start | bytes 3145736 | tf_op jit(solution)/shard_map/ppermute | solution.py:285
  232.0 9.4 %collective-permute-start.37 = (bf16[2,2,4,64,2688]{4,3,2,1,0:T(8,128)(2,1)}, bf16[2,2,4,64,2688]{4,3,2,1,0:T(8,128)(2,1)}, u32[]{:S(2)}, u32[]{:S(2)}) collective-permute-start(bf16[2,2,4,64,2688]{4,3,2,1,0:T(8,128)(2,1)} %get-tuple-element.147), channel_id=1, source_target_pairs={{0,2},{2,0},{1,3},{3,1},{4,6},{6,4},{5,7},{7,5},{8,10},{10,8},{9,1... | collective-permute-start | bytes 16515080 | tf_op jit(solution)/shard_map/ppermute | solution.py:285
  232.2 48.7 %collective-permute-start.35 = (bf16[2,2,64,2048]{3,2,1,0:T(8,128)(2,1)}, bf16[2,2,64,2048]{3,2,1,0:T(8,128)(2,1)}, u32[]{:S(2)}, u32[]{:S(2)}) collective-permute-start(bf16[2,2,64,2048]{3,2,1,0:T(8,128)(2,1)} %get-tuple-element.302), channel_id=1, source_target_pairs={{0,8},{8,0},{16,24},{24,16},{1,9},{9,1},{17,25},{25,17},{2,10},{10... | collective-permute-start | bytes 3145736 | tf_op jit(solution)/shard_map/ppermute | solution.py:285
  236.5 49.1 %collective-permute-start.40 = (bf16[2,2,64,2048]{3,2,1,0:T(8,128)(2,1)}, bf16[2,2,64,2048]{3,2,1,0:T(8,128)(2,1)}, u32[]{:S(2)}, u32[]{:S(2)}) collective-permute-start(bf16[2,2,64,2048]{3,2,1,0:T(8,128)(2,1)} %fusion.1), channel_id=1, source_target_pairs={{0,16},{8,24},{16,0},{24,8},{1,17},{9,25},{17,1},{25,9},{2,18},{10... | collective-permute-start | bytes 3145736 | tf_op jit(solution)/shard_map/ppermute | solution.py:285
  247.0 27.5 %collective-permute-start.38 = (bf16[2,64,2688]{2,1,0:T(8,128)(2,1)}, bf16[2,64,2688]{2,1,0:T(8,128)(2,1)}, u32[]{:S(2)}, u32[]{:S(2)}) collective-permute-start(bf16[2,64,2688]{2,1,0:T(8,128)(2,1)} %get-tuple-element.315), channel_id=1, source_target_pairs={{0,1},{1,5},{5,4},{4,0},{2,3},{3,7},{7,6},{6,2},{8,9},{9,13},{13,1... | collective-permute-start | bytes 2064392 | tf_op jit(solution)/shard_map/ppermute | solution.py:285
  249.0 25.4 %collective-permute-start.39 = (bf16[2,64,2688]{2,1,0:T(8,128)(2,1)}, bf16[2,64,2688]{2,1,0:T(8,128)(2,1)}, u32[]{:S(2)}, u32[]{:S(2)}) collective-permute-start(bf16[2,64,2688]{2,1,0:T(8,128)(2,1)} %get-tuple-element.314), channel_id=1, source_target_pairs={{1,0},{5,1},{4,5},{0,4},{3,2},{7,3},{6,7},{2,6},{9,8},{13,9},{12,1... | collective-permute-start | bytes 2064392 | tf_op jit(solution)/shard_map/ppermute | solution.py:285
  277.4 32.3 %collective-permute-start.42 = (bf16[4,64,2688]{2,1,0:T(8,128)(2,1)}, bf16[4,64,2688]{2,1,0:T(8,128)(2,1)}, u32[]{:S(2)}, u32[]{:S(2)}) collective-permute-start(bf16[4,64,2688]{2,1,0:T(8,128)(2,1)} %pad_maximum_fusion.1), channel_id=1, source_target_pairs={{1,0},{5,1},{4,5},{0,4},{3,2},{7,3},{6,7},{2,6},{9,8},{13,9},{12,1... | collective-permute-start | bytes 4128776 | tf_op jit(solution)/shard_map/ppermute | solution.py:285
  280.1 31.7 %collective-permute-start.41 = (bf16[4,64,2688]{2,1,0:T(8,128)(2,1)S(1)}, bf16[4,64,2688]{2,1,0:T(8,128)(2,1)S(1)}, u32[]{:S(2)}, u32[]{:S(2)}) collective-permute-start(bf16[4,64,2688]{2,1,0:T(8,128)(2,1)S(1)} %pad_maximum_fusion), channel_id=1, source_target_pairs={{0,1},{1,5},{5,4},{4,0},{2,3},{3,7},{7,6},{6,2},{8,9},{9,13},{13,1... | collective-permute-start | bytes 4128776 | tf_op jit(solution)/shard_map/ppermute | solution.py:285
  311.8 11.3 %collective-permute-start.43 = (bf16[2,2,4,64,1536]{4,3,2,1,0:T(8,128)(2,1)}, bf16[2,2,4,64,1536]{4,3,2,1,0:T(8,128)(2,1)}, u32[]{:S(2)}, u32[]{:S(2)}) collective-permute-start(bf16[2,2,4,64,1536]{4,3,2,1,0:T(8,128)(2,1)} %get-tuple-element.163), channel_id=1, source_target_pairs={{0,2},{2,0},{1,3},{3,1},{4,6},{6,4},{5,7},{7,5},{8,10},{10,8},{9,1... | collective-permute-start | bytes 9437192 | tf_op jit(solution)/shard_map/ppermute | solution.py:285
  315.2 14.7 %collective-permute-start.48 = (bf16[272,1024]{1,0:T(8,128)(2,1)S(1)}, bf16[272,1024]{1,0:T(8,128)(2,1)S(1)}, u32[]{:S(2)}, u32[]{:S(2)}) collective-permute-start(bf16[272,1024]{1,0:T(8,128)(2,1)S(1)} %slice.150), channel_id=1, source_target_pairs={{0,1},{1,0},{2,3},{3,2},{4,5},{5,4},{6,7},{7,6},{8,9},{9,8},{10,11... | collective-permute-start | bytes 1671176 | tf_op jit(solution)/shard_map/ppermute | solution.py:285
  315.9 16.5 %collective-permute-start.47 = (bf16[2,64,2048]{2,1,0:T(8,128)(2,1)}, bf16[2,64,2048]{2,1,0:T(8,128)(2,1)S(1)}, u32[]{:S(2)}, u32[]{:S(2)}) collective-permute-start(bf16[2,64,2048]{2,1,0:T(8,128)(2,1)} %fusion.21), channel_id=1, source_target_pairs={{0,4},{4,0},{1,5},{5,1},{2,6},{6,2},{3,7},{7,3},{8,12},{12,8},{9,1... | collective-permute-start | bytes 1572872 | tf_op jit(solution)/shard_map/ppermute | solution.py:285
  321.1 11.3 %collective-permute-start.46 = (bf16[64,2688]{1,0:T(8,128)(2,1)S(1)}, bf16[64,2688]{1,0:T(8,128)(2,1)S(1)}, u32[]{:S(2)}, u32[]{:S(2)}) collective-permute-start(bf16[64,2688]{1,0:T(8,128)(2,1)S(1)} %get-tuple-element.308), channel_id=1, source_target_pairs={{0,8},{8,0},{16,24},{24,16},{1,9},{9,1},{17,25},{25,17},{2,10},{10... | collective-permute-start | bytes 1032200 | tf_op jit(solution)/shard_map/ppermute | solution.py:285
  322.5 22.6 %collective-permute-start.51 = (bf16[64,2688]{1,0:T(8,128)(2,1)S(1)}, bf16[64,2688]{1,0:T(8,128)(2,1)S(1)}, u32[]{:S(2)}, u32[]{:S(2)}) collective-permute-start(bf16[64,2688]{1,0:T(8,128)(2,1)S(1)} %get-tuple-element.307), channel_id=1, source_target_pairs={{0,8},{8,0},{16,24},{24,16},{1,9},{9,1},{17,25},{25,17},{2,10},{10... | collective-permute-start | bytes 1032200 | tf_op jit(solution)/shard_map/ppermute | solution.py:285
  325.6 12.6 %collective-permute-start.44 = (bf16[2,64,1536]{2,1,0:T(8,128)(2,1)S(1)}, bf16[2,64,1536]{2,1,0:T(8,128)(2,1)S(1)}, u32[]{:S(2)}, u32[]{:S(2)}) collective-permute-start(bf16[2,64,1536]{2,1,0:T(8,128)(2,1)S(1)} %get-tuple-element.317), channel_id=1, source_target_pairs={{0,1},{1,5},{5,4},{4,0},{2,3},{3,7},{7,6},{6,2},{8,9},{9,13},{13,1... | collective-permute-start | bytes 1179656 | tf_op jit(solution)/shard_map/ppermute | solution.py:285
  329.9 10.3 %collective-permute-start.45 = (bf16[2,64,1536]{2,1,0:T(8,128)(2,1)S(1)}, bf16[2,64,1536]{2,1,0:T(8,128)(2,1)S(1)}, u32[]{:S(2)}, u32[]{:S(2)}) collective-permute-start(bf16[2,64,1536]{2,1,0:T(8,128)(2,1)S(1)} %get-tuple-element.316), channel_id=1, source_target_pairs={{1,0},{5,1},{4,5},{0,4},{3,2},{7,3},{6,7},{2,6},{9,8},{13,9},{12,1... | collective-permute-start | bytes 1179656 | tf_op jit(solution)/shard_map/ppermute | solution.py:285
  332.5 17.3 %collective-permute-start.52 = (bf16[64,2688]{1,0:T(8,128)(2,1)S(1)}, bf16[64,2688]{1,0:T(8,128)(2,1)S(1)}, u32[]{:S(2)}, u32[]{:S(2)}) collective-permute-start(bf16[64,2688]{1,0:T(8,128)(2,1)S(1)} %fusion.17), channel_id=1, source_target_pairs={{0,16},{8,24},{16,0},{24,8},{1,17},{9,25},{17,1},{25,9},{2,18},{10... | collective-permute-start | bytes 1032200 | tf_op jit(solution)/shard_map/ppermute | solution.py:285
  341.3 20.5 %collective-permute-start.50 = (bf16[4,64,1536]{2,1,0:T(8,128)(2,1)}, bf16[4,64,1536]{2,1,0:T(8,128)(2,1)}, u32[]{:S(2)}, u32[]{:S(2)}) collective-permute-start(bf16[4,64,1536]{2,1,0:T(8,128)(2,1)} %pad_maximum_fusion.3), channel_id=1, source_target_pairs={{1,0},{5,1},{4,5},{0,4},{3,2},{7,3},{6,7},{2,6},{9,8},{13,9},{12,1... | collective-permute-start | bytes 2359304 | tf_op jit(solution)/shard_map/ppermute | solution.py:285
  344.0 17.8 %collective-permute-start.49 = (bf16[4,64,1536]{2,1,0:T(8,128)(2,1)}, bf16[4,64,1536]{2,1,0:T(8,128)(2,1)}, u32[]{:S(2)}, u32[]{:S(2)}) collective-permute-start(bf16[4,64,1536]{2,1,0:T(8,128)(2,1)} %pad_maximum_fusion.2), channel_id=1, source_target_pairs={{0,1},{1,5},{5,4},{4,0},{2,3},{3,7},{7,6},{6,2},{8,9},{9,13},{13,1... | collective-permute-start | bytes 2359304 | tf_op jit(solution)/shard_map/ppermute | solution.py:285
  364.9 9.6 %collective-permute-start.57 = (bf16[64,2048]{1,0:T(8,128)(2,1)}, bf16[64,2048]{1,0:T(8,128)(2,1)}, u32[]{:S(2)}, u32[]{:S(2)}) collective-permute-start(bf16[64,2048]{1,0:T(8,128)(2,1)} %fusion.31), channel_id=1, source_target_pairs={{0,1},{1,0},{2,3},{3,2},{4,5},{5,4},{6,7},{7,6},{8,9},{9,8},{10,11... | collective-permute-start | bytes 786440 | tf_op jit(solution)/shard_map/ppermute | solution.py:285
  365.2 15.5 %collective-permute-start.53 = (bf16[260,1024]{1,0:T(8,128)(2,1)}, bf16[260,1024]{1,0:T(8,128)(2,1)}, u32[]{:S(2)}, u32[]{:S(2)}) collective-permute-start(bf16[260,1024]{1,0:T(8,128)(2,1)} %slice.158), channel_id=1, source_target_pairs={{0,1},{1,0},{2,3},{3,2},{4,5},{5,4},{6,7},{7,6},{8,9},{9,8},{10,11... | collective-permute-start | bytes 1597448 | tf_op jit(solution)/shard_map/ppermute | solution.py:285
  369.5 13.1 %collective-permute-start.54 = (bf16[64,1536]{1,0:T(8,128)(2,1)}, bf16[64,1536]{1,0:T(8,128)(2,1)S(1)}, u32[]{:S(2)}, u32[]{:S(2)}) collective-permute-start(bf16[64,1536]{1,0:T(8,128)(2,1)} %get-tuple-element.313), channel_id=1, source_target_pairs={{0,8},{8,0},{16,24},{24,16},{1,9},{9,1},{17,25},{25,17},{2,10},{10... | collective-permute-start | bytes 589832 | tf_op jit(solution)/shard_map/ppermute | solution.py:285
  370.5 14.4 %collective-permute-start.55 = (bf16[64,1536]{1,0:T(8,128)(2,1)}, bf16[64,1536]{1,0:T(8,128)(2,1)S(1)}, u32[]{:S(2)}, u32[]{:S(2)}) collective-permute-start(bf16[64,1536]{1,0:T(8,128)(2,1)} %get-tuple-element.312), channel_id=1, source_target_pairs={{0,16},{8,24},{16,0},{24,8},{1,17},{9,25},{17,1},{25,9},{2,18},{10... | collective-permute-start | bytes 589832 | tf_op jit(solution)/shard_map/ppermute | solution.py:285
  372.4 12.5 %collective-permute-start.56 = (bf16[64,1536]{1,0:T(8,128)(2,1)}, bf16[64,1536]{1,0:T(8,128)(2,1)S(1)}, u32[]{:S(2)}, u32[]{:S(2)}) collective-permute-start(bf16[64,1536]{1,0:T(8,128)(2,1)} %get-tuple-element.311), channel_id=1, source_target_pairs={{0,24},{8,16},{16,8},{24,0},{1,25},{9,17},{17,9},{25,1},{2,26},{10... | collective-permute-start | bytes 589832 | tf_op jit(solution)/shard_map/ppermute | solution.py:285
  390.2 4.9 %collective-permute-start.59 = (f32[8,128]{1,0:T(8,128)S(1)}, f32[8,128]{1,0:T(8,128)S(1)}, u32[]{:S(2)}, u32[]{:S(2)}) collective-permute-start(f32[8,128]{1,0:T(8,128)S(1)} %broadcast_add_fusion), channel_id=1, source_target_pairs={{0,1},{1,0},{4,5},{5,4},{2,3},{3,2},{6,7},{7,6},{8,9},{9,8},{12,13... | collective-permute-start | bytes 12296 | tf_op jit(solution)/shard_map/ppermute | solution.py:285
  391.7 3.6 collective-permute-start.60
  392.0 4.5 %collective-permute-start.61 = (f32[8,128]{1,0:T(8,128)S(1)}, f32[8,128]{1,0:T(8,128)S(1)}, u32[]{:S(2)}, u32[]{:S(2)}) collective-permute-start(f32[8,128]{1,0:T(8,128)S(1)} %broadcast_add_fusion), channel_id=1, source_target_pairs={{0,5},{1,4},{4,1},{5,0},{2,7},{3,6},{6,3},{7,2},{8,13},{9,12},{12,... | collective-permute-start | bytes 12296 | tf_op jit(solution)/shard_map/ppermute | solution.py:285
  396.5 11.3 %collective-permute-start.62 = (f32[8,128]{1,0:T(8,128)S(1)}, f32[8,128]{1,0:T(8,128)S(1)}, u32[]{:S(2)}, u32[]{:S(2)}) collective-permute-start(f32[8,128]{1,0:T(8,128)S(1)} %add_add_fusion.1), channel_id=1, source_target_pairs={{0,8},{8,0},{16,24},{24,16},{1,9},{9,1},{17,25},{25,17},{2,10},{10... | collective-permute-start | bytes 12296 | tf_op jit(solution)/shard_map/ppermute | solution.py:285
  399.1 8.7 %collective-permute-start.63 = (f32[8,128]{1,0:T(8,128)S(1)}, f32[8,128]{1,0:T(8,128)S(1)}, u32[]{:S(2)}, u32[]{:S(2)}) collective-permute-start(f32[8,128]{1,0:T(8,128)S(1)} %add_add_fusion.1), channel_id=1, source_target_pairs={{0,16},{8,24},{16,0},{24,8},{1,17},{9,25},{17,1},{25,9},{2,18},{10... | collective-permute-start | bytes 12296 | tf_op jit(solution)/shard_map/ppermute | solution.py:285
  400.6 7.2 %collective-permute-start.64 = (f32[8,128]{1,0:T(8,128)S(1)}, f32[8,128]{1,0:T(8,128)S(1)}, u32[]{:S(2)}, u32[]{:S(2)}) collective-permute-start(f32[8,128]{1,0:T(8,128)S(1)} %add_add_fusion.1), channel_id=1, source_target_pairs={{0,24},{8,16},{16,8},{24,0},{1,25},{9,17},{17,9},{25,1},{2,26},{10... | collective-permute-start | bytes 12296 | tf_op jit(solution)/shard_map/ppermute | solution.py:285
  (64 other events, 433.4 us)

commit v4 on v3

--- a/solution.py
+++ b/solution.py
@@ -848,6 +848,7 @@
     lane = lax.broadcasted_iota(jnp.int32, k.shape, 1)
     scale = HEAD**-0.5
     queries = q_ref[0]
+    queries_turned, grad_turned = queries.T, grad.T
     outs = []
     for h, (q, own_grad) in enumerate(zip(head_parts(queries, lane, scale), head_parts(grad, lane))):
         log_total = l_ref[:, h * HEAD : h * HEAD + 1]
@@ -855,11 +856,13 @@
         prob_grad = mm(own_grad, v, NT)
         score_grad = probs * (prob_grad - jnp.sum(probs * prob_grad, axis=-1, keepdims=True))
         score_grad = score_grad.astype(LOW)
+        mine = slice(h * HEAD, (h + 1) * HEAD)
         outs.append(
-            (mm(score_grad, k) * scale, mm(score_grad, queries, TN) * scale, mm(probs.astype(LOW), grad, TN))
+            (mm(score_grad, k) * scale, mm(queries_turned[mine], score_grad) * scale, mm(grad_turned[mine], probs.astype(LOW)))
         )
-    for i in range(3):
-        o_ref[i] = jnp.where(lane < HEAD, outs[0][i], outs[1][i]).astype(LOW)
+    o_ref[0] = jnp.where(lane < HEAD, outs[0][0], outs[1][0]).astype(LOW)
+    for i in (1, 2):
+        o_ref[i] = jnp.concatenate([outs[0][i], outs[1][i]], axis=0).T.astype(LOW)
 
 
 def final_rows_kernel(own_ref, other_ref, o_ref):

time: 428 us -> 425 us (level)
  transfers between devices with their start and end apart: 65 -> 65, of which waited for: 31 -> 32; matrix products, arithmetic and copies ran while one was open for 14% -> 14% of each run, Pallas kernels for 31% -> 31%
where the time goes in v4:
time: 425 us; the launch traced here: 417 us
  Pallas kernels  165 us (39%)
  waiting for transfers between devices  95.7 us (23%)
  starting transfers between devices  68.2 us (16%)
  other arithmetic  49.9 us (12%)
  local copies, waits for them, and re-layouts  30.1 us (7%)
  between operations  8.15 us (2%)
    ppermute x65, waiting for transfers between devices, send(): return lax.ppermute(block, axes, list(pairs))  95.7 us
    ppermute x65, starting transfers between devices, send(): return lax.ppermute(block, axes, list(pairs))  68.2 us
    pallas_call x1, Pallas kernels, inner_back(): pl.pallas_call(functools.partial(inner_kernel, chunks // 2, len(downs)),...  29.9 us
    pallas_call x1, Pallas kernels, attention_back(): pl.pallas_call(attend_back_kernel, grid=(pairs,), in_specs=pair_specs(tot...  21.4 us
    pallas_call x1, Pallas kernels, attention(): pl.pallas_call(attend_kernel, grid=(pairs,), in_specs=pair_specs(total, p...  18.1 us
    pallas_call x1, Pallas kernels, qkv_back(): pl.pallas_call(functools.partial(qkv_back_kernel, per_side), grid=(2 * pe...  17.2 us
    pallas_call x1, Pallas kernels, up(): pl.pallas_call(functools.partial(up_kernel, per_side), grid=(2 * per_side...  16.1 us
    pallas_call x1, Pallas kernels, down(): pl.pallas_call(functools.partial(down_kernel, chunks // 2, len(pieces)),...  15.5 us
  transfers between devices with their start and end apart: 65, of which 32 were waited for; matrix products, arithmetic and copies ran while one was open for 14% of the time, Pallas kernels for 31%

profile of v4, /device:TPU:0, one launch (start us, length us, event | category | flops | bytes accessed | tf_op | source)
XLA Modules:
  0.0 416.8 jit_solution(7937906732181553828)
XLA Ops:
  1.9 3.0 collective-permute-start
  6.1 1.6 collective-permute-start.1
  7.7 2.6 collective-permute-start.2
  12.5 1.8 join_pair.2.own
  22.8 2.1 collective-permute-done.2.refs_2_
  25.0 2.3 collective-permute-done.7.other
  27.3 2.3 join_column.3.refs_0_
  33.3 2.7 collective-permute-start.5
  36.3 12.2 %collective-permute-done.8.refs_1_ = bf16[4,64,1536]{2,1,0:T(8,128)(2,1)} collective-permute-done((bf16[4,64,1536]{2,1,0:T(8,128)(2,1)}, bf16[4,64,1536]{2,1,0:T(8,128)(2,1)}, u32[]{:S(2)}, u32[]{:S(2)}) %collective-permute-start.8) | collective-permute-done | bytes 786464 | tf_op jit(solution)/shard_map/ppermute | solution.py:285
  52.7 7.3 %collective-permute-done.5.refs_2_ = bf16[64,2688]{1,0:T(8,128)(2,1)S(1)} collective-permute-done((bf16[64,2688]{1,0:T(8,128)(2,1)S(1)}, bf16[64,2688]{1,0:T(8,128)(2,1)S(1)}, u32[]{:S(2)}, u32[]{:S(2)}) %collective-permute-start.5) | collective-permute-done | bytes 344096 | tf_op jit(solution)/shard_map/ppermute | solution.py:285
  62.5 2.4 join_pair.3.refs_0_
  64.9 2.4 join_column.2.refs_0_.refs_8_
  67.3 3.4 collective-permute-start.17
  71.7 1.7 collective-permute-start.18
  73.7 8.2 %project.1.q_ref.k_ref.v_ref = bf16[6,544,512]{2,1,0:T(8,128)(2,1)} custom-call(bf16[544,1024]{1,0:T(8,128)(2,1)} %pad.15.x_ref, bf16[4,64,1536]{2,1,0:T(8,128)(2,1)} %join_column.3.refs_0_, bf16[4,64,1536]{2,1,0:T(8,128)(2,1)} %collective-permute-done.8.refs_1_, bf16[4,64,1536]{2,1,0:T(8,128)(2,1)} %collective-permute-done.10.refs_2_, ...), custom_call_target="tpu_custom_call" | custom-call | flops 6600000000 | bytes 12000000 | tf_op jit(solution)/shard_map/project/pallas_call | solution.py:463
  81.9 18.1 %attention.1 = (bf16[544,1024]{1,0:T(8,128)(2,1)}, f32[544,1024]{1,0:T(8,128)}) custom-call(bf16[6,544,512]{2,1,0:T(8,128)(2,1)} %project.1.q_ref.k_ref.v_ref, bf16[6,544,512]{2,1,0:T(8,128)(2,1)} %project.1.q_ref.k_ref.v_ref, bf16[6,544,512]{2,1,0:T(8,128)(2,1)} %project.1.q_ref.k_ref.v_ref, bf16[544,544]{1,0:T(8,128)(2,1)} %select_convert_fusion.bias_ref), custom_call_target="tpu_custom_call" | custom-call | flops 18699999232 | bytes 34000000 | tf_op jit(solution)/shard_map/attention/pallas_call | solution.py:507
  100.1 3.7 collective-permute-done.18.refs_1_.refs_9_
  107.4 9.9 %collective-permute-done.17.refs_2_ = bf16[2,2,64,2048]{3,2,1,0:T(8,128)(2,1)} collective-permute-done((bf16[2,2,64,2048]{3,2,1,0:T(8,128)(2,1)}, bf16[2,2,64,2048]{3,2,1,0:T(8,128)(2,1)}, u32[]{:S(2)}, u32[]{:S(2)}) %collective-permute-start.17) | collective-permute-done | bytes 1048608 | tf_op jit(solution)/shard_map/ppermute | solution.py:285
  117.8 3.5 collective-permute-done.20.refs_3_.refs_11_
  127.1 16.1 %up.1 = (bf16[544,1024]{1,0:T(8,128)(2,1)}, f32[544,1024]{1,0:T(8,128)}, f32[544,128]{1,0:T(8,128)}, f32[8,1024]{1,0:T(8,128)}, bf16[8,544,512]{2,1,0:T(8,128)(2,1)}, /*index=5*/bf16[8,544,512]{2,1,0:T(8,128)(2,1)}) custom-call(bf16[544,1024]{1,0:T(8,128)(2,1)} %pad.15.x_ref, bf16[544,1024]{1,0:T(8,128)(2,1)} %get-tuple-element.123.ctx_ref, ...), custom_call_target="tpu_custom_call" | custom-call | flops 24199999488 | bytes 44000000 | tf_op jit(solution)/shard_map/up/pallas_call | solution.py:597
  143.2 7.4 %collective-permute-done.28.refs_3_ = bf16[2,2,64,2048]{3,2,1,0:T(8,128)(2,1)} collective-permute-done((bf16[2,2,64,2048]{3,2,1,0:T(8,128)(2,1)}, bf16[2,2,64,2048]{3,2,1,0:T(8,128)(2,1)}, u32[]{:S(2)}, u32[]{:S(2)}) %collective-permute-start.28) | collective-permute-done | bytes 1048608 | tf_op jit(solution)/shard_map/ppermute | solution.py:285
  150.6 2.8 collective-permute-done.32.refs_7_
  154.4 15.5 %down.1 = (bf16[544,1024]{1,0:T(8,128)(2,1)}, f32[544,1024]{1,0:T(8,128)}, bf16[544,1024]{1,0:T(8,128)(2,1)}, f32[8,1024]{1,0:T(8,128)}) custom-call(bf16[8,544,512]{2,1,0:T(8,128)(2,1)} %get-tuple-element.125.g_ref.b_ref, f32[544,1024]{1,0:T(8,128)} %get-tuple-element.126.n_ref, f32[8,1024]{1,0:T(8,128)} %get-tuple-element.127.norms_ref, ...), custom_call_target="tpu_custom_call" | custom-call | flops 18699999232 | bytes 34000000 | tf_op jit(solution)/shard_map/down/pallas_call | solution.py:660
  170.0 12.7 %down_grad.1 = (bf16[4,2,2,64,2048]{4,3,2,1,0:T(8,128)(2,1)}, bf16[4,2,2,64,2048]{4,3,2,1,0:T(8,128)(2,1)}) custom-call(bf16[544,1024]{1,0:T(8,128)(2,1)} %get-tuple-element.133.a_ref.f_ref, bf16[8,544,512]{2,1,0:T(8,128)(2,1)} %get-tuple-element.125.g_ref.b_ref), custom_call_target="tpu_custom_call" | custom-call | flops 9900000256 | bytes 18000000 | tf_op jit(solution)/shard_map/down_grad/pallas_call | solution.py:720
  182.9 2.0 collective-permute-start.33
  184.9 5.3 %collective-permute-done.34 = bf16[4,2,2,64,2048]{4,3,2,1,0:T(8,128)(2,1)} collective-permute-done((bf16[4,2,2,64,2048]{4,3,2,1,0:T(8,128)(2,1)}, bf16[4,2,2,64,2048]{4,3,2,1,0:T(8,128)(2,1)}, u32[]{:S(2)}, u32[]{:S(2)}) %collective-permute-start.34) | collective-permute-done | bytes 4194336 | tf_op jit(solution)/shard_map/ppermute | solution.py:285
  190.2 4.4 %fusion.9 = (bf16[2,2,64,2048]{3,2,1,0:T(8,128)(2,1)}, bf16[2,2,64,2048]{3,2,1,0:T(8,128)(2,1)}) fusion(bf16[4,2,2,64,2048]{4,3,2,1,0:T(8,128)(2,1)} %collective-permute-done.34, s32[]{:T(128)S(6)} %select_n.192, bf16[4,2,2,64,2048]{4,3,2,1,0:T(8,128)(2,1)} %get-tuple-element.131, s32[]{:T(128)S(6)} %select_n.190), kind=kLoop, calls=%fused_computation.33 | loop fusion | flops 4194304 | bytes 6291464 | tf_op jit(solution)/shard_map/convert_element_type | solution.py:1167
  195.5 29.9 %inner_back.1 = (bf16[2,2,4,64,2688]{4,3,2,1,0:T(8,128)(2,1)}, bf16[2,2,4,64,2688]{4,3,2,1,0:T(8,128)(2,1)}, f32[544,1024]{1,0:T(8,128)}, bf16[544,1024]{1,0:T(8,128)(2,1)}, f32[8,1024]{1,0:T(8,128)}) custom-call(bf16[544,1024]{1,0:T(8,128)(2,1)} %get-tuple-element.133.a_ref.f_ref, bf16[8,544,512]{2,1,0:T(8,128)(2,1)} %get-tuple-element.134.d_ref, ...), custom_call_target="tpu_custom_call" | custom-call | flops 35200000000 | bytes 64000000 | tf_op jit(solution)/shard_map/inner_back/pallas_call | solution.py:778
  225.4 6.5 %out_back.1 = (bf16[2,2,4,64,2688]{4,3,2,1,0:T(8,128)(2,1)}, bf16[2,2,4,64,2688]{4,3,2,1,0:T(8,128)(2,1)}, bf16[544,1024]{1,0:T(8,128)(2,1)}) custom-call(bf16[544,1024]{1,0:T(8,128)(2,1)} %get-tuple-element.141.a_ref, bf16[544,1024]{1,0:T(8,128)(2,1)} %get-tuple-element.123.ctx_ref, ...), custom_call_target="tpu_custom_call", output_to_operand_aliasing={{0}: (4, {}), {1}: (5, {})} | custom-call | flops 4400000000 | bytes 8000000 | tf_op jit(solution)/shard_map/out_back/pallas_call | solution.py:832
  233.4 3.1 fusion.1
  236.5 3.0 collective-permute-start.40
  239.4 2.0 collective-permute-done.37
  241.4 4.3 %convert_add_fusion = (f32[1,1,4,64,2688]{4,3,2,1,0:T(8,128)S(1)}, bf16[1,1,4,64,2688]{4,3,2,1,0:T(8,128)(2,1)S(1)}, f32[1,1,4,64,2688]{4,3,2,1,0:T(8,128)S(1)}) fusion(bf16[2,2,4,64,2688]{4,3,2,1,0:T(8,128)(2,1)} %collective-permute-done.37, s32[]{:T(128)S(6)} %select_n.209, s32[]{:T(128)S(6)} %select_n.212, ...), kind=kLoop, calls=%fused_computation.3 | loop fusion | flops 6881280 | bytes 15138840 | tf_op jit(solution)/shard_map/add | solution.py:960
  247.0 2.0 collective-permute-start.38
  249.1 21.4 %attention_back.1.g_ref = bf16[3,544,1024]{2,1,0:T(8,128)(2,1)} custom-call(bf16[6,544,512]{2,1,0:T(8,128)(2,1)} %project.1.q_ref.k_ref.v_ref, bf16[6,544,512]{2,1,0:T(8,128)(2,1)} %project.1.q_ref.k_ref.v_ref, bf16[6,544,512]{2,1,0:T(8,128)(2,1)} %project.1.q_ref.k_ref.v_ref, bf16[544,544]{1,0:T(8,128)(2,1)} %select_convert_fusion.bias_ref, ...), custom_call_target="tpu_custom_call" | custom-call | flops 27499999232 | bytes 50000000 | tf_op jit(solution)/shard_map/attention_back/pallas_call | solution.py:897
  270.6 1.6 fusion.5
  278.6 7.0 %collective-permute-done.40 = bf16[2,2,64,2048]{3,2,1,0:T(8,128)(2,1)} collective-permute-done((bf16[2,2,64,2048]{3,2,1,0:T(8,128)(2,1)}, bf16[2,2,64,2048]{3,2,1,0:T(8,128)(2,1)}, u32[]{:S(2)}, u32[]{:S(2)}) %collective-permute-start.40) | collective-permute-done | bytes 1048608 | tf_op jit(solution)/shard_map/ppermute | solution.py:285
  285.6 2.9 fusion.2
  290.7 17.2 %qkv_back.1 = (bf16[2,2,4,64,1536]{4,3,2,1,0:T(8,128)(2,1)}, bf16[2,2,4,64,1536]{4,3,2,1,0:T(8,128)(2,1)}, bf16[544,1024]{1,0:T(8,128)(2,1)}) custom-call(bf16[544,1024]{1,0:T(8,128)(2,1)} %pad.15.x_ref, bf16[3,544,1024]{2,1,0:T(8,128)(2,1)} %attention_back.1.g_ref, f32[544,1024]{1,0:T(8,128)} %get-tuple-element.158.r_ref, ...), custom_call_target="tpu_custom_call" | custom-call | flops 17600000000 | bytes 32000000 | tf_op jit(solution)/shard_map/qkv_back/pallas_call | solution.py:940
  309.5 1.9 slice.158
  311.4 1.8 collective-permute-start.48
  313.2 2.0 collective-permute-start.47
  315.2 3.4 fusion
  319.0 1.7 collective-permute-start.51
  320.7 2.3 convert_add_fusion.2
  323.2 3.0 collective-permute-done.48
  326.2 2.4 collective-permute-start.45
  329.8 2.3 collective-permute-start.52
  333.1 2.6 collective-permute-done.44
  337.6 2.2 collective-permute-start.50
  341.6 4.4 %collective-permute-done.52 = bf16[64,2688]{1,0:T(8,128)(2,1)S(1)} collective-permute-done((bf16[64,2688]{1,0:T(8,128)(2,1)S(1)}, bf16[64,2688]{1,0:T(8,128)(2,1)S(1)}, u32[]{:S(2)}, u32[]{:S(2)}) %collective-permute-start.52) | collective-permute-done | bytes 344096 | tf_op jit(solution)/shard_map/ppermute | solution.py:285
  346.7 10.1 %final_rows.1 = bf16[532,2,1024]{2,1,0:T(2,128)(2,1)} custom-call(bf16[532,1024]{1,0:T(8,128)(2,1)} %copy-done.5, bf16[532,1024]{1,0:T(8,128)(2,1)} %copy-done.21), custom_call_target="tpu_custom_call" | custom-call | tf_op jit(solution)/shard_map/final_rows/pallas_call | solution.py:881
  358.3 2.2 fusion.3
  361.6 1.7 collective-permute-start.53
  366.7 2.9 collective-permute-start.55
  370.9 2.6 multiply_reduce_fusion
  373.5 4.8 %collective-permute-done.53 = bf16[260,1024]{1,0:T(8,128)(2,1)} collective-permute-done((bf16[260,1024]{1,0:T(8,128)(2,1)}, bf16[260,1024]{1,0:T(8,128)(2,1)}, u32[]{:S(2)}, u32[]{:S(2)}) %collective-permute-start.53) | collective-permute-done | bytes 532512 | tf_op jit(solution)/shard_map/ppermute | solution.py:285
  378.3 1.9 constant_dynamic-update-slice_fusion
  387.8 1.6 collective-permute-start.60
  392.1 1.9 collective-permute-done.61
  394.0 2.6 collective-permute-start.62
  399.4 5.4 %copy.79 = f32[2,532,1024]{2,0,1:T(2,128)} copy(f32[2,532,1024]{2,1,0:T(8,128)S(1)} %convert_bitcast_fusion) | data formatting | bytes 8716288
  408.0 3.2 multiply_add_fusion
  411.3 1.6 multiply_add_fusion.1
  (288 shorter events, 77.6 us)
Async XLA Ops:
  1.9 9.9 %collective-permute-start = (bf16[64,2048]{1,0:T(8,128)(2,1)S(1)}, bf16[64,2048]{1,0:T(8,128)(2,1)S(1)}, u32[]{:S(2)}, u32[]{:S(2)}) collective-permute-start(bf16[64,2048]{1,0:T(8,128)(2,1)S(1)} %convert_bitcast_fusion.1.own), channel_id=1, source_target_pairs={{0,1},{1,0},{2,3},{3,2},{4,5},{5,4},{6,7},{7,6},{8,9},{9,8},{10,11... | collective-permute-start | bytes 786440 | tf_op jit(solution)/shard_map/ppermute | solution.py:285
  6.1 16.8 %collective-permute-start.1 = (bf16[64,1536]{1,0:T(8,128)(2,1)S(1)}, bf16[64,1536]{1,0:T(8,128)(2,1)S(1)}, u32[]{:S(2)}, u32[]{:S(2)}) collective-permute-start(bf16[64,1536]{1,0:T(8,128)(2,1)S(1)} %pad_maximum_fusion.4.refs_0_), channel_id=1, source_target_pairs={{0,8},{8,0},{16,24},{24,16},{1,9},{9,1},{17,25},{25,17},{2,10},{10... | collective-permute-start | bytes 589832 | tf_op jit(solution)/shard_map/ppermute | solution.py:285
  7.7 17.3 %collective-permute-start.2 = (bf16[64,1536]{1,0:T(8,128)(2,1)S(1)}, bf16[64,1536]{1,0:T(8,128)(2,1)}, u32[]{:S(2)}, u32[]{:S(2)}) collective-permute-start(bf16[64,1536]{1,0:T(8,128)(2,1)S(1)} %pad_maximum_fusion.4.refs_0_), channel_id=1, source_target_pairs={{0,16},{8,24},{16,0},{24,8},{1,17},{9,25},{17,1},{25,9},{2,18},{10... | collective-permute-start | bytes 589832 | tf_op jit(solution)/shard_map/ppermute | solution.py:285
  10.3 14.7 %collective-permute-start.3 = (bf16[64,1536]{1,0:T(8,128)(2,1)S(1)}, bf16[64,1536]{1,0:T(8,128)(2,1)}, u32[]{:S(2)}, u32[]{:S(2)}) collective-permute-start(bf16[64,1536]{1,0:T(8,128)(2,1)S(1)} %pad_maximum_fusion.4.refs_0_), channel_id=1, source_target_pairs={{0,24},{8,16},{16,8},{24,0},{1,25},{9,17},{17,9},{25,1},{2,26},{10... | collective-permute-start | bytes 589832 | tf_op jit(solution)/shard_map/ppermute | solution.py:285
  14.4 12.9 %collective-permute-start.7 = (bf16[2,64,2048]{2,1,0:T(8,128)(2,1)}, bf16[2,64,2048]{2,1,0:T(8,128)(2,1)S(1)}, u32[]{:S(2)}, u32[]{:S(2)}) collective-permute-start(bf16[2,64,2048]{2,1,0:T(8,128)(2,1)} %join_pair.2.own), channel_id=1, source_target_pairs={{0,4},{4,0},{1,5},{5,1},{2,6},{6,2},{3,7},{7,3},{8,12},{12,8},{9,1... | collective-permute-start | bytes 1572872 | tf_op jit(solution)/shard_map/ppermute | solution.py:285
  29.6 19.9 %collective-permute-start.10 = (bf16[4,64,1536]{2,1,0:T(8,128)(2,1)}, bf16[4,64,1536]{2,1,0:T(8,128)(2,1)}, u32[]{:S(2)}, u32[]{:S(2)}) collective-permute-start(bf16[4,64,1536]{2,1,0:T(8,128)(2,1)} %join_column.3.refs_0_), channel_id=1, source_target_pairs={{1,0},{5,1},{4,5},{0,4},{3,2},{7,3},{6,7},{2,6},{9,8},{13,9},{12,1... | collective-permute-start | bytes 2359304 | tf_op jit(solution)/shard_map/ppermute | solution.py:285
  31.1 17.3 %collective-permute-start.8 = (bf16[4,64,1536]{2,1,0:T(8,128)(2,1)}, bf16[4,64,1536]{2,1,0:T(8,128)(2,1)}, u32[]{:S(2)}, u32[]{:S(2)}) collective-permute-start(bf16[4,64,1536]{2,1,0:T(8,128)(2,1)} %join_column.3.refs_0_), channel_id=1, source_target_pairs={{0,1},{1,5},{5,4},{4,0},{2,3},{3,7},{7,6},{6,2},{8,9},{9,13},{13,1... | collective-permute-start | bytes 2359304 | tf_op jit(solution)/shard_map/ppermute | solution.py:285
  31.8 19.3 %collective-permute-start.4 = (bf16[64,2688]{1,0:T(8,128)(2,1)S(1)}, bf16[64,2688]{1,0:T(8,128)(2,1)S(1)}, u32[]{:S(2)}, u32[]{:S(2)}) collective-permute-start(bf16[64,2688]{1,0:T(8,128)(2,1)S(1)} %fusion.28.refs_0_), channel_id=1, source_target_pairs={{0,8},{8,0},{16,24},{24,16},{1,9},{9,1},{17,25},{25,17},{2,10},{10... | collective-permute-start | bytes 1032200 | tf_op jit(solution)/shard_map/ppermute | solution.py:285
  33.3 26.6 %collective-permute-start.5 = (bf16[64,2688]{1,0:T(8,128)(2,1)S(1)}, bf16[64,2688]{1,0:T(8,128)(2,1)S(1)}, u32[]{:S(2)}, u32[]{:S(2)}) collective-permute-start(bf16[64,2688]{1,0:T(8,128)(2,1)S(1)} %fusion.28.refs_0_), channel_id=1, source_target_pairs={{0,16},{8,24},{16,0},{24,8},{1,17},{9,25},{17,1},{25,9},{2,18},{10... | collective-permute-start | bytes 1032200 | tf_op jit(solution)/shard_map/ppermute | solution.py:285
  36.0 24.0 %collective-permute-start.6 = (bf16[64,2688]{1,0:T(8,128)(2,1)S(1)}, bf16[64,2688]{1,0:T(8,128)(2,1)S(1)}, u32[]{:S(2)}, u32[]{:S(2)}) collective-permute-start(bf16[64,2688]{1,0:T(8,128)(2,1)S(1)} %fusion.28.refs_0_), channel_id=1, source_target_pairs={{0,24},{8,16},{16,8},{24,0},{1,25},{9,17},{17,9},{25,1},{2,26},{10... | collective-permute-start | bytes 1032200 | tf_op jit(solution)/shard_map/ppermute | solution.py:285
  48.5 18.8 %collective-permute-start.12 = (bf16[4,64,1536]{2,1,0:T(8,128)(2,1)S(1)}, bf16[4,64,1536]{2,1,0:T(8,128)(2,1)S(1)}, u32[]{:S(2)}, u32[]{:S(2)}) collective-permute-start(bf16[4,64,1536]{2,1,0:T(8,128)(2,1)S(1)} %copy-done.25), channel_id=1, source_target_pairs={{0,2},{2,0},{1,3},{3,1},{4,6},{6,4},{5,7},{7,5},{8,10},{10,8},{9,1... | collective-permute-start | bytes 2359304 | tf_op jit(solution)/shard_map/ppermute | solution.py:285
  49.5 11.6 %collective-permute-start.9 = (bf16[2,64,1536]{2,1,0:T(8,128)(2,1)S(1)}, bf16[2,64,1536]{2,1,0:T(8,128)(2,1)S(1)}, u32[]{:S(2)}, u32[]{:S(2)}) collective-permute-start(bf16[2,64,1536]{2,1,0:T(8,128)(2,1)S(1)} %slice.166), channel_id=1, source_target_pairs={{0,1},{1,5},{5,4},{4,0},{2,3},{3,7},{7,6},{6,2},{8,9},{9,13},{13,1... | collective-permute-start | bytes 1179656 | tf_op jit(solution)/shard_map/ppermute | solution.py:285
  51.2 11.3 %collective-permute-start.11 = (bf16[2,64,1536]{2,1,0:T(8,128)(2,1)S(1)}, bf16[2,64,1536]{2,1,0:T(8,128)(2,1)S(1)}, u32[]{:S(2)}, u32[]{:S(2)}) collective-permute-start(bf16[2,64,1536]{2,1,0:T(8,128)(2,1)S(1)} %slice.167), channel_id=1, source_target_pairs={{1,0},{5,1},{4,5},{0,4},{3,2},{7,3},{6,7},{2,6},{9,8},{13,9},{12,1... | collective-permute-start | bytes 1179656 | tf_op jit(solution)/shard_map/ppermute | solution.py:285
  60.0 13.4 %collective-permute-start.13 = (bf16[4,64,1536]{2,1,0:T(8,128)(2,1)}, bf16[4,64,1536]{2,1,0:T(8,128)(2,1)}, u32[]{:S(2)}, u32[]{:S(2)}) collective-permute-start(bf16[4,64,1536]{2,1,0:T(8,128)(2,1)} %collective-permute-done.8.refs_1_), channel_id=1, source_target_pairs={{0,2},{2,0},{1,3},{3,1},{4,6},{6,4},{5,7},{7,5},{8,10},{10,8},{9,1... | collective-permute-start | bytes 2359304 | tf_op jit(solution)/shard_map/ppermute | solution.py:285
  60.0 13.7 %collective-permute-start.14 = (bf16[4,64,1536]{2,1,0:T(8,128)(2,1)}, bf16[4,64,1536]{2,1,0:T(8,128)(2,1)}, u32[]{:S(2)}, u32[]{:S(2)}) collective-permute-start(bf16[4,64,1536]{2,1,0:T(8,128)(2,1)} %collective-permute-done.10.refs_2_), channel_id=1, source_target_pairs={{0,2},{2,0},{1,3},{3,1},{4,6},{6,4},{5,7},{7,5},{8,10},{10,8},{9,1... | collective-permute-start | bytes 2359304 | tf_op jit(solution)/shard_map/ppermute | solution.py:285
  61.1 9.6 %collective-permute-start.15 = (bf16[2,64,1536]{2,1,0:T(8,128)(2,1)S(1)}, bf16[2,64,1536]{2,1,0:T(8,128)(2,1)}, u32[]{:S(2)}, u32[]{:S(2)}) collective-permute-start(bf16[2,64,1536]{2,1,0:T(8,128)(2,1)S(1)} %collective-permute-done.9.refs_3_), channel_id=1, source_target_pairs={{0,2},{2,0},{1,3},{3,1},{4,6},{6,4},{5,7},{7,5},{8,10},{10,8},{9,1... | collective-permute-start | bytes 1179656 | tf_op jit(solution)/shard_map/ppermute | solution.py:285
  62.5 9.2 %collective-permute-start.16 = (bf16[2,64,1536]{2,1,0:T(8,128)(2,1)S(1)}, bf16[2,64,1536]{2,1,0:T(8,128)(2,1)}, u32[]{:S(2)}, u32[]{:S(2)}) collective-permute-start(bf16[2,64,1536]{2,1,0:T(8,128)(2,1)S(1)} %collective-permute-done.11.refs_4_), channel_id=1, source_target_pairs={{0,2},{2,0},{1,3},{3,1},{4,6},{6,4},{5,7},{7,5},{8,10},{10,8},{9,1... | collective-permute-start | bytes 1179656 | tf_op jit(solution)/shard_map/ppermute | solution.py:285
  67.3 50.0 %collective-permute-start.17 = (bf16[2,2,64,2048]{3,2,1,0:T(8,128)(2,1)}, bf16[2,2,64,2048]{3,2,1,0:T(8,128)(2,1)}, u32[]{:S(2)}, u32[]{:S(2)}) collective-permute-start(bf16[2,2,64,2048]{3,2,1,0:T(8,128)(2,1)} %join_pair.3.refs_0_), channel_id=1, source_target_pairs={{0,16},{8,24},{16,0},{24,8},{1,17},{9,25},{17,1},{25,9},{2,18},{10... | collective-permute-start | bytes 3145736 | tf_op jit(solution)/shard_map/ppermute | solution.py:285
  70.7 46.8 %collective-permute-start.27 = (bf16[2,2,64,2048]{3,2,1,0:T(8,128)(2,1)}, bf16[2,2,64,2048]{3,2,1,0:T(8,128)(2,1)}, u32[]{:S(2)}, u32[]{:S(2)}) collective-permute-start(bf16[2,2,64,2048]{3,2,1,0:T(8,128)(2,1)} %join_pair.3.refs_0_), channel_id=1, source_target_pairs={{0,8},{8,0},{16,24},{24,16},{1,9},{9,1},{17,25},{25,17},{2,10},{10... | collective-permute-start | bytes 3145736 | tf_op jit(solution)/shard_map/ppermute | solution.py:285
  71.7 32.1 %collective-permute-start.18 = (bf16[4,64,2688]{2,1,0:T(8,128)(2,1)}, bf16[4,64,2688]{2,1,0:T(8,128)(2,1)S(1)}, u32[]{:S(2)}, u32[]{:S(2)}) collective-permute-start(bf16[4,64,2688]{2,1,0:T(8,128)(2,1)} %join_column.2.refs_0_.refs_8_), channel_id=1, source_target_pairs={{0,1},{1,5},{5,4},{4,0},{2,3},{3,7},{7,6},{6,2},{8,9},{9,13},{13,1... | collective-permute-start | bytes 4128776 | tf_op jit(solution)/shard_map/ppermute | solution.py:285
  73.4 31.8 %collective-permute-start.19 = (bf16[4,64,2688]{2,1,0:T(8,128)(2,1)}, bf16[4,64,2688]{2,1,0:T(8,128)(2,1)S(1)}, u32[]{:S(2)}, u32[]{:S(2)}) collective-permute-start(bf16[4,64,2688]{2,1,0:T(8,128)(2,1)} %join_column.2.refs_0_.refs_8_), channel_id=1, source_target_pairs={{1,0},{5,1},{4,5},{0,4},{3,2},{7,3},{6,7},{2,6},{9,8},{13,9},{12,1... | collective-permute-start | bytes 4128776 | tf_op jit(solution)/shard_map/ppermute | solution.py:285
  73.7 48.9 %collective-permute-start.22 = (bf16[4,64,2688]{2,1,0:T(8,128)(2,1)}, bf16[4,64,2688]{2,1,0:T(8,128)(2,1)}, u32[]{:S(2)}, u32[]{:S(2)}) collective-permute-start(bf16[4,64,2688]{2,1,0:T(8,128)(2,1)} %join_column.2.refs_0_.refs_8_), channel_id=1, source_target_pairs={{0,2},{2,0},{1,3},{3,1},{4,6},{6,4},{5,7},{7,5},{8,10},{10,8},{9,1... | collective-permute-start | bytes 4128776 | tf_op jit(solution)/shard_map/ppermute | solution.py:285
  105.2 16.1 %collective-permute-start.20 = (bf16[2,64,2688]{2,1,0:T(8,128)(2,1)S(1)}, bf16[2,64,2688]{2,1,0:T(8,128)(2,1)S(1)}, u32[]{:S(2)}, u32[]{:S(2)}) collective-permute-start(bf16[2,64,2688]{2,1,0:T(8,128)(2,1)S(1)} %slice.129), channel_id=1, source_target_pairs={{0,1},{1,5},{5,4},{4,0},{2,3},{3,7},{7,6},{6,2},{8,9},{9,13},{13,1... | collective-permute-start | bytes 2064392 | tf_op jit(solution)/shard_map/ppermute | solution.py:285
  106.8 15.8 %collective-permute-start.21 = (bf16[2,64,2688]{2,1,0:T(8,128)(2,1)S(1)}, bf16[2,64,2688]{2,1,0:T(8,128)(2,1)S(1)}, u32[]{:S(2)}, u32[]{:S(2)}) collective-permute-start(bf16[2,64,2688]{2,1,0:T(8,128)(2,1)S(1)} %slice.130), channel_id=1, source_target_pairs={{1,0},{5,1},{4,5},{0,4},{3,2},{7,3},{6,7},{2,6},{9,8},{13,9},{12,1... | collective-permute-start | bytes 2064392 | tf_op jit(solution)/shard_map/ppermute | solution.py:285
  117.3 8.7 %collective-permute-start.23 = (bf16[4,64,2688]{2,1,0:T(8,128)(2,1)S(1)}, bf16[4,64,2688]{2,1,0:T(8,128)(2,1)S(1)}, u32[]{:S(2)}, u32[]{:S(2)}) collective-permute-start(bf16[4,64,2688]{2,1,0:T(8,128)(2,1)S(1)} %collective-permute-done.18.refs_1_.refs_9_), channel_id=1, source_target_pairs={{0,2},{2,0},{1,3},{3,1},{4,6},{6,4},{5,7},{7,5},{8,10},{10,8},{9,1... | collective-permute-start | bytes 4128776 | tf_op jit(solution)/shard_map/ppermute | solution.py:285
  117.5 9.6 %collective-permute-start.24 = (bf16[4,64,2688]{2,1,0:T(8,128)(2,1)S(1)}, bf16[4,64,2688]{2,1,0:T(8,128)(2,1)}, u32[]{:S(2)}, u32[]{:S(2)}) collective-permute-start(bf16[4,64,2688]{2,1,0:T(8,128)(2,1)S(1)} %collective-permute-done.19.refs_2_.refs_10_), channel_id=1, source_target_pairs={{0,2},{2,0},{1,3},{3,1},{4,6},{6,4},{5,7},{7,5},{8,10},{10,8},{9,1... | collective-permute-start | bytes 4128776 | tf_op jit(solution)/shard_map/ppermute | solution.py:285
  121.3 2.1 collective-permute-start.25
  122.6 2.4 collective-permute-start.26
  122.6 27.9 %collective-permute-start.29 = (bf16[2,2,64,2048]{3,2,1,0:T(8,128)(2,1)}, bf16[2,2,64,2048]{3,2,1,0:T(8,128)(2,1)}, u32[]{:S(2)}, u32[]{:S(2)}) collective-permute-start(bf16[2,2,64,2048]{3,2,1,0:T(8,128)(2,1)} %join_pair.3.refs_0_), channel_id=1, source_target_pairs={{0,2},{2,0},{1,3},{3,1},{4,6},{6,4},{5,7},{7,5},{8,10},{10,8},{9,1... | collective-permute-start | bytes 3145736 | tf_op jit(solution)/shard_map/ppermute | solution.py:285
  123.5 27.1 %collective-permute-start.30 = (bf16[2,2,64,2048]{3,2,1,0:T(8,128)(2,1)}, bf16[2,2,64,2048]{3,2,1,0:T(8,128)(2,1)}, u32[]{:S(2)}, u32[]{:S(2)}) collective-permute-start(bf16[2,2,64,2048]{3,2,1,0:T(8,128)(2,1)} %collective-permute-done.27.refs_1_), channel_id=1, source_target_pairs={{0,2},{2,0},{1,3},{3,1},{4,6},{6,4},{5,7},{7,5},{8,10},{10,8},{9,1... | collective-permute-start | bytes 3145736 | tf_op jit(solution)/shard_map/ppermute | solution.py:285
  125.0 25.5 %collective-permute-start.28 = (bf16[2,2,64,2048]{3,2,1,0:T(8,128)(2,1)}, bf16[2,2,64,2048]{3,2,1,0:T(8,128)(2,1)}, u32[]{:S(2)}, u32[]{:S(2)}) collective-permute-start(bf16[2,2,64,2048]{3,2,1,0:T(8,128)(2,1)} %collective-permute-done.17.refs_2_), channel_id=1, source_target_pairs={{0,8},{8,0},{16,24},{24,16},{1,9},{9,1},{17,25},{25,17},{2,10},{10... | collective-permute-start | bytes 3145736 | tf_op jit(solution)/shard_map/ppermute | solution.py:285
  127.0 23.5 %collective-permute-start.31 = (bf16[2,2,64,2048]{3,2,1,0:T(8,128)(2,1)}, bf16[2,2,64,2048]{3,2,1,0:T(8,128)(2,1)}, u32[]{:S(2)}, u32[]{:S(2)}) collective-permute-start(bf16[2,2,64,2048]{3,2,1,0:T(8,128)(2,1)} %collective-permute-done.17.refs_2_), channel_id=1, source_target_pairs={{0,2},{2,0},{1,3},{3,1},{4,6},{6,4},{5,7},{7,5},{8,10},{10,8},{9,1... | collective-permute-start | bytes 3145736 | tf_op jit(solution)/shard_map/ppermute | solution.py:285
  150.5 2.9 collective-permute-start.32
  182.6 7.5 %collective-permute-start.34 = (bf16[4,2,2,64,2048]{4,3,2,1,0:T(8,128)(2,1)}, bf16[4,2,2,64,2048]{4,3,2,1,0:T(8,128)(2,1)}, u32[]{:S(2)}, u32[]{:S(2)}) collective-permute-start(bf16[4,2,2,64,2048]{4,3,2,1,0:T(8,128)(2,1)} %get-tuple-element.132), channel_id=1, source_target_pairs={{0,2},{2,0},{1,3},{3,1},{4,6},{6,4},{5,7},{7,5},{8,10},{10,8},{9,1... | collective-permute-start | bytes 12582920 | tf_op jit(solution)/shard_map/ppermute | solution.py:285
  182.9 42.6 %collective-permute-start.33 = (bf16[532,1024]{1,0:T(8,128)(2,1)S(1)}, bf16[532,1024]{1,0:T(8,128)(2,1)S(1)}, u32[]{:S(2)}, u32[]{:S(2)}) collective-permute-start(bf16[532,1024]{1,0:T(8,128)(2,1)S(1)} %slice.131.own_ref), channel_id=1, source_target_pairs={{0,1},{1,0},{2,3},{3,2},{4,5},{5,4},{6,7},{7,6},{8,9},{9,8},{10,11... | collective-permute-start | bytes 3268616 | tf_op jit(solution)/shard_map/ppermute | solution.py:285
  194.6 30.9 %collective-permute-start.36 = (bf16[2,2,64,2048]{3,2,1,0:T(8,128)(2,1)}, bf16[2,2,64,2048]{3,2,1,0:T(8,128)(2,1)S(1)}, u32[]{:S(2)}, u32[]{:S(2)}) collective-permute-start(bf16[2,2,64,2048]{3,2,1,0:T(8,128)(2,1)} %get-tuple-element.303), channel_id=1, source_target_pairs={{0,8},{8,0},{16,24},{24,16},{1,9},{9,1},{17,25},{25,17},{2,10},{10... | collective-permute-start | bytes 3145736 | tf_op jit(solution)/shard_map/ppermute | solution.py:285
  232.0 9.4 %collective-permute-start.37 = (bf16[2,2,4,64,2688]{4,3,2,1,0:T(8,128)(2,1)}, bf16[2,2,4,64,2688]{4,3,2,1,0:T(8,128)(2,1)}, u32[]{:S(2)}, u32[]{:S(2)}) collective-permute-start(bf16[2,2,4,64,2688]{4,3,2,1,0:T(8,128)(2,1)} %get-tuple-element.147), channel_id=1, source_target_pairs={{0,2},{2,0},{1,3},{3,1},{4,6},{6,4},{5,7},{7,5},{8,10},{10,8},{9,1... | collective-permute-start | bytes 16515080 | tf_op jit(solution)/shard_map/ppermute | solution.py:285
  232.2 46.4 %collective-permute-start.35 = (bf16[2,2,64,2048]{3,2,1,0:T(8,128)(2,1)}, bf16[2,2,64,2048]{3,2,1,0:T(8,128)(2,1)}, u32[]{:S(2)}, u32[]{:S(2)}) collective-permute-start(bf16[2,2,64,2048]{3,2,1,0:T(8,128)(2,1)} %get-tuple-element.302), channel_id=1, source_target_pairs={{0,8},{8,0},{16,24},{24,16},{1,9},{9,1},{17,25},{25,17},{2,10},{10... | collective-permute-start | bytes 3145736 | tf_op jit(solution)/shard_map/ppermute | solution.py:285
  236.5 49.1 %collective-permute-start.40 = (bf16[2,2,64,2048]{3,2,1,0:T(8,128)(2,1)}, bf16[2,2,64,2048]{3,2,1,0:T(8,128)(2,1)}, u32[]{:S(2)}, u32[]{:S(2)}) collective-permute-start(bf16[2,2,64,2048]{3,2,1,0:T(8,128)(2,1)} %fusion.1), channel_id=1, source_target_pairs={{0,16},{8,24},{16,0},{24,8},{1,17},{9,25},{17,1},{25,9},{2,18},{10... | collective-permute-start | bytes 3145736 | tf_op jit(solution)/shard_map/ppermute | solution.py:285
  247.0 23.6 %collective-permute-start.38 = (bf16[2,64,2688]{2,1,0:T(8,128)(2,1)}, bf16[2,64,2688]{2,1,0:T(8,128)(2,1)}, u32[]{:S(2)}, u32[]{:S(2)}) collective-permute-start(bf16[2,64,2688]{2,1,0:T(8,128)(2,1)} %get-tuple-element.315), channel_id=1, source_target_pairs={{0,1},{1,5},{5,4},{4,0},{2,3},{3,7},{7,6},{6,2},{8,9},{9,13},{13,1... | collective-permute-start | bytes 2064392 | tf_op jit(solution)/shard_map/ppermute | solution.py:285
  249.0 21.6 %collective-permute-start.39 = (bf16[2,64,2688]{2,1,0:T(8,128)(2,1)}, bf16[2,64,2688]{2,1,0:T(8,128)(2,1)}, u32[]{:S(2)}, u32[]{:S(2)}) collective-permute-start(bf16[2,64,2688]{2,1,0:T(8,128)(2,1)} %get-tuple-element.314), channel_id=1, source_target_pairs={{1,0},{5,1},{4,5},{0,4},{3,2},{7,3},{6,7},{2,6},{9,8},{13,9},{12,1... | collective-permute-start | bytes 2064392 | tf_op jit(solution)/shard_map/ppermute | solution.py:285
  273.5 34.4 %collective-permute-start.42 = (bf16[4,64,2688]{2,1,0:T(8,128)(2,1)}, bf16[4,64,2688]{2,1,0:T(8,128)(2,1)}, u32[]{:S(2)}, u32[]{:S(2)}) collective-permute-start(bf16[4,64,2688]{2,1,0:T(8,128)(2,1)} %pad_maximum_fusion.1), channel_id=1, source_target_pairs={{1,0},{5,1},{4,5},{0,4},{3,2},{7,3},{6,7},{2,6},{9,8},{13,9},{12,1... | collective-permute-start | bytes 4128776 | tf_op jit(solution)/shard_map/ppermute | solution.py:285
  276.3 31.7 %collective-permute-start.41 = (bf16[4,64,2688]{2,1,0:T(8,128)(2,1)S(1)}, bf16[4,64,2688]{2,1,0:T(8,128)(2,1)S(1)}, u32[]{:S(2)}, u32[]{:S(2)}) collective-permute-start(bf16[4,64,2688]{2,1,0:T(8,128)(2,1)S(1)} %pad_maximum_fusion), channel_id=1, source_target_pairs={{0,1},{1,5},{5,4},{4,0},{2,3},{3,7},{7,6},{6,2},{8,9},{9,13},{13,1... | collective-permute-start | bytes 4128776 | tf_op jit(solution)/shard_map/ppermute | solution.py:285
  308.0 12.7 %collective-permute-start.43 = (bf16[2,2,4,64,1536]{4,3,2,1,0:T(8,128)(2,1)}, bf16[2,2,4,64,1536]{4,3,2,1,0:T(8,128)(2,1)}, u32[]{:S(2)}, u32[]{:S(2)}) collective-permute-start(bf16[2,2,4,64,1536]{4,3,2,1,0:T(8,128)(2,1)} %get-tuple-element.163), channel_id=1, source_target_pairs={{0,2},{2,0},{1,3},{3,1},{4,6},{6,4},{5,7},{7,5},{8,10},{10,8},{9,1... | collective-permute-start | bytes 9437192 | tf_op jit(solution)/shard_map/ppermute | solution.py:285
  311.4 14.8 %collective-permute-start.48 = (bf16[272,1024]{1,0:T(8,128)(2,1)S(1)}, bf16[272,1024]{1,0:T(8,128)(2,1)S(1)}, u32[]{:S(2)}, u32[]{:S(2)}) collective-permute-start(bf16[272,1024]{1,0:T(8,128)(2,1)S(1)} %slice.150), channel_id=1, source_target_pairs={{0,1},{1,0},{2,3},{3,2},{4,5},{5,4},{6,7},{7,6},{8,9},{9,8},{10,11... | collective-permute-start | bytes 1671176 | tf_op jit(solution)/shard_map/ppermute | solution.py:285
  313.2 15.4 %collective-permute-start.47 = (bf16[2,64,2048]{2,1,0:T(8,128)(2,1)}, bf16[2,64,2048]{2,1,0:T(8,128)(2,1)S(1)}, u32[]{:S(2)}, u32[]{:S(2)}) collective-permute-start(bf16[2,64,2048]{2,1,0:T(8,128)(2,1)} %fusion.21), channel_id=1, source_target_pairs={{0,4},{4,0},{1,5},{5,1},{2,6},{6,2},{3,7},{7,3},{8,12},{12,8},{9,1... | collective-permute-start | bytes 1572872 | tf_op jit(solution)/shard_map/ppermute | solution.py:285
  318.6 11.1 %collective-permute-start.46 = (bf16[64,2688]{1,0:T(8,128)(2,1)S(1)}, bf16[64,2688]{1,0:T(8,128)(2,1)S(1)}, u32[]{:S(2)}, u32[]{:S(2)}) collective-permute-start(bf16[64,2688]{1,0:T(8,128)(2,1)S(1)} %get-tuple-element.308), channel_id=1, source_target_pairs={{0,8},{8,0},{16,24},{24,16},{1,9},{9,1},{17,25},{25,17},{2,10},{10... | collective-permute-start | bytes 1032200 | tf_op jit(solution)/shard_map/ppermute | solution.py:285
  319.0 22.6 %collective-permute-start.51 = (bf16[64,2688]{1,0:T(8,128)(2,1)S(1)}, bf16[64,2688]{1,0:T(8,128)(2,1)S(1)}, u32[]{:S(2)}, u32[]{:S(2)}) collective-permute-start(bf16[64,2688]{1,0:T(8,128)(2,1)S(1)} %get-tuple-element.307), channel_id=1, source_target_pairs={{0,8},{8,0},{16,24},{24,16},{1,9},{9,1},{17,25},{25,17},{2,10},{10... | collective-permute-start | bytes 1032200 | tf_op jit(solution)/shard_map/ppermute | solution.py:285
  323.2 12.6 %collective-permute-start.44 = (bf16[2,64,1536]{2,1,0:T(8,128)(2,1)S(1)}, bf16[2,64,1536]{2,1,0:T(8,128)(2,1)S(1)}, u32[]{:S(2)}, u32[]{:S(2)}) collective-permute-start(bf16[2,64,1536]{2,1,0:T(8,128)(2,1)S(1)} %get-tuple-element.317), channel_id=1, source_target_pairs={{0,1},{1,5},{5,4},{4,0},{2,3},{3,7},{7,6},{6,2},{8,9},{9,13},{13,1... | collective-permute-start | bytes 1179656 | tf_op jit(solution)/shard_map/ppermute | solution.py:285
  326.2 10.2 %collective-permute-start.45 = (bf16[2,64,1536]{2,1,0:T(8,128)(2,1)S(1)}, bf16[2,64,1536]{2,1,0:T(8,128)(2,1)S(1)}, u32[]{:S(2)}, u32[]{:S(2)}) collective-permute-start(bf16[2,64,1536]{2,1,0:T(8,128)(2,1)S(1)} %get-tuple-element.316), channel_id=1, source_target_pairs={{1,0},{5,1},{4,5},{0,4},{3,2},{7,3},{6,7},{2,6},{9,8},{13,9},{12,1... | collective-permute-start | bytes 1179656 | tf_op jit(solution)/shard_map/ppermute | solution.py:285
  329.8 16.1 %collective-permute-start.52 = (bf16[64,2688]{1,0:T(8,128)(2,1)S(1)}, bf16[64,2688]{1,0:T(8,128)(2,1)S(1)}, u32[]{:S(2)}, u32[]{:S(2)}) collective-permute-start(bf16[64,2688]{1,0:T(8,128)(2,1)S(1)} %fusion.17), channel_id=1, source_target_pairs={{0,16},{8,24},{16,0},{24,8},{1,17},{9,25},{17,1},{25,9},{2,18},{10... | collective-permute-start | bytes 1032200 | tf_op jit(solution)/shard_map/ppermute | solution.py:285
  337.6 20.3 %collective-permute-start.50 = (bf16[4,64,1536]{2,1,0:T(8,128)(2,1)}, bf16[4,64,1536]{2,1,0:T(8,128)(2,1)}, u32[]{:S(2)}, u32[]{:S(2)}) collective-permute-start(bf16[4,64,1536]{2,1,0:T(8,128)(2,1)} %pad_maximum_fusion.3), channel_id=1, source_target_pairs={{1,0},{5,1},{4,5},{0,4},{3,2},{7,3},{6,7},{2,6},{9,8},{13,9},{12,1... | collective-permute-start | bytes 2359304 | tf_op jit(solution)/shard_map/ppermute | solution.py:285
  340.7 17.6 %collective-permute-start.49 = (bf16[4,64,1536]{2,1,0:T(8,128)(2,1)}, bf16[4,64,1536]{2,1,0:T(8,128)(2,1)}, u32[]{:S(2)}, u32[]{:S(2)}) collective-permute-start(bf16[4,64,1536]{2,1,0:T(8,128)(2,1)} %pad_maximum_fusion.2), channel_id=1, source_target_pairs={{0,1},{1,5},{5,4},{4,0},{2,3},{3,7},{7,6},{6,2},{8,9},{9,13},{13,1... | collective-permute-start | bytes 2359304 | tf_op jit(solution)/shard_map/ppermute | solution.py:285
  361.4 9.6 %collective-permute-start.57 = (bf16[64,2048]{1,0:T(8,128)(2,1)}, bf16[64,2048]{1,0:T(8,128)(2,1)}, u32[]{:S(2)}, u32[]{:S(2)}) collective-permute-start(bf16[64,2048]{1,0:T(8,128)(2,1)} %fusion.31), channel_id=1, source_target_pairs={{0,1},{1,0},{2,3},{3,2},{4,5},{5,4},{6,7},{7,6},{8,9},{9,8},{10,11... | collective-permute-start | bytes 786440 | tf_op jit(solution)/shard_map/ppermute | solution.py:285
  361.6 16.7 %collective-permute-start.53 = (bf16[260,1024]{1,0:T(8,128)(2,1)}, bf16[260,1024]{1,0:T(8,128)(2,1)}, u32[]{:S(2)}, u32[]{:S(2)}) collective-permute-start(bf16[260,1024]{1,0:T(8,128)(2,1)} %slice.158), channel_id=1, source_target_pairs={{0,1},{1,0},{2,3},{3,2},{4,5},{5,4},{6,7},{7,6},{8,9},{9,8},{10,11... | collective-permute-start | bytes 1597448 | tf_op jit(solution)/shard_map/ppermute | solution.py:285
  366.0 14.2 %collective-permute-start.54 = (bf16[64,1536]{1,0:T(8,128)(2,1)}, bf16[64,1536]{1,0:T(8,128)(2,1)S(1)}, u32[]{:S(2)}, u32[]{:S(2)}) collective-permute-start(bf16[64,1536]{1,0:T(8,128)(2,1)} %get-tuple-element.313), channel_id=1, source_target_pairs={{0,8},{8,0},{16,24},{24,16},{1,9},{9,1},{17,25},{25,17},{2,10},{10... | collective-permute-start | bytes 589832 | tf_op jit(solution)/shard_map/ppermute | solution.py:285
  366.7 14.8 %collective-permute-start.55 = (bf16[64,1536]{1,0:T(8,128)(2,1)}, bf16[64,1536]{1,0:T(8,128)(2,1)S(1)}, u32[]{:S(2)}, u32[]{:S(2)}) collective-permute-start(bf16[64,1536]{1,0:T(8,128)(2,1)} %get-tuple-element.312), channel_id=1, source_target_pairs={{0,16},{8,24},{16,0},{24,8},{1,17},{9,25},{17,1},{25,9},{2,18},{10... | collective-permute-start | bytes 589832 | tf_op jit(solution)/shard_map/ppermute | solution.py:285
  369.6 11.9 %collective-permute-start.56 = (bf16[64,1536]{1,0:T(8,128)(2,1)}, bf16[64,1536]{1,0:T(8,128)(2,1)S(1)}, u32[]{:S(2)}, u32[]{:S(2)}) collective-permute-start(bf16[64,1536]{1,0:T(8,128)(2,1)} %get-tuple-element.311), channel_id=1, source_target_pairs={{0,24},{8,16},{16,8},{24,0},{1,25},{9,17},{17,9},{25,1},{2,26},{10... | collective-permute-start | bytes 589832 | tf_op jit(solution)/shard_map/ppermute | solution.py:285
  386.8 5.3 %collective-permute-start.59 = (f32[8,128]{1,0:T(8,128)S(1)}, f32[8,128]{1,0:T(8,128)S(1)}, u32[]{:S(2)}, u32[]{:S(2)}) collective-permute-start(f32[8,128]{1,0:T(8,128)S(1)} %broadcast_add_fusion), channel_id=1, source_target_pairs={{0,1},{1,0},{4,5},{5,4},{2,3},{3,2},{6,7},{7,6},{8,9},{9,8},{12,13... | collective-permute-start | bytes 12296 | tf_op jit(solution)/shard_map/ppermute | solution.py:285
  387.8 4.2 %collective-permute-start.60 = (f32[8,128]{1,0:T(8,128)S(1)}, f32[8,128]{1,0:T(8,128)S(1)}, u32[]{:S(2)}, u32[]{:S(2)}) collective-permute-start(f32[8,128]{1,0:T(8,128)S(1)} %broadcast_add_fusion), channel_id=1, source_target_pairs={{0,4},{1,5},{4,0},{5,1},{2,6},{3,7},{6,2},{7,3},{8,12},{9,13},{12,... | collective-permute-start | bytes 12296 | tf_op jit(solution)/shard_map/ppermute | solution.py:285
  389.5 4.5 %collective-permute-start.61 = (f32[8,128]{1,0:T(8,128)S(1)}, f32[8,128]{1,0:T(8,128)S(1)}, u32[]{:S(2)}, u32[]{:S(2)}) collective-permute-start(f32[8,128]{1,0:T(8,128)S(1)} %broadcast_add_fusion), channel_id=1, source_target_pairs={{0,5},{1,4},{4,1},{5,0},{2,7},{3,6},{6,3},{7,2},{8,13},{9,12},{12,... | collective-permute-start | bytes 12296 | tf_op jit(solution)/shard_map/ppermute | solution.py:285
  394.0 10.8 %collective-permute-start.62 = (f32[8,128]{1,0:T(8,128)S(1)}, f32[8,128]{1,0:T(8,128)S(1)}, u32[]{:S(2)}, u32[]{:S(2)}) collective-permute-start(f32[8,128]{1,0:T(8,128)S(1)} %add_add_fusion.1), channel_id=1, source_target_pairs={{0,8},{8,0},{16,24},{24,16},{1,9},{9,1},{17,25},{25,17},{2,10},{10... | collective-permute-start | bytes 12296 | tf_op jit(solution)/shard_map/ppermute | solution.py:285
  396.6 8.2 %collective-permute-start.63 = (f32[8,128]{1,0:T(8,128)S(1)}, f32[8,128]{1,0:T(8,128)S(1)}, u32[]{:S(2)}, u32[]{:S(2)}) collective-permute-start(f32[8,128]{1,0:T(8,128)S(1)} %add_add_fusion.1), channel_id=1, source_target_pairs={{0,16},{8,24},{16,0},{24,8},{1,17},{9,25},{17,1},{25,9},{2,18},{10... | collective-permute-start | bytes 12296 | tf_op jit(solution)/shard_map/ppermute | solution.py:285
  397.6 7.3 %collective-permute-start.64 = (f32[8,128]{1,0:T(8,128)S(1)}, f32[8,128]{1,0:T(8,128)S(1)}, u32[]{:S(2)}, u32[]{:S(2)}) collective-permute-start(f32[8,128]{1,0:T(8,128)S(1)} %add_add_fusion.1), channel_id=1, source_target_pairs={{0,24},{8,16},{16,8},{24,0},{1,25},{9,17},{17,9},{25,1},{2,26},{10... | collective-permute-start | bytes 12296 | tf_op jit(solution)/shard_map/ppermute | solution.py:285
  (64 other events, 432.7 us)
